TPU v7x, 1024 devices: a whole 4x4x32 slice. The times are simulated.
1024 devices in a mesh: sfc: 512 (over y, x, z), grp: 2 (over core).
Axes of the slice: x: 4, y: 4, z: 32, core: 2. Of those that a mesh axis runs over, the one named last changes fastest.
Arguments:
- right_side: float32 [5, 5, 5, 131072], P(None, None, None, ('sfc', 'grp')), may hold values from -8 to 8
- cell_level: int32 [131072], P(('sfc', 'grp')), may hold values from 0 to 3
- own_slot: int32 [393216], P(('sfc', 'grp')), may hold values from 0 to 767
- near_slot: int32 [393216], P(('sfc', 'grp')), may hold values from 0 to 1151, as said below
- face_kind: int32 [393216], P(('sfc', 'grp')), may hold values from 0 to 5
- orientation: int32 [393216], P(('sfc', 'grp')), may hold values from 0 to 7
- penalty: float32 [393216], P(('sfc', 'grp')), may hold values from 2 to 32
- send_slots: int32 [393216], P(('sfc', 'grp')), may hold values from 0 to 767
- subface_maps: float32 [4, 25, 25], replicated, may hold values from -1.25 to 1.25
Outputs:
- solution: float32 [5, 5, 5, 131072], P(None, None, None, ('sfc', 'grp'))
- residual: float32 [5, 5, 5, 131072], P(None, None, None, ('sfc', 'grp'))
Inputs may be any that keep to these rules, and one draw needn't show every extreme that they name: `own_slot`: a face slot f * 128 + c of the same device. `near_slot`: 768 + k * 96 + i for position i of the received block k; since a device has exactly 384 entries, its near slots are a permutation of its 384 received positions. `face_kind`: 0 boundary face, 1 conforming face, 2 + s the fine side of a hanging face with subface s. `send_slots`: a device's entries k * 96 to k * 96 + 95 are face slots of its own cells sent to the device at offset (+1, -1, +2, -2)[k].
All inputs are finite; a program needn't handle non-finite values.
Results may differ from a plain program's by a relative error of at most 0.00021.
Values sent between devices are 32-bit elements; how exact they have to be, the bound alone decides.
No kernel may reach another device: no remote copies, remote signals or barrier semaphores. Data moves between devices by JAX's collectives and lax.ppermute only.
A program may use at most 32 MiB of HBM per device.

v0:
```python
import jax
import jax.numpy as jnp
import numpy as np
from jax import lax
from jax.sharding import Mesh
from jax.sharding import PartitionSpec as P

NODES = 5
ITERS = 3
SFC = ("sfc_0", "sfc_1", "sfc_2")
SFC_GRP = ("sfc_0", "sfc_1", "sfc_2", "grp")


mass_shift = 1.0
highest = lax.Precision.HIGHEST


def partner_2(block, axis, distance):
    count = lax.axis_size(axis)
    route = []
    for low in range(count):
        high = low | 1 << distance
        if high != low and high < count:
            route += [(low, high), (high, low)]
    return lax.ppermute(block, axis, route)


def shifted(block, axis, distance):
    devices = range(lax.axis_size(axis))
    route = [(i - distance, i) for i in devices if i - distance in devices]
    return lax.ppermute(block, axis, route)


def one_axis_at_a_time(value, axes):
    for axis in axes:
        value = lax.psum(value, axis)
    return value


def node_tables():
    points = np.array([-1.0, -np.sqrt(3.0 / 7.0), 0.0, np.sqrt(3.0 / 7.0), 1.0])
    weights = np.array([0.1, 49.0 / 90.0, 32.0 / 45.0, 49.0 / 90.0, 0.1])
    identity = np.eye(5)
    spacing = points[:, None] - points[None, :] + identity
    barycentric = 1.0 / np.prod(spacing, axis=1)
    offdiag = barycentric[None, :] / barycentric[:, None] / spacing
    diagonal = np.sum(1.0 / spacing, axis=1) - 1.0
    derivs = np.where(identity > 0.5, diagonal[:, None], offdiag)
    stiffness = derivs.T @ (weights[:, None] * derivs)
    return (jnp.asarray(stiffness, jnp.float32), jnp.asarray(weights, jnp.float32))


def volume_term(field, scale, tables):
    stiffness, weights = tables
    first = weights[:, None, None, None]
    second = weights[None, :, None, None]
    third = weights[None, None, :, None]
    along_first = jnp.einsum("ia,abcz->ibcz", stiffness, field, precision=highest)
    along_second = jnp.einsum("jb,abcz->ajcz", stiffness, field, precision=highest)
    along_third = jnp.einsum("kc,abcz->abkz", stiffness, field, precision=highest)
    grads = (
        along_first * second * third + along_second * first * third + along_third * first * second
    )
    return scale * grads + mass_shift * scale * scale * scale * first * second * third * field


def face_traces(field):
    last = NODES - 1
    return jnp.stack(
        [field[0], field[last], field[:, 0], field[:, last], field[:, :, 0], field[:, :, last]],
        axis=-2,
    )


def lift_faces(faces):
    last = NODES - 1
    rest = faces.shape[2:-2] + faces.shape[-1:]
    volume = jnp.zeros((NODES, NODES, NODES) + rest, faces.dtype)
    volume = volume.at[0].add(faces[..., 0, :])
    volume = volume.at[last].add(faces[..., 1, :])
    volume = volume.at[:, 0].add(faces[..., 2, :])
    volume = volume.at[:, last].add(faces[..., 3, :])
    volume = volume.at[:, :, 0].add(faces[..., 4, :])
    volume = volume.at[:, :, last].add(faces[..., 5, :])
    return volume


def orient_forward(values, codes):
    values = jnp.where(codes & 1 == 1, values[::-1], values)
    values = jnp.where(codes & 2 == 2, values[:, ::-1], values)
    return jnp.where(codes & 4 == 4, jnp.swapaxes(values, 0, 1), values)


def orient_back(values, codes):
    values = jnp.where(codes & 4 == 4, jnp.swapaxes(values, 0, 1), values)
    values = jnp.where(codes & 2 == 2, values[:, ::-1], values)
    return jnp.where(codes & 1 == 1, values[::-1], values)


def map_traces(values, kinds, maps, transpose_maps):
    width = NODES * NODES
    flat = values.reshape(width, -1)
    stacked = jnp.swapaxes(maps, 1, 2) if transpose_maps else maps
    moved = jnp.dot(stacked.reshape(4 * width, width), flat, precision=highest).reshape(
        4, width, -1
    )
    selector = kinds[None, :] == jnp.arange(4, dtype=jnp.int32)[:, None] + 2
    result = jnp.where(kinds == 1, flat, 0.0) + jnp.sum(
        jnp.where(selector[:, None, :], moved, 0.0), axis=0
    )
    return result.reshape(values.shape)


def face_terms(own_values, near_values, kinds, orients, penalty, maps, weights):
    face_mass = weights[:, None, None] * weights[None, :, None]
    mapped = map_traces(orient_forward(near_values, orients), kinds, maps, False)
    jump = own_values - mapped
    own_term = penalty * face_mass * jump
    near_term = -orient_back(map_traces(own_term, kinds, maps, True), orients)
    return (own_term, near_term)


def route_blocks(blocks):
    core = lax.axis_index("grp")
    partner = partner_2(jnp.stack([blocks[0], blocks[1]]), "grp", 0)
    upward = shifted(jnp.stack([blocks[2], partner[0]]), SFC, 1)
    downward = shifted(jnp.stack([blocks[3], partner[1]]), SFC, -1)
    plus_one = jnp.where(core == 1, partner[0], upward[1])
    minus_one = jnp.where(core == 0, partner[1], downward[1])
    return (plus_one, minus_one, upward[0], downward[0])


def apply_operator(
    field, scale, own_slot, near_slot, kinds, orients, penalty, send_slots, maps, tables
):
    count = field.shape[-1]
    slots = 6 * count
    width = NODES * NODES
    ghost = send_slots.shape[0] // 4
    traces = face_traces(field).reshape(width, slots)
    sent = jnp.take(traces, send_slots, axis=1)
    arrived = route_blocks(
        tuple((sent[:, position * ghost : (position + 1) * ghost] for position in range(4)))
    )
    volume = volume_term(field, scale, tables)
    pool = jnp.concatenate((traces,) + arrived, axis=1)
    own_values = jnp.take(pool, own_slot, axis=1).reshape(NODES, NODES, -1)
    near_values = jnp.take(pool, near_slot, axis=1).reshape(NODES, NODES, -1)
    own_term, near_term = face_terms(
        own_values, near_values, kinds, orients, penalty, maps, tables[1]
    )
    gathered = jnp.zeros_like(pool).at[:, own_slot].add(own_term.reshape(width, -1))
    gathered = gathered.at[:, near_slot].add(near_term.reshape(width, -1))
    returned = tuple(
        (
            gathered[:, slots + position * ghost : slots + (position + 1) * ghost]
            for position in range(4)
        )
    )
    came_back = route_blocks((returned[1], returned[0], returned[3], returned[2]))
    back = jnp.concatenate((came_back[1], came_back[0], came_back[3], came_back[2]), axis=1)
    local = gathered[:, :slots].at[:, send_slots].add(back)
    faces = local.reshape(NODES, NODES, 6, count)
    return volume + lift_faces(faces)


def body(
    right_side,
    cell_level,
    own_slot,
    near_slot,
    face_kind,
    orientation,
    penalty,
    send_slots,
    subface_maps,
):
    tables = node_tables()
    scale = jnp.exp2(-cell_level.astype(jnp.float32))
    count = right_side.shape[-1]
    scaled_penalty = penalty * jnp.take(scale, own_slot % count)

    def operate(field):
        return apply_operator(
            field,
            scale,
            own_slot,
            near_slot,
            face_kind,
            orientation,
            scaled_penalty,
            send_slots,
            subface_maps,
            tables,
        )

    solution = jnp.zeros_like(right_side)
    residual = right_side
    weighted = operate(residual)
    for iteration in range(ITERS):
        totals = (
            one_axis_at_a_time(jnp.sum(residual * residual), SFC_GRP),
            one_axis_at_a_time(jnp.sum(weighted * residual), SFC_GRP),
        )
        more = iteration + 1 < ITERS
        if more:
            product = operate(weighted)
        if iteration == 0:
            step_size = totals[0] / totals[1]
            carried = product
            searched = weighted
            direction = residual
        else:
            blend_ratio = totals[0] / norm_before
            step_size = totals[0] / (totals[1] - blend_ratio * totals[0] / step_before)
            if more:
                carried = product + blend_ratio * carried
            searched = weighted + blend_ratio * searched
            direction = residual + blend_ratio * direction
        solution = solution + step_size * direction
        residual = residual - step_size * searched
        if more:
            weighted = weighted - step_size * carried
        norm_before = totals[0]
        step_before = step_size
    return (solution, residual)


def solution(mesh):
    finer = Mesh(
        mesh.devices.reshape(4, 4, 32, mesh.shape["grp"]), ("sfc_0", "sfc_1", "sfc_2", "grp")
    )
    in_specs = (
        P(None, None, None, SFC_GRP),
        P(SFC_GRP),
        P(SFC_GRP),
        P(SFC_GRP),
        P(SFC_GRP),
        P(SFC_GRP),
        P(SFC_GRP),
        P(SFC_GRP),
        P(),
    )
    out_specs = (P(None, None, None, SFC_GRP), P(None, None, None, SFC_GRP))
    return jax.shard_map(body, mesh=finer, in_specs=in_specs, out_specs=out_specs, check_vma=False)
```

profile of v0, /device:TPU:1, one launch (start us, length us, event | category | flops | bytes accessed | tf_op | source)
XLA Modules:
  0.0 400.1 jit_solution(6407310464844686131)
XLA Ops:
  4.8 16.1 %collective-permute-start = (f32[2,25,96]{2,0,1:T(2,128)S(1)}, f32[2,25,96]{2,0,1:T(2,128)S(1)}, u32[]{:S(2)}, u32[]{:S(2)}) collective-permute-start(f32[2,25,96]{2,0,1:T(2,128)S(1)} %pad_maximum_fusion), channel_id=1, source_target_pairs={{0,1},{1,0},{2,3},{3,2},{4,5},{5,4},{6,7},{7,6},{8,9},{9,8},{10,11... | collective-permute-start | bytes 57608 | tf_op jit(solution)/shard_map/ppermute | solution.py:25
  23.9 2.7 gather_fusion
  27.0 1.3 collective-permute-start.2
  28.3 4.0 collective-permute-start.1
  33.7 1.1 gather_fusion.2
  35.1 1.1 gather_fusion.3
  37.4 2.0 scatter_custom_fusion
  40.2 2.8 scatter_fusion
  43.3 3.1 collective-permute-start.3
  47.2 1.3 collective-permute-start.4
  48.6 4.6 %collective-permute-start.5 = (f32[2,25,96]{2,0,1:T(2,128)S(1)}, f32[2,25,96]{2,0,1:T(2,128)S(1)}, u32[]{:S(2)}, u32[]{:S(2)}) collective-permute-start(f32[2,25,96]{2,0,1:T(2,128)S(1)} %pad_maximum_fusion.5), channel_id=1, source_target_pairs={{0,2},{2,4},{4,6},{6,8},{8,10},{10,12},{12,14},{14,16},{16,18},{18... | collective-permute-start | bytes 57608 | tf_op jit(solution)/shard_map/ppermute | solution.py:31
  54.4 2.8 scatter_fusion.1
  58.8 1.1 gather_fusion.4
  60.3 3.1 collective-permute-start.6
  64.3 1.3 collective-permute-start.8
  65.7 4.7 %collective-permute-start.7 = (f32[2,25,96]{2,0,1:T(2,128)S(1)}, f32[2,25,96]{2,0,1:T(2,128)S(1)}, u32[]{:S(2)}, u32[]{:S(2)}) collective-permute-start(f32[2,25,96]{2,0,1:T(2,128)S(1)} %pad_maximum_fusion.7), channel_id=1, source_target_pairs={{0,2},{2,4},{4,6},{6,8},{8,10},{10,12},{12,14},{14,16},{16,18},{18... | collective-permute-start | bytes 57608 | tf_op jit(solution)/shard_map/ppermute | solution.py:31
  71.6 1.1 gather_fusion.5
  72.8 1.1 gather_fusion.6
  75.7 2.0 scatter_custom_fusion.3
  78.1 2.8 scatter_fusion.2
  81.2 3.1 collective-permute-start.9
  85.2 1.3 collective-permute-start.10
  86.6 4.5 %collective-permute-start.11 = (f32[2,25,96]{2,0,1:T(2,128)S(1)}, f32[2,25,96]{2,0,1:T(2,128)S(1)}, u32[]{:S(2)}, u32[]{:S(2)}) collective-permute-start(f32[2,25,96]{2,0,1:T(2,128)S(1)} %pad_maximum_fusion.11), channel_id=1, source_target_pairs={{0,2},{2,4},{4,6},{6,8},{8,10},{10,12},{12,14},{14,16},{16,18},{18... | collective-permute-start | bytes 57608 | tf_op jit(solution)/shard_map/ppermute | solution.py:31
  91.4 28.5 %all-reduce.11 = (f32[]{:T(128)}, f32[]{:T(128)}) all-reduce(f32[]{:T(128)} %multiply_reduce_fusion.5, f32[]{:T(128)} %get-tuple-element.357), channel_id=1, replica_groups=mesh['sfc_0'=4,'sfc_1'=4,'sfc_2'=32,'grp'=2] {'sfc_0'}, use_global_device_ids=true, to_apply=%region_1.2 | all-reduce | flops 2 | bytes 16 | tf_op jit(solution)/shard_map/psum | solution.py:36
  119.9 6.6 %all-reduce.8 = (f32[]{:T(128)}, f32[]{:T(128)}) all-reduce(f32[]{:T(128)} %get-tuple-element.246, f32[]{:T(128)} %get-tuple-element.247), channel_id=1, replica_groups=mesh['sfc_0'=4,'sfc_1'=4,'sfc_2'=32,'grp'=2] {'sfc_1'}, use_global_device_ids=true, to_apply=%region_2.3 | all-reduce | flops 2 | bytes 16 | tf_op jit(solution)/shard_map/psum | solution.py:36
  126.5 42.1 %all-reduce.5 = (f32[]{:T(128)}, f32[]{:T(128)}) all-reduce(f32[]{:T(128)} %get-tuple-element.240, f32[]{:T(128)} %get-tuple-element.241), channel_id=1, replica_groups=mesh['sfc_0'=4,'sfc_1'=4,'sfc_2'=32,'grp'=2] {'sfc_2'}, use_global_device_ids=true, to_apply=%region_3.4 | all-reduce | flops 2 | bytes 16 | tf_op jit(solution)/shard_map/psum | solution.py:36
  168.6 21.5 %all-reduce.14 = (f32[]{:T(128)}, f32[]{:T(128)}) all-reduce(f32[]{:T(128)} %get-tuple-element.234, f32[]{:T(128)} %get-tuple-element.235), channel_id=1, replica_groups=mesh['sfc_0'=4,'sfc_1'=4,'sfc_2'=32,'grp'=2] {'grp'}, use_global_device_ids=true, to_apply=%region_4.5 | all-reduce | flops 2 | bytes 16 | tf_op jit(solution)/shard_map/psum | solution.py:36
  191.9 2.8 scatter_fusion.3
  196.5 1.1 gather_fusion.7
  197.9 2.3 collective-permute-start.12
  201.2 1.3 collective-permute-start.14
  202.5 4.2 %collective-permute-start.13 = (f32[2,25,96]{2,0,1:T(2,128)S(1)}, f32[2,25,96]{2,0,1:T(2,128)S(1)}, u32[]{:S(2)}, u32[]{:S(2)}) collective-permute-start(f32[2,25,96]{2,0,1:T(2,128)S(1)} %pad_maximum_fusion.13), channel_id=1, source_target_pairs={{0,2},{2,4},{4,6},{6,8},{8,10},{10,12},{12,14},{14,16},{16,18},{18... | collective-permute-start | bytes 57608 | tf_op jit(solution)/shard_map/ppermute | solution.py:31
  207.9 1.1 gather_fusion.8
  209.0 1.1 gather_fusion.9
  211.9 2.0 scatter_custom_fusion.6
  214.4 2.8 scatter_fusion.4
  217.5 3.3 collective-permute-start.15
  221.7 1.3 collective-permute-start.16
  223.0 4.6 %collective-permute-start.17 = (f32[2,25,96]{2,0,1:T(2,128)S(1)}, f32[2,25,96]{2,0,1:T(2,128)S(1)}, u32[]{:S(2)}, u32[]{:S(2)}) collective-permute-start(f32[2,25,96]{2,0,1:T(2,128)S(1)} %pad_maximum_fusion.17), channel_id=1, source_target_pairs={{0,2},{2,4},{4,6},{6,8},{8,10},{10,12},{12,14},{14,16},{16,18},{18... | collective-permute-start | bytes 57608 | tf_op jit(solution)/shard_map/ppermute | solution.py:31
  227.8 12.3 %all-reduce.10 = (f32[]{:T(128)}, f32[]{:T(128)}) all-reduce(f32[]{:T(128)} %get-tuple-element.229, f32[]{:T(128)} %get-tuple-element.228), channel_id=1, replica_groups=mesh['sfc_0'=4,'sfc_1'=4,'sfc_2'=32,'grp'=2] {'sfc_0'}, use_global_device_ids=true, to_apply=%region_16.19 | all-reduce | flops 2 | bytes 16 | tf_op jit(solution)/shard_map/psum | solution.py:36
  240.1 6.7 %all-reduce.7 = (f32[]{:T(128)}, f32[]{:T(128)}) all-reduce(f32[]{:T(128)} %get-tuple-element.244, f32[]{:T(128)} %get-tuple-element.245), channel_id=1, replica_groups=mesh['sfc_0'=4,'sfc_1'=4,'sfc_2'=32,'grp'=2] {'sfc_1'}, use_global_device_ids=true, to_apply=%region_17.20 | all-reduce | flops 2 | bytes 16 | tf_op jit(solution)/shard_map/psum | solution.py:36
  246.8 42.6 %all-reduce.4 = (f32[]{:T(128)}, f32[]{:T(128)}) all-reduce(f32[]{:T(128)} %get-tuple-element.238, f32[]{:T(128)} %get-tuple-element.239), channel_id=1, replica_groups=mesh['sfc_0'=4,'sfc_1'=4,'sfc_2'=32,'grp'=2] {'sfc_2'}, use_global_device_ids=true, to_apply=%region_18.21 | all-reduce | flops 2 | bytes 16 | tf_op jit(solution)/shard_map/psum | solution.py:36
  289.4 21.2 %all-reduce.13 = (f32[]{:T(128)}, f32[]{:T(128)}) all-reduce(f32[]{:T(128)} %get-tuple-element.232, f32[]{:T(128)} %get-tuple-element.233), channel_id=1, replica_groups=mesh['sfc_0'=4,'sfc_1'=4,'sfc_2'=32,'grp'=2] {'grp'}, use_global_device_ids=true, to_apply=%region_19.22 | all-reduce | flops 2 | bytes 16 | tf_op jit(solution)/shard_map/psum | solution.py:36
  315.6 2.8 scatter_fusion.5
  319.5 8.3 %all-reduce.9 = (f32[]{:T(128)}, f32[]{:T(128)}) all-reduce(f32[]{:T(128)} %get-tuple-element.227, f32[]{:T(128)} %get-tuple-element.226), channel_id=1, replica_groups=mesh['sfc_0'=4,'sfc_1'=4,'sfc_2'=32,'grp'=2] {'sfc_0'}, use_global_device_ids=true, to_apply=%region_31.34 | all-reduce | flops 2 | bytes 16 | tf_op jit(solution)/shard_map/psum | solution.py:36
  327.9 6.6 %all-reduce.6 = (f32[]{:T(128)}, f32[]{:T(128)}) all-reduce(f32[]{:T(128)} %get-tuple-element.242, f32[]{:T(128)} %get-tuple-element.243), channel_id=1, replica_groups=mesh['sfc_0'=4,'sfc_1'=4,'sfc_2'=32,'grp'=2] {'sfc_1'}, use_global_device_ids=true, to_apply=%region_32.35 | all-reduce | flops 2 | bytes 16 | tf_op jit(solution)/shard_map/psum | solution.py:36
  334.5 39.5 %all-reduce.3 = (f32[]{:T(128)}, f32[]{:T(128)}) all-reduce(f32[]{:T(128)} %get-tuple-element.236, f32[]{:T(128)} %get-tuple-element.237), channel_id=1, replica_groups=mesh['sfc_0'=4,'sfc_1'=4,'sfc_2'=32,'grp'=2] {'sfc_2'}, use_global_device_ids=true, to_apply=%region_33.36 | all-reduce | flops 2 | bytes 16 | tf_op jit(solution)/shard_map/psum | solution.py:36
  374.0 20.7 %all-reduce.12 = (f32[]{:T(128)}, f32[]{:T(128)}) all-reduce(f32[]{:T(128)} %get-tuple-element.230, f32[]{:T(128)} %get-tuple-element.231), channel_id=1, replica_groups=mesh['sfc_0'=4,'sfc_1'=4,'sfc_2'=32,'grp'=2] {'grp'}, use_global_device_ids=true, to_apply=%region_34.37 | all-reduce | flops 2 | bytes 16 | tf_op jit(solution)/shard_map/psum | solution.py:36
  (328 shorter events, 30.9 us)
Async XLA Ops:
  0.6 1.0 copy-start
  1.9 0.7 copy-start.7
  2.6 0.7 copy-start.8
  4.7 16.1 %copy-start.5 = (s32[384]{0:T(512)S(1)}, s32[384]{0:T(512)}, u32[]{:S(2)}) copy-start(s32[384]{0:T(512)} %param.53) | copy-start | bytes 4612
  4.8 22.1 %collective-permute-start = (f32[2,25,96]{2,0,1:T(2,128)S(1)}, f32[2,25,96]{2,0,1:T(2,128)S(1)}, u32[]{:S(2)}, u32[]{:S(2)}) collective-permute-start(f32[2,25,96]{2,0,1:T(2,128)S(1)} %pad_maximum_fusion), channel_id=1, source_target_pairs={{0,1},{1,0},{2,3},{3,2},{4,5},{5,4},{6,7},{7,6},{8,9},{9,8},{10,11... | collective-permute-start | bytes 57608 | tf_op jit(solution)/shard_map/ppermute | solution.py:25
  20.9 0.7 copy-start.3
  21.8 0.7 copy-start.1
  22.5 0.7 copy-start.11
  23.2 0.7 copy-start.6
  23.2 0.7 copy-start.9
  23.9 2.7 copy-start.10
  26.9 5.4 %copy-start.2 = (f32[4,25,25]{2,0,1:T(4,128)S(1)}, f32[4,25,25]{2,0,1:T(4,128)}, u32[]{:S(2)}) copy-start(f32[4,25,25]{2,0,1:T(4,128)} %param.59) | copy-start | bytes 30004
  27.0 5.7 %collective-permute-start.2 = (f32[2,25,96]{2,0,1:T(2,128)S(1)}, f32[2,25,96]{2,0,1:T(2,128)S(1)}, u32[]{:S(2)}, u32[]{:S(2)}) collective-permute-start(f32[2,25,96]{2,0,1:T(2,128)S(1)} %pad_maximum_fusion.2), channel_id=1, source_target_pairs={{2,0},{4,2},{6,4},{8,6},{10,8},{12,10},{14,12},{16,14},{18,16},{20... | collective-permute-start | bytes 57608 | tf_op jit(solution)/shard_map/ppermute | solution.py:31
  28.3 4.9 %collective-permute-start.1 = (f32[2,25,96]{2,0,1:T(2,128)S(1)}, f32[2,25,96]{2,0,1:T(2,128)S(1)}, u32[]{:S(2)}, u32[]{:S(2)}) collective-permute-start(f32[2,25,96]{2,0,1:T(2,128)S(1)} %pad_maximum_fusion.1), channel_id=1, source_target_pairs={{0,2},{2,4},{4,6},{6,8},{8,10},{10,12},{12,14},{14,16},{16,18},{18... | collective-permute-start | bytes 57608 | tf_op jit(solution)/shard_map/ppermute | solution.py:31
  43.3 3.9 collective-permute-start.3
  47.2 6.1 %collective-permute-start.4 = (f32[2,25,96]{2,0,1:T(2,128)S(1)}, f32[2,25,96]{2,0,1:T(2,128)S(1)}, u32[]{:S(2)}, u32[]{:S(2)}) collective-permute-start(f32[2,25,96]{2,0,1:T(2,128)S(1)} %pad_maximum_fusion.4), channel_id=1, source_target_pairs={{2,0},{4,2},{6,4},{8,6},{10,8},{12,10},{14,12},{16,14},{18,16},{20... | collective-permute-start | bytes 57608 | tf_op jit(solution)/shard_map/ppermute | solution.py:31
  48.6 5.5 %collective-permute-start.5 = (f32[2,25,96]{2,0,1:T(2,128)S(1)}, f32[2,25,96]{2,0,1:T(2,128)S(1)}, u32[]{:S(2)}, u32[]{:S(2)}) collective-permute-start(f32[2,25,96]{2,0,1:T(2,128)S(1)} %pad_maximum_fusion.5), channel_id=1, source_target_pairs={{0,2},{2,4},{4,6},{6,8},{8,10},{10,12},{12,14},{14,16},{16,18},{18... | collective-permute-start | bytes 57608 | tf_op jit(solution)/shard_map/ppermute | solution.py:31
  60.3 4.0 collective-permute-start.6
  64.3 6.7 %collective-permute-start.8 = (f32[2,25,96]{2,0,1:T(2,128)S(1)}, f32[2,25,96]{2,0,1:T(2,128)S(1)}, u32[]{:S(2)}, u32[]{:S(2)}) collective-permute-start(f32[2,25,96]{2,0,1:T(2,128)S(1)} %pad_maximum_fusion.8), channel_id=1, source_target_pairs={{2,0},{4,2},{6,4},{8,6},{10,8},{12,10},{14,12},{16,14},{18,16},{20... | collective-permute-start | bytes 57608 | tf_op jit(solution)/shard_map/ppermute | solution.py:31
  65.7 5.5 %collective-permute-start.7 = (f32[2,25,96]{2,0,1:T(2,128)S(1)}, f32[2,25,96]{2,0,1:T(2,128)S(1)}, u32[]{:S(2)}, u32[]{:S(2)}) collective-permute-start(f32[2,25,96]{2,0,1:T(2,128)S(1)} %pad_maximum_fusion.7), channel_id=1, source_target_pairs={{0,2},{2,4},{4,6},{6,8},{8,10},{10,12},{12,14},{14,16},{16,18},{18... | collective-permute-start | bytes 57608 | tf_op jit(solution)/shard_map/ppermute | solution.py:31
  81.2 4.0 collective-permute-start.9
  85.2 106.3 %collective-permute-start.10 = (f32[2,25,96]{2,0,1:T(2,128)S(1)}, f32[2,25,96]{2,0,1:T(2,128)S(1)}, u32[]{:S(2)}, u32[]{:S(2)}) collective-permute-start(f32[2,25,96]{2,0,1:T(2,128)S(1)} %pad_maximum_fusion.10), channel_id=1, source_target_pairs={{2,0},{4,2},{6,4},{8,6},{10,8},{12,10},{14,12},{16,14},{18,16},{20... | collective-permute-start | bytes 57608 | tf_op jit(solution)/shard_map/ppermute | solution.py:31
  86.6 105.0 %collective-permute-start.11 = (f32[2,25,96]{2,0,1:T(2,128)S(1)}, f32[2,25,96]{2,0,1:T(2,128)S(1)}, u32[]{:S(2)}, u32[]{:S(2)}) collective-permute-start(f32[2,25,96]{2,0,1:T(2,128)S(1)} %pad_maximum_fusion.11), channel_id=1, source_target_pairs={{0,2},{2,4},{4,6},{6,8},{8,10},{10,12},{12,14},{14,16},{16,18},{18... | collective-permute-start | bytes 57608 | tf_op jit(solution)/shard_map/ppermute | solution.py:31
  195.1 0.7 copy-start.4
  197.9 3.1 collective-permute-start.12
  201.2 5.8 %collective-permute-start.14 = (f32[2,25,96]{2,0,1:T(2,128)S(1)}, f32[2,25,96]{2,0,1:T(2,128)S(1)}, u32[]{:S(2)}, u32[]{:S(2)}) collective-permute-start(f32[2,25,96]{2,0,1:T(2,128)S(1)} %pad_maximum_fusion.14), channel_id=1, source_target_pairs={{2,0},{4,2},{6,4},{8,6},{10,8},{12,10},{14,12},{16,14},{18,16},{20... | collective-permute-start | bytes 57608 | tf_op jit(solution)/shard_map/ppermute | solution.py:31
  202.5 4.9 %collective-permute-start.13 = (f32[2,25,96]{2,0,1:T(2,128)S(1)}, f32[2,25,96]{2,0,1:T(2,128)S(1)}, u32[]{:S(2)}, u32[]{:S(2)}) collective-permute-start(f32[2,25,96]{2,0,1:T(2,128)S(1)} %pad_maximum_fusion.13), channel_id=1, source_target_pairs={{0,2},{2,4},{4,6},{6,8},{8,10},{10,12},{12,14},{14,16},{16,18},{18... | collective-permute-start | bytes 57608 | tf_op jit(solution)/shard_map/ppermute | solution.py:31
  217.5 4.1 %collective-permute-start.15 = (f32[2,25,96]{2,0,1:T(2,128)S(1)}, f32[2,25,96]{2,0,1:T(2,128)S(1)}, u32[]{:S(2)}, u32[]{:S(2)}) collective-permute-start(f32[2,25,96]{2,0,1:T(2,128)S(1)} %pad_maximum_fusion.15), channel_id=1, source_target_pairs={{0,1},{1,0},{2,3},{3,2},{4,5},{5,4},{6,7},{7,6},{8,9},{9,8},{10,11... | collective-permute-start | bytes 57608 | tf_op jit(solution)/shard_map/ppermute | solution.py:25
  221.7 93.6 %collective-permute-start.16 = (f32[2,25,96]{2,0,1:T(2,128)S(1)}, f32[2,25,96]{2,0,1:T(2,128)S(1)}, u32[]{:S(2)}, u32[]{:S(2)}) collective-permute-start(f32[2,25,96]{2,0,1:T(2,128)S(1)} %pad_maximum_fusion.16), channel_id=1, source_target_pairs={{2,0},{4,2},{6,4},{8,6},{10,8},{12,10},{14,12},{16,14},{18,16},{20... | collective-permute-start | bytes 57608 | tf_op jit(solution)/shard_map/ppermute | solution.py:31
  223.0 92.2 %collective-permute-start.17 = (f32[2,25,96]{2,0,1:T(2,128)S(1)}, f32[2,25,96]{2,0,1:T(2,128)S(1)}, u32[]{:S(2)}, u32[]{:S(2)}) collective-permute-start(f32[2,25,96]{2,0,1:T(2,128)S(1)} %pad_maximum_fusion.17), channel_id=1, source_target_pairs={{0,2},{2,4},{4,6},{6,8},{8,10},{10,12},{12,14},{14,16},{16,18},{18... | collective-permute-start | bytes 57608 | tf_op jit(solution)/shard_map/ppermute | solution.py:31
where the time goes:
time: 401 us; the launch traced here: 400 us
  blocking collectives  257 us (64%)
  starting transfers between devices  65.3 us (16%)
  other arithmetic  28.7 us (7%)
  local copies, waits for them, and re-layouts  27.7 us (7%)
  between operations  12.6 us (3%)
  matrix products  4.96 us (1%)
  waiting for transfers between devices  4.16 us (1%)
    psum x12, blocking collectives, one_axis_at_a_time(): value = lax.psum(value, axis)  257 us
    ppermute x12, starting transfers between devices, shifted(): return lax.ppermute(block, axis, route)  34.4 us
    ppermute x6, starting transfers between devices, partner_2(): return lax.ppermute(block, axis, route)  30.9 us
    scatter-add x3, other arithmetic, apply_operator(): gathered = gathered.at[:, near_slot].add(near_term.reshape(width, -1))  8.54 us
    scatter-add x3, other arithmetic, apply_operator(): local = gathered[:, :slots].at[:, send_slots].add(back)  8.33 us
  transfers between devices with their start and end apart: 18, of which 8 were waited for; matrix products, arithmetic and copies ran while one was open for 2% of the time, Pallas kernels for 0%

commit v1 on v0

--- a/solution.py
+++ b/solution.py
@@ -7,6 +7,7 @@
 
 NODES = 5
 ITERS = 3
+SIGMA = 32.0
 SFC = ("sfc_0", "sfc_1", "sfc_2")
 SFC_GRP = ("sfc_0", "sfc_1", "sfc_2", "grp")
 
@@ -31,10 +32,10 @@
     return lax.ppermute(block, axis, route)
 
 
-def one_axis_at_a_time(value, axes):
-    for axis in axes:
-        value = lax.psum(value, axis)
-    return value
+def sum_over(value, axes):
+    count = lax.axis_size(axes)
+    copies = lax.optimization_barrier(jnp.broadcast_to(value[None], (count,) + value.shape))
+    return jnp.sum(lax.all_to_all(copies, axes, 0, 0, tiled=True), axis=0)
 
 
 def node_tables():
@@ -162,6 +163,36 @@
     local = gathered[:, :slots].at[:, send_slots].add(back)
     faces = local.reshape(NODES, NODES, 6, count)
     return volume + lift_faces(faces)
+
+
+def coefficients(moments):
+    def inner(one, two, shift):
+        return sum(
+            one[i] * two[j] * moments[i + j + shift]
+            for i in range(len(one))
+            for j in range(len(two))
+        )
+
+    iterate, remains, search = [], [1.0], [1.0]
+    norm_now = moments[0]
+    for iteration in range(ITERS):
+        step = norm_now / inner(search, search, 1)
+        iterate = [
+            (iterate[i] if i < len(iterate) else 0.0) + step * search[i] for i in range(len(search))
+        ]
+        image = [0.0] + search
+        remains = [
+            (remains[i] if i < len(remains) else 0.0) - step * image[i] for i in range(len(image))
+        ]
+        if iteration + 1 < ITERS:
+            norm_next = inner(remains, remains, 0)
+            blend = norm_next / norm_now
+            search = [
+                remains[i] + (blend * search[i] if i < len(search) else 0.0)
+                for i in range(len(remains))
+            ]
+            norm_now = norm_next
+    return iterate, remains
 
 
 def body(
@@ -194,35 +225,16 @@
             tables,
         )
 
-    solution = jnp.zeros_like(right_side)
-    residual = right_side
-    weighted = operate(residual)
+    powers = [right_side]
     for iteration in range(ITERS):
-        totals = (
-            one_axis_at_a_time(jnp.sum(residual * residual), SFC_GRP),
-            one_axis_at_a_time(jnp.sum(weighted * residual), SFC_GRP),
-        )
-        more = iteration + 1 < ITERS
-        if more:
-            product = operate(weighted)
-        if iteration == 0:
-            step_size = totals[0] / totals[1]
-            carried = product
-            searched = weighted
-            direction = residual
-        else:
-            blend_ratio = totals[0] / norm_before
-            step_size = totals[0] / (totals[1] - blend_ratio * totals[0] / step_before)
-            if more:
-                carried = product + blend_ratio * carried
-            searched = weighted + blend_ratio * searched
-            direction = residual + blend_ratio * direction
-        solution = solution + step_size * direction
-        residual = residual - step_size * searched
-        if more:
-            weighted = weighted - step_size * carried
-        norm_before = totals[0]
-        step_before = step_size
+        powers.append(operate(powers[-1]) * (1.0 / SIGMA))
+    local = [jnp.sum(powers[(k + 0) // 2] * powers[(k + 1) // 2]) for k in range(2 * ITERS)]
+    totals = jnp.pad(jnp.stack(local), (0, 128 - 2 * ITERS))[None]
+    totals = sum_over(sum_over(totals, ("sfc_2",)), ("sfc_0", "sfc_1", "grp"))
+    moments = [totals[0, k] for k in range(2 * ITERS)]
+    iterate, remains = coefficients(moments)
+    solution = sum((c * (1.0 / SIGMA)) * v for c, v in zip(iterate, powers))
+    residual = sum(c * v for c, v in zip(remains, powers))
     return (solution, residual)
 
 

time: 401 us -> 224 us (0.56)
  blocking collectives: 257 us -> 69.8 us
  local copies, waits for them, and re-layouts: 27.7 us -> 32.3 us
    psum x12 -> x0, blocking collectives: 257 us -> none  [one_axis_at_a_time(): value = lax.psum(value, axis)]
    all_to_all x0 -> x2, blocking collectives: none -> 69.8 us  [sum_over(): return jnp.sum(lax.all_to_all(copies, axes, 0, 0, tiled=True), axis=0)]
  transfers between devices with their start and end apart: 18 -> 18, of which waited for: 8 -> 11; matrix products, arithmetic and copies ran while one was open for 2% -> 3% of each run, Pallas kernels for 0% -> 0%
where the time goes in v1:
time: 224 us; the launch traced here: 223 us
  blocking collectives  69.8 us (31%)
  starting transfers between devices  66.5 us (30%)
  local copies, waits for them, and re-layouts  32.3 us (14%)
  other arithmetic  28.7 us (13%)
  between operations  16 us (7%)
  waiting for transfers between devices  5.47 us (2%)
  matrix products  4.32 us (2%)
    all_to_all x2, blocking collectives, sum_over(): return jnp.sum(lax.all_to_all(copies, axes, 0, 0, tiled=True), axis=0)  69.8 us
    ppermute x12, starting transfers between devices, shifted(): return lax.ppermute(block, axis, route)  34.9 us
    ppermute x6, starting transfers between devices, partner_2(): return lax.ppermute(block, axis, route)  31.6 us
    scatter-add x3, other arithmetic, apply_operator(): gathered = gathered.at[:, near_slot].add(near_term.reshape(width, -1))  8.54 us
    scatter-add x3, other arithmetic, apply_operator(): local = gathered[:, :slots].at[:, send_slots].add(back)  8.33 us
    unnamed x65, local copies, waits for them, and re-layouts  6.76 us
    scatter-add x3, other arithmetic, apply_operator(): jnp.zeros_like(pool).at[:, own_slot].add(own_term.reshape(width, -1))  5.95 us
  transfers between devices with their start and end apart: 18, of which 11 were waited for; matrix products, arithmetic and copies ran while one was open for 3% of the time, Pallas kernels for 0%

profile of v1, /device:TPU:1, one launch (start us, length us, event | category | flops | bytes accessed | tf_op | source)
XLA Modules:
  0.0 223.1 jit_solution(6990405166315898151)
XLA Ops:
  0.6 1.0 copy.444
  2.6 0.7 copy-done.8
  3.3 1.1 gather_fusion.1
  4.8 16.1 %collective-permute-start = (f32[2,25,96]{2,0,1:T(2,128)S(1)}, f32[2,25,96]{2,0,1:T(2,128)S(1)}, u32[]{:S(2)}, u32[]{:S(2)}) collective-permute-start(f32[2,25,96]{2,0,1:T(2,128)S(1)} %pad_maximum_fusion), channel_id=1, source_target_pairs={{0,1},{1,0},{2,3},{3,2},{4,5},{5,4},{6,7},{7,6},{8,9},{9,8},{10,11... | collective-permute-start | bytes 57608 | tf_op jit(solution)/shard_map/ppermute | solution.py:26
  23.2 0.7 copy-done.6
  23.9 2.7 %gather_fusion = f32[384]{0:T(512)S(1)} fusion(f32[128]{0:T(128)S(1)} %get-tuple-element.346, s32[1024]{0:T(1024)S(1)} %get-tuple-element.352), kind=kCustom, calls=%fused_computation.9 | custom fusion | bytes 4608 | tf_op jit(solution)/shard_map/jit(_take)/gather | solution.py:212
  27.0 1.3 collective-permute-start.2
  28.3 4.0 %collective-permute-start.1 = (f32[2,25,96]{2,0,1:T(2,128)S(1)}, f32[2,25,96]{2,0,1:T(2,128)S(1)}, u32[]{:S(2)}, u32[]{:S(2)}) collective-permute-start(f32[2,25,96]{2,0,1:T(2,128)S(1)} %pad_maximum_fusion.1), channel_id=1, source_target_pairs={{0,2},{2,4},{4,6},{6,8},{8,10},{10,12},{12,14},{14,16},{16,18},{18... | collective-permute-start | bytes 57608 | tf_op jit(solution)/shard_map/ppermute | solution.py:32
  33.7 1.1 gather_fusion.2
  35.1 1.1 gather_fusion.3
  37.4 2.0 scatter_custom_fusion
  40.2 2.8 %scatter_fusion = f32[25,1152]{0,1:T(8,128)S(1)} fusion(f32[25,1152]{0,1:T(8,128)S(1)} %scatter_custom_fusion, s32[384]{0:T(512)S(1)} %get-tuple-element.347, f32[384,25]{1,0:T(8,128)S(1)} %copy.472), kind=kCustom, calls=%fused_computation.11 | custom fusion | flops 9600 | bytes 116736 | tf_op jit(solution)/shard_map/scatter-add | solution.py:154
  43.3 3.1 %collective-permute-start.3 = (f32[2,25,96]{2,0,1:T(2,128)S(1)}, f32[2,25,96]{2,0,1:T(2,128)S(1)}, u32[]{:S(2)}, u32[]{:S(2)}) collective-permute-start(f32[2,25,96]{2,0,1:T(2,128)S(1)} %pad_maximum_fusion.3), channel_id=1, source_target_pairs={{0,1},{1,0},{2,3},{3,2},{4,5},{5,4},{6,7},{7,6},{8,9},{9,8},{10,11... | collective-permute-start | bytes 57608 | tf_op jit(solution)/shard_map/ppermute | solution.py:26
  47.3 1.3 collective-permute-start.4
  48.6 4.5 %collective-permute-start.5 = (f32[2,25,96]{2,0,1:T(2,128)S(1)}, f32[2,25,96]{2,0,1:T(2,128)S(1)}, u32[]{:S(2)}, u32[]{:S(2)}) collective-permute-start(f32[2,25,96]{2,0,1:T(2,128)S(1)} %pad_maximum_fusion.5), channel_id=1, source_target_pairs={{0,2},{2,4},{4,6},{6,8},{8,10},{10,12},{12,14},{14,16},{16,18},{18... | collective-permute-start | bytes 57608 | tf_op jit(solution)/shard_map/ppermute | solution.py:32
  53.3 0.8 collective-permute-done.5
  54.4 2.8 %scatter_fusion.1 = f32[25,768]{0,1:T(8,128)S(1)} fusion(f32[25,768]{0,1:T(8,128)S(1)} %slice.949, s32[384]{0:T(512)S(1)} %get-tuple-element.348, f32[384,25]{1,0:T(8,128)S(1)} %copy.477), kind=kCustom, calls=%fused_computation.12 | custom fusion | flops 9600 | bytes 116736 | tf_op jit(solution)/shard_map/scatter-add | solution.py:163
  58.5 1.1 gather_fusion.4
  60.0 3.1 %collective-permute-start.6 = (f32[2,25,96]{2,0,1:T(2,128)S(1)}, f32[2,25,96]{2,0,1:T(2,128)S(1)}, u32[]{:S(2)}, u32[]{:S(2)}) collective-permute-start(f32[2,25,96]{2,0,1:T(2,128)S(1)} %pad_maximum_fusion.6), channel_id=1, source_target_pairs={{0,1},{1,0},{2,3},{3,2},{4,5},{5,4},{6,7},{7,6},{8,9},{9,8},{10,11... | collective-permute-start | bytes 57608 | tf_op jit(solution)/shard_map/ppermute | solution.py:26
  63.2 0.7 collective-permute-done.6
  64.0 1.3 collective-permute-start.8
  65.3 4.7 %collective-permute-start.7 = (f32[2,25,96]{2,0,1:T(2,128)S(1)}, f32[2,25,96]{2,0,1:T(2,128)S(1)}, u32[]{:S(2)}, u32[]{:S(2)}) collective-permute-start(f32[2,25,96]{2,0,1:T(2,128)S(1)} %pad_maximum_fusion.7), channel_id=1, source_target_pairs={{0,2},{2,4},{4,6},{6,8},{8,10},{10,12},{12,14},{14,16},{16,18},{18... | collective-permute-start | bytes 57608 | tf_op jit(solution)/shard_map/ppermute | solution.py:32
  71.3 1.1 gather_fusion.5
  72.4 1.1 gather_fusion.6
  75.3 2.0 scatter_custom_fusion.3
  77.8 2.8 %scatter_fusion.2 = f32[25,1152]{0,1:T(8,128)S(1)} fusion(f32[25,1152]{0,1:T(8,128)S(1)} %scatter_custom_fusion.3, s32[384]{0:T(512)S(1)} %get-tuple-element.347, f32[384,25]{1,0:T(8,128)S(1)} %copy.513), kind=kCustom, calls=%fused_computation.14 | custom fusion | flops 9600 | bytes 116736 | tf_op jit(solution)/shard_map/scatter-add | solution.py:154
  80.9 3.1 %collective-permute-start.9 = (f32[2,25,96]{2,0,1:T(2,128)S(1)}, f32[2,25,96]{2,0,1:T(2,128)S(1)}, u32[]{:S(2)}, u32[]{:S(2)}) collective-permute-start(f32[2,25,96]{2,0,1:T(2,128)S(1)} %pad_maximum_fusion.9), channel_id=1, source_target_pairs={{0,1},{1,0},{2,3},{3,2},{4,5},{5,4},{6,7},{7,6},{8,9},{9,8},{10,11... | collective-permute-start | bytes 57608 | tf_op jit(solution)/shard_map/ppermute | solution.py:26
  84.9 1.3 collective-permute-start.10
  86.2 4.6 %collective-permute-start.11 = (f32[2,25,96]{2,0,1:T(2,128)S(1)}, f32[2,25,96]{2,0,1:T(2,128)S(1)}, u32[]{:S(2)}, u32[]{:S(2)}) collective-permute-start(f32[2,25,96]{2,0,1:T(2,128)S(1)} %pad_maximum_fusion.11), channel_id=1, source_target_pairs={{0,2},{2,4},{4,6},{6,8},{8,10},{10,12},{12,14},{14,16},{16,18},{18... | collective-permute-start | bytes 57608 | tf_op jit(solution)/shard_map/ppermute | solution.py:32
  92.0 2.8 %scatter_fusion.3 = f32[25,768]{0,1:T(8,128)S(1)} fusion(f32[25,768]{0,1:T(8,128)S(1)} %slice.986, s32[384]{0:T(512)S(1)} %get-tuple-element.348, f32[384,25]{1,0:T(8,128)S(1)} %copy.518), kind=kCustom, calls=%fused_computation.15 | custom fusion | flops 9600 | bytes 116736 | tf_op jit(solution)/shard_map/scatter-add | solution.py:163
  96.6 1.1 gather_fusion.7
  98.1 3.1 %collective-permute-start.12 = (f32[2,25,96]{2,0,1:T(2,128)S(1)}, f32[2,25,96]{2,0,1:T(2,128)S(1)}, u32[]{:S(2)}, u32[]{:S(2)}) collective-permute-start(f32[2,25,96]{2,0,1:T(2,128)S(1)} %pad_maximum_fusion.12), channel_id=1, source_target_pairs={{0,1},{1,0},{2,3},{3,2},{4,5},{5,4},{6,7},{7,6},{8,9},{9,8},{10,11... | collective-permute-start | bytes 57608 | tf_op jit(solution)/shard_map/ppermute | solution.py:26
  102.1 1.3 collective-permute-start.14
  103.5 4.8 %collective-permute-start.13 = (f32[2,25,96]{2,0,1:T(2,128)S(1)}, f32[2,25,96]{2,0,1:T(2,128)S(1)}, u32[]{:S(2)}, u32[]{:S(2)}) collective-permute-start(f32[2,25,96]{2,0,1:T(2,128)S(1)} %pad_maximum_fusion.13), channel_id=1, source_target_pairs={{0,2},{2,4},{4,6},{6,8},{8,10},{10,12},{12,14},{14,16},{16,18},{18... | collective-permute-start | bytes 57608 | tf_op jit(solution)/shard_map/ppermute | solution.py:32
  109.4 1.1 gather_fusion.8
  110.5 1.1 gather_fusion.9
  113.4 2.0 scatter_custom_fusion.6
  115.9 2.8 %scatter_fusion.4 = f32[25,1152]{0,1:T(8,128)S(1)} fusion(f32[25,1152]{0,1:T(8,128)S(1)} %scatter_custom_fusion.6, s32[384]{0:T(512)S(1)} %get-tuple-element.347, f32[384,25]{1,0:T(8,128)S(1)} %copy.555), kind=kCustom, calls=%fused_computation.17 | custom fusion | flops 9600 | bytes 116736 | tf_op jit(solution)/shard_map/scatter-add | solution.py:154
  119.0 3.1 %collective-permute-start.15 = (f32[2,25,96]{2,0,1:T(2,128)S(1)}, f32[2,25,96]{2,0,1:T(2,128)S(1)}, u32[]{:S(2)}, u32[]{:S(2)}) collective-permute-start(f32[2,25,96]{2,0,1:T(2,128)S(1)} %pad_maximum_fusion.15), channel_id=1, source_target_pairs={{0,1},{1,0},{2,3},{3,2},{4,5},{5,4},{6,7},{7,6},{8,9},{9,8},{10,11... | collective-permute-start | bytes 57608 | tf_op jit(solution)/shard_map/ppermute | solution.py:26
  123.0 1.3 collective-permute-start.16
  124.3 4.6 %collective-permute-start.17 = (f32[2,25,96]{2,0,1:T(2,128)S(1)}, f32[2,25,96]{2,0,1:T(2,128)S(1)}, u32[]{:S(2)}, u32[]{:S(2)}) collective-permute-start(f32[2,25,96]{2,0,1:T(2,128)S(1)} %pad_maximum_fusion.17), channel_id=1, source_target_pairs={{0,2},{2,4},{4,6},{6,8},{8,10},{10,12},{12,14},{14,16},{16,18},{18... | collective-permute-start | bytes 57608 | tf_op jit(solution)/shard_map/ppermute | solution.py:32
  128.9 0.7 multiply_reduce_fusion.2
  130.2 2.8 %scatter_fusion.5 = f32[25,768]{0,1:T(8,128)S(1)} fusion(f32[25,768]{0,1:T(8,128)S(1)} %slice.1023, s32[384]{0:T(512)S(1)} %get-tuple-element.348, f32[384,25]{1,0:T(8,128)S(1)} %copy.560), kind=kCustom, calls=%fused_computation.18 | custom fusion | flops 9600 | bytes 116736 | tf_op jit(solution)/shard_map/scatter-add | solution.py:163
  133.4 0.8 multiply_reduce_fusion
  134.2 3.8 %stack.207 = f32[6]{0:T(128)S(1)} concatenate(f32[1]{0:T(128)} %bitcast, f32[1]{0:T(128)} %bitcast.33, f32[1]{0:T(128)} %bitcast.34, f32[1]{0:T(128)} %bitcast.60, f32[1]{0:T(128)} %bitcast.61, f32[1]{0:T(128)} %bitcast.91), dimensions={0} | concatenate | bytes 48 | tf_op jit(solution)/shard_map/stack | solution.py:232
  138.0 44.2 %all_to_all.10 = f32[32,1,128]{2,1,0:T(1,128)S(1)} all-to-all(f32[32,1,128]{2,1,0:T(1,128)S(1)} %broadcast_in_dim.181), channel_id=1, replica_groups=mesh['sfc_0'=4,'sfc_1'=4,'sfc_2'=32,'grp'=2] {'sfc_2'}, dimensions={0} | all-to-all | bytes 32768 | tf_op jit(solution)/shard_map/all_to_all | solution.py:38
  182.2 25.6 %all_to_all.11 = f32[32,1,128]{2,1,0:T(1,128)S(1)} all-to-all(f32[32,1,128]{2,1,0:T(1,128)S(1)} %broadcast_in_dim.182), channel_id=1, replica_groups=mesh['sfc_0'=4,'sfc_1'=4,'sfc_2'=32,'grp'=2] {'sfc_0','sfc_1','grp'}, dimensions={0} | all-to-all | bytes 32768 | tf_op jit(solution)/shard_map/all_to_all | solution.py:38
  207.9 0.7 fusion.81
  (332 shorter events, 25.5 us)
Async XLA Ops:
  0.6 1.0 copy-start
  1.9 0.7 copy-start.7
  2.6 0.7 copy-start.8
  4.7 16.1 %copy-start.5 = (s32[384]{0:T(512)S(1)}, s32[384]{0:T(512)}, u32[]{:S(2)}) copy-start(s32[384]{0:T(512)} %param.53) | copy-start | bytes 4612
  4.8 22.1 %collective-permute-start = (f32[2,25,96]{2,0,1:T(2,128)S(1)}, f32[2,25,96]{2,0,1:T(2,128)S(1)}, u32[]{:S(2)}, u32[]{:S(2)}) collective-permute-start(f32[2,25,96]{2,0,1:T(2,128)S(1)} %pad_maximum_fusion), channel_id=1, source_target_pairs={{0,1},{1,0},{2,3},{3,2},{4,5},{5,4},{6,7},{7,6},{8,9},{9,8},{10,11... | collective-permute-start | bytes 57608 | tf_op jit(solution)/shard_map/ppermute | solution.py:26
  20.9 0.7 copy-start.3
  21.8 0.7 copy-start.1
  22.5 0.7 copy-start.11
  23.2 0.7 copy-start.6
  23.2 0.7 copy-start.9
  23.9 2.7 %copy-start.10 = (f32[384]{0:T(512)S(1)}, f32[384]{0:T(512)}, u32[]{:S(2)}) copy-start(f32[384]{0:T(512)} %param.57) | copy-start | bytes 4612
  26.9 5.4 %copy-start.2 = (f32[4,25,25]{2,0,1:T(4,128)S(1)}, f32[4,25,25]{2,0,1:T(4,128)}, u32[]{:S(2)}) copy-start(f32[4,25,25]{2,0,1:T(4,128)} %param.59) | copy-start | bytes 30004
  27.0 5.7 %collective-permute-start.2 = (f32[2,25,96]{2,0,1:T(2,128)S(1)}, f32[2,25,96]{2,0,1:T(2,128)S(1)}, u32[]{:S(2)}, u32[]{:S(2)}) collective-permute-start(f32[2,25,96]{2,0,1:T(2,128)S(1)} %pad_maximum_fusion.2), channel_id=1, source_target_pairs={{2,0},{4,2},{6,4},{8,6},{10,8},{12,10},{14,12},{16,14},{18,16},{20... | collective-permute-start | bytes 57608 | tf_op jit(solution)/shard_map/ppermute | solution.py:32
  28.3 4.9 %collective-permute-start.1 = (f32[2,25,96]{2,0,1:T(2,128)S(1)}, f32[2,25,96]{2,0,1:T(2,128)S(1)}, u32[]{:S(2)}, u32[]{:S(2)}) collective-permute-start(f32[2,25,96]{2,0,1:T(2,128)S(1)} %pad_maximum_fusion.1), channel_id=1, source_target_pairs={{0,2},{2,4},{4,6},{6,8},{8,10},{10,12},{12,14},{14,16},{16,18},{18... | collective-permute-start | bytes 57608 | tf_op jit(solution)/shard_map/ppermute | solution.py:32
  43.3 3.9 %collective-permute-start.3 = (f32[2,25,96]{2,0,1:T(2,128)S(1)}, f32[2,25,96]{2,0,1:T(2,128)S(1)}, u32[]{:S(2)}, u32[]{:S(2)}) collective-permute-start(f32[2,25,96]{2,0,1:T(2,128)S(1)} %pad_maximum_fusion.3), channel_id=1, source_target_pairs={{0,1},{1,0},{2,3},{3,2},{4,5},{5,4},{6,7},{7,6},{8,9},{9,8},{10,11... | collective-permute-start | bytes 57608 | tf_op jit(solution)/shard_map/ppermute | solution.py:26
  47.3 6.0 %collective-permute-start.4 = (f32[2,25,96]{2,0,1:T(2,128)S(1)}, f32[2,25,96]{2,0,1:T(2,128)S(1)}, u32[]{:S(2)}, u32[]{:S(2)}) collective-permute-start(f32[2,25,96]{2,0,1:T(2,128)S(1)} %pad_maximum_fusion.4), channel_id=1, source_target_pairs={{2,0},{4,2},{6,4},{8,6},{10,8},{12,10},{14,12},{16,14},{18,16},{20... | collective-permute-start | bytes 57608 | tf_op jit(solution)/shard_map/ppermute | solution.py:32
  48.6 5.5 %collective-permute-start.5 = (f32[2,25,96]{2,0,1:T(2,128)S(1)}, f32[2,25,96]{2,0,1:T(2,128)S(1)}, u32[]{:S(2)}, u32[]{:S(2)}) collective-permute-start(f32[2,25,96]{2,0,1:T(2,128)S(1)} %pad_maximum_fusion.5), channel_id=1, source_target_pairs={{0,2},{2,4},{4,6},{6,8},{8,10},{10,12},{12,14},{14,16},{16,18},{18... | collective-permute-start | bytes 57608 | tf_op jit(solution)/shard_map/ppermute | solution.py:32
  60.0 3.9 %collective-permute-start.6 = (f32[2,25,96]{2,0,1:T(2,128)S(1)}, f32[2,25,96]{2,0,1:T(2,128)S(1)}, u32[]{:S(2)}, u32[]{:S(2)}) collective-permute-start(f32[2,25,96]{2,0,1:T(2,128)S(1)} %pad_maximum_fusion.6), channel_id=1, source_target_pairs={{0,1},{1,0},{2,3},{3,2},{4,5},{5,4},{6,7},{7,6},{8,9},{9,8},{10,11... | collective-permute-start | bytes 57608 | tf_op jit(solution)/shard_map/ppermute | solution.py:26
  64.0 6.7 %collective-permute-start.8 = (f32[2,25,96]{2,0,1:T(2,128)S(1)}, f32[2,25,96]{2,0,1:T(2,128)S(1)}, u32[]{:S(2)}, u32[]{:S(2)}) collective-permute-start(f32[2,25,96]{2,0,1:T(2,128)S(1)} %pad_maximum_fusion.8), channel_id=1, source_target_pairs={{2,0},{4,2},{6,4},{8,6},{10,8},{12,10},{14,12},{16,14},{18,16},{20... | collective-permute-start | bytes 57608 | tf_op jit(solution)/shard_map/ppermute | solution.py:32
  65.3 5.5 %collective-permute-start.7 = (f32[2,25,96]{2,0,1:T(2,128)S(1)}, f32[2,25,96]{2,0,1:T(2,128)S(1)}, u32[]{:S(2)}, u32[]{:S(2)}) collective-permute-start(f32[2,25,96]{2,0,1:T(2,128)S(1)} %pad_maximum_fusion.7), channel_id=1, source_target_pairs={{0,2},{2,4},{4,6},{6,8},{8,10},{10,12},{12,14},{14,16},{16,18},{18... | collective-permute-start | bytes 57608 | tf_op jit(solution)/shard_map/ppermute | solution.py:32
  80.9 3.9 %collective-permute-start.9 = (f32[2,25,96]{2,0,1:T(2,128)S(1)}, f32[2,25,96]{2,0,1:T(2,128)S(1)}, u32[]{:S(2)}, u32[]{:S(2)}) collective-permute-start(f32[2,25,96]{2,0,1:T(2,128)S(1)} %pad_maximum_fusion.9), channel_id=1, source_target_pairs={{0,1},{1,0},{2,3},{3,2},{4,5},{5,4},{6,7},{7,6},{8,9},{9,8},{10,11... | collective-permute-start | bytes 57608 | tf_op jit(solution)/shard_map/ppermute | solution.py:26
  84.9 6.2 %collective-permute-start.10 = (f32[2,25,96]{2,0,1:T(2,128)S(1)}, f32[2,25,96]{2,0,1:T(2,128)S(1)}, u32[]{:S(2)}, u32[]{:S(2)}) collective-permute-start(f32[2,25,96]{2,0,1:T(2,128)S(1)} %pad_maximum_fusion.10), channel_id=1, source_target_pairs={{2,0},{4,2},{6,4},{8,6},{10,8},{12,10},{14,12},{16,14},{18,16},{20... | collective-permute-start | bytes 57608 | tf_op jit(solution)/shard_map/ppermute | solution.py:32
  86.2 5.5 %collective-permute-start.11 = (f32[2,25,96]{2,0,1:T(2,128)S(1)}, f32[2,25,96]{2,0,1:T(2,128)S(1)}, u32[]{:S(2)}, u32[]{:S(2)}) collective-permute-start(f32[2,25,96]{2,0,1:T(2,128)S(1)} %pad_maximum_fusion.11), channel_id=1, source_target_pairs={{0,2},{2,4},{4,6},{6,8},{8,10},{10,12},{12,14},{14,16},{16,18},{18... | collective-permute-start | bytes 57608 | tf_op jit(solution)/shard_map/ppermute | solution.py:32
  95.3 0.7 copy-start.4
  98.1 3.9 %collective-permute-start.12 = (f32[2,25,96]{2,0,1:T(2,128)S(1)}, f32[2,25,96]{2,0,1:T(2,128)S(1)}, u32[]{:S(2)}, u32[]{:S(2)}) collective-permute-start(f32[2,25,96]{2,0,1:T(2,128)S(1)} %pad_maximum_fusion.12), channel_id=1, source_target_pairs={{0,1},{1,0},{2,3},{3,2},{4,5},{5,4},{6,7},{7,6},{8,9},{9,8},{10,11... | collective-permute-start | bytes 57608 | tf_op jit(solution)/shard_map/ppermute | solution.py:26
  102.1 6.4 %collective-permute-start.14 = (f32[2,25,96]{2,0,1:T(2,128)S(1)}, f32[2,25,96]{2,0,1:T(2,128)S(1)}, u32[]{:S(2)}, u32[]{:S(2)}) collective-permute-start(f32[2,25,96]{2,0,1:T(2,128)S(1)} %pad_maximum_fusion.14), channel_id=1, source_target_pairs={{2,0},{4,2},{6,4},{8,6},{10,8},{12,10},{14,12},{16,14},{18,16},{20... | collective-permute-start | bytes 57608 | tf_op jit(solution)/shard_map/ppermute | solution.py:32
  103.5 5.5 %collective-permute-start.13 = (f32[2,25,96]{2,0,1:T(2,128)S(1)}, f32[2,25,96]{2,0,1:T(2,128)S(1)}, u32[]{:S(2)}, u32[]{:S(2)}) collective-permute-start(f32[2,25,96]{2,0,1:T(2,128)S(1)} %pad_maximum_fusion.13), channel_id=1, source_target_pairs={{0,2},{2,4},{4,6},{6,8},{8,10},{10,12},{12,14},{14,16},{16,18},{18... | collective-permute-start | bytes 57608 | tf_op jit(solution)/shard_map/ppermute | solution.py:32
  119.0 4.0 %collective-permute-start.15 = (f32[2,25,96]{2,0,1:T(2,128)S(1)}, f32[2,25,96]{2,0,1:T(2,128)S(1)}, u32[]{:S(2)}, u32[]{:S(2)}) collective-permute-start(f32[2,25,96]{2,0,1:T(2,128)S(1)} %pad_maximum_fusion.15), channel_id=1, source_target_pairs={{0,1},{1,0},{2,3},{3,2},{4,5},{5,4},{6,7},{7,6},{8,9},{9,8},{10,11... | collective-permute-start | bytes 57608 | tf_op jit(solution)/shard_map/ppermute | solution.py:26
  123.0 6.6 %collective-permute-start.16 = (f32[2,25,96]{2,0,1:T(2,128)S(1)}, f32[2,25,96]{2,0,1:T(2,128)S(1)}, u32[]{:S(2)}, u32[]{:S(2)}) collective-permute-start(f32[2,25,96]{2,0,1:T(2,128)S(1)} %pad_maximum_fusion.16), channel_id=1, source_target_pairs={{2,0},{4,2},{6,4},{8,6},{10,8},{12,10},{14,12},{16,14},{18,16},{20... | collective-permute-start | bytes 57608 | tf_op jit(solution)/shard_map/ppermute | solution.py:32
  124.3 5.5 %collective-permute-start.17 = (f32[2,25,96]{2,0,1:T(2,128)S(1)}, f32[2,25,96]{2,0,1:T(2,128)S(1)}, u32[]{:S(2)}, u32[]{:S(2)}) collective-permute-start(f32[2,25,96]{2,0,1:T(2,128)S(1)} %pad_maximum_fusion.17), channel_id=1, source_target_pairs={{0,2},{2,4},{4,6},{6,8},{8,10},{10,12},{12,14},{14,16},{16,18},{18... | collective-permute-start | bytes 57608 | tf_op jit(solution)/shard_map/ppermute | solution.py:32

commit v2 on v1

v2 whole, which is shorter than its diff:
```python
import functools

import jax
import jax.numpy as jnp
import numpy as np
from jax import lax
from jax.experimental import pallas as pl
from jax.experimental.pallas import tpu as pltpu
from jax.sharding import Mesh
from jax.sharding import PartitionSpec as P

NODES = 5
WIDTH = 25
CELLS = 128
GHOST = 96
ITERS = 3
SIGMA = 32.0
MASS_SHIFT = 1.0
Z_AXIS = ("sfc_2",)
OTHERS = ("sfc_0", "sfc_1", "grp")
SFC = ("sfc_0", "sfc_1", "sfc_2")
SFC_GRP = ("sfc_0", "sfc_1", "sfc_2", "grp")
VMEM_LIMIT = 24 * 1024 * 1024

f32 = jnp.float32
bf16 = jnp.bfloat16
highest = lax.Precision.HIGHEST


def node_tables():
    points = np.array([-1.0, -np.sqrt(3.0 / 7.0), 0.0, np.sqrt(3.0 / 7.0), 1.0])
    weights = np.array([0.1, 49.0 / 90.0, 32.0 / 45.0, 49.0 / 90.0, 0.1])
    identity = np.eye(5)
    spacing = points[:, None] - points[None, :] + identity
    barycentric = 1.0 / np.prod(spacing, axis=1)
    offdiag = barycentric[None, :] / barycentric[:, None] / spacing
    diagonal = np.sum(1.0 / spacing, axis=1) - 1.0
    derivs = np.where(identity > 0.5, diagonal[:, None], offdiag)
    stiffness = derivs.T @ (weights[:, None] * derivs)
    return stiffness, weights


STIFFNESS, WEIGHTS = node_tables()
FACE_MASS = [float(WEIGHTS[t // 5] * WEIGHTS[t % 5]) for t in range(WIDTH)]


def volume_tables():
    mass = np.diag(WEIGHTS)
    grads = (
        np.kron(np.kron(STIFFNESS, mass), mass)
        + np.kron(np.kron(mass, STIFFNESS), mass)
        + np.kron(np.kron(mass, mass), STIFFNESS)
    )
    full = np.zeros((128, 128), np.float32)
    full[:125, :125] = grads
    column = np.zeros((128, 128), np.float32)
    column[:125] = np.diag(np.kron(np.kron(mass, mass), mass))[:, None] * MASS_SHIFT
    return full, column


def face_node(face, t):
    high, low = t // 5, t % 5
    side = 4 * (face % 2)
    if face < 2:
        return 25 * side + t
    if face < 4:
        return 25 * high + 5 * side + low
    return 25 * high + 5 * low + side


def split(value):
    first = value.astype(bf16).astype(f32)
    rest = value - first
    second = rest.astype(bf16).astype(f32)
    third = (rest - second).astype(bf16).astype(f32)
    return first, second, third


def rev_first(planes, mask):
    return [jnp.where(mask, planes[5 * (4 - t // 5) + t % 5], planes[t]) for t in range(WIDTH)]


def rev_second(planes, mask):
    return [jnp.where(mask, planes[5 * (t // 5) + 4 - t % 5], planes[t]) for t in range(WIDTH)]


def swap(planes, mask):
    return [jnp.where(mask, planes[5 * (t % 5) + t // 5], planes[t]) for t in range(WIDTH)]


def orient_masks(codes):
    codes = codes.astype(jnp.int32)
    return (codes & 1) == 1, (codes & 2) == 2, (codes & 4) == 4


def orient_forward(planes, masks):
    return swap(rev_second(rev_first(planes, masks[0]), masks[1]), masks[2])


def orient_back(planes, masks):
    return rev_first(rev_second(swap(planes, masks[2]), masks[1]), masks[0])


def read_planes(ref, count=WIDTH):
    return [ref[8 * t : 8 * t + 8, :] for t in range(count)]


def gather_planes(field, face, cell):
    rows = {}

    def at(node):
        if node not in rows:
            row = jnp.broadcast_to(field[node : node + 1, :], (8, 128))
            rows[node] = jnp.take_along_axis(row, cell, axis=1, mode="promise_in_bounds")
        return rows[node]

    masks = [face == k for k in range(5)]
    planes = []
    for t in range(WIDTH):
        value = at(face_node(5, t))
        for k in range(5):
            value = jnp.where(masks[k], at(face_node(k, t)), value)
        planes.append(value)
    return planes


def write_messages(source, both_ref, up_ref, down_ref):
    def pair(ref, start, sent, own):
        ref[pl.ds(start, 28, stride=2), :] = source[pl.ds(4 + sent, 28, stride=8), :]
        ref[pl.ds(start + 1, 28, stride=2), :] = source[pl.ds(own, 28, stride=8), :]

    pair(both_ref, 0, 0, 1)
    pair(both_ref, 56, 1, 0)
    pair(up_ref, 0, 2, 3)
    pair(down_ref, 0, 3, 2)


def first_kernel(
    rhs_ref,
    level_ref,
    own_ref,
    near_ref,
    kind_ref,
    orient_ref,
    penalty_ref,
    send_ref,
    field_ref,
    planes_ref,
    index_ref,
    both_ref,
    up_ref,
    down_ref,
):
    for a in range(5):
        for b in range(5):
            field_ref[25 * a + 5 * b : 25 * a + 5 * b + 5, :] = rhs_ref[a, b]
    field_ref[125:128, :] = jnp.zeros((3, 128), f32)
    own = own_ref[...]
    pieces = split(penalty_ref[...])
    rows = [
        (own >> 7).astype(f32),
        (own & 127).astype(f32),
        kind_ref[...].astype(f32),
        orient_ref[...].astype(f32),
        pieces[0],
        pieces[1],
        pieces[2],
        jnp.zeros((1, 384), f32),
    ]
    table = jnp.concatenate(rows, axis=0).astype(bf16)
    spot = lax.broadcasted_iota(jnp.int32, (512, 384), 0)
    lane = spot & 127
    wanted = jnp.where(lane < GHOST, 6 * CELLS + (spot >> 7) * GHOST + lane, -1)
    onehot = jnp.where(wanted == near_ref[...], 1.0, 0.0).astype(bf16)
    moved = lax.dot_general(
        table, onehot, (((1,), (1,)), ((), ())), preferred_element_type=f32
    )
    zeros = jnp.zeros((4, 128), f32)

    def upper(row):
        parts = [row[:, 128 * k : 128 * k + 128] for k in range(4)]
        return jnp.concatenate(parts + [zeros], axis=0)

    own_face, own_cell = upper(moved[0:1]), upper(moved[1:2])
    penalty = upper(moved[4:5] + moved[5:6] + moved[6:7])
    send = send_ref[...]
    sub = lax.broadcasted_iota(jnp.int32, (8, 128), 0)
    face = jnp.where(sub < 4, own_face.astype(jnp.int32), send >> 7)
    cell = jnp.where(sub < 4, own_cell.astype(jnp.int32), send & 127)
    index_ref[0:8, :] = face
    index_ref[8:16, :] = cell
    scale = jnp.exp2(-jnp.broadcast_to(level_ref[...], (8, 128)).astype(f32))
    scaled = penalty * jnp.take_along_axis(scale, cell, axis=1, mode="promise_in_bounds")
    for t, plane in enumerate(gather_planes(field_ref, face, cell)):
        planes_ref[8 * t : 8 * t + 8, :] = plane
    planes_ref[200:208, :] = upper(moved[2:3])
    planes_ref[208:216, :] = upper(moved[3:4])
    planes_ref[216:224, :] = scaled
    write_messages(planes_ref, both_ref, up_ref, down_ref)


def local_volume(field, level_ref, grads_ref, mass_ref):
    scale = jnp.exp2(-level_ref[...].astype(f32))
    grads = jnp.dot(grads_ref[...], field, precision=highest, preferred_element_type=f32)
    return scale * grads + (scale * scale * scale) * (mass_ref[...] * field)


def volume_kernel(field_ref, level_ref, grads_ref, mass_ref, volume_ref):
    volume_ref[...] = local_volume(field_ref[...], level_ref, grads_ref, mass_ref)


def map_sent(maps_ref, planes_ref, meta_ref, masks):
    turned = orient_forward(read_planes(planes_ref), masks)
    result = []
    for i in range(WIDTH):
        total = None
        for j in range(WIDTH):
            at = 8 * (WIDTH * j + i)
            term = maps_ref[at : at + 8, :] * turned[j]
            total = term if total is None else total + term
        result.append(total)
    return result


def middle_kernel(
    field_ref, level_ref, grads_ref, mass_ref, maps_ref, planes_ref, meta_ref, volume_ref, sent_ref
):
    volume_ref[...] = local_volume(field_ref[...], level_ref, grads_ref, mass_ref)
    masks = orient_masks(meta_ref[8:16, :])
    for t, plane in enumerate(map_sent(maps_ref, planes_ref, meta_ref, masks)):
        sent_ref[8 * t : 8 * t + 8, :] = plane


def read_messages(core_ref, partner_ref, below_ref, above_ref, got_ref):
    low = core_ref[0] == 0

    def rows(ref, start):
        return ref[pl.ds(start, 28, stride=2), :]

    def put(row, value):
        got_ref[pl.ds(row, 28, stride=8), :] = value

    for j, (from_below, from_above) in enumerate(((0, 1), (5, 4))):
        put(from_below, jnp.where(low, rows(below_ref, 56 + j), rows(partner_ref, j)))
        put(from_above, jnp.where(low, rows(partner_ref, 56 + j), rows(above_ref, 56 + j)))
    put(2, rows(below_ref, 0))
    put(7, rows(below_ref, 1))
    put(3, rows(above_ref, 0))
    put(6, rows(above_ref, 1))


def build_maps(plain_ref, turned_ref, kind, maps_ref):
    code = lax.broadcasted_iota(jnp.int32, (8, 128), 0)
    code = jnp.where(code < 4, code + 2, jnp.where(code == 4, 1, -1)).astype(f32)
    for half, table_ref in enumerate((plain_ref, turned_ref)):
        table = jnp.concatenate(split(table_ref[...]), axis=0)
        table = jnp.transpose(table).astype(bf16)
        chosen = []
        for row in range(4 * half, 4 * half + 4):
            chosen.append(jnp.where(code == kind[row : row + 1, :], 1.0, 0.0))
        chosen = jnp.concatenate(chosen, axis=1)
        chosen = jnp.concatenate([chosen] * 3, axis=0).astype(bf16)
        values = jnp.dot(table, chosen, preferred_element_type=f32)
        for k in range(4):
            maps_ref[pl.ds(4 * half + k, 640, stride=8), :] = values[:, 128 * k : 128 * k + 128]


def add_faces(volume_ref, planes, index_ref, pieces_ref, field_ref):
    for t, plane in enumerate(planes):
        pieces_ref[8 * t : 8 * t + 8, :] = plane
    pieces_ref[200:256, :] = jnp.zeros((56, 128), f32)
    face, cell = index_ref[0:8, :], index_ref[8:16, :]
    key = (face & 1) * 128 + cell
    axis = face >> 1
    slot = lax.broadcasted_iota(jnp.int32, (256, 128), 0)
    left, right = [], []
    for row in range(8):
        value = jnp.concatenate(split(pieces_ref[pl.ds(row, 32, stride=8), :]), axis=0)
        chosen = axis[row : row + 1, :]
        left.append(
            jnp.concatenate([jnp.where(chosen == k, value, 0.0) for k in range(3)], axis=0).astype(
                bf16
            )
        )
        right.append(jnp.where(slot == key[row : row + 1, :], 1.0, 0.0).astype(bf16))
    total = lax.dot_general(
        jnp.concatenate(left, axis=1),
        jnp.concatenate(right, axis=1),
        (((1,), (1,)), ((), ())),
        preferred_element_type=f32,
    )
    total = total * (1.0 / SIGMA)
    field_ref[...] = volume_ref[...] * (1.0 / SIGMA)
    for k in range(3):
        part = total[96 * k : 96 * k + 32] + total[96 * k + 32 : 96 * k + 64]
        part = part + total[96 * k + 64 : 96 * k + 96]
        for side in range(2):
            value = part[:WIDTH, 128 * side : 128 * side + 128]
            if k == 0:
                field_ref[100 * side : 100 * side + 25, :] += value
            elif k == 1:
                for a in range(5):
                    at = 25 * a + 20 * side
                    field_ref[at : at + 5, :] += value[5 * a : 5 * a + 5]
            else:
                field_ref[pl.ds(4 * side, 25, stride=5), :] += value


def combine(got_ref, planes_ref, sent, maps_ref, penalty, masks):
    sub = lax.broadcasted_iota(jnp.int32, (8, 128), 0)
    owned = sub < 4
    got = read_planes(got_ref)
    turned = orient_forward(got, masks)
    mixed = [
        jnp.where(owned, turned[t], (penalty * FACE_MASS[t]) * (got[t] - sent[t]))
        for t in range(WIDTH)
    ]
    mapped = []
    for i in range(WIDTH):
        total = None
        for j in range(WIDTH):
            at = 8 * (WIDTH * i + j)
            term = maps_ref[at : at + 8, :] * mixed[j]
            total = term if total is None else total + term
        mapped.append(total)
    back = orient_back(mapped, masks)
    return [
        jnp.where(
            owned,
            (penalty * FACE_MASS[t]) * (planes_ref[8 * t : 8 * t + 8, :] - mapped[t]),
            -back[t],
        )
        for t in range(WIDTH)
    ]


def next_messages(field_ref, index_ref, planes_ref, both_ref, up_ref, down_ref):
    face, cell = index_ref[0:8, :], index_ref[8:16, :]
    for t, plane in enumerate(gather_planes(field_ref, face, cell)):
        planes_ref[8 * t : 8 * t + 8, :] = plane
    planes_ref[200:224, :] = jnp.zeros((24, 128), f32)
    write_messages(planes_ref, both_ref, up_ref, down_ref)


def second_kernel(
    core_ref,
    partner_ref,
    below_ref,
    above_ref,
    old_ref,
    volume_ref,
    index_ref,
    plain_ref,
    turned_ref,
    field_ref,
    planes_ref,
    meta_ref,
    maps_ref,
    both_ref,
    up_ref,
    down_ref,
    got_ref,
    pieces_ref,
):
    read_messages(core_ref, partner_ref, below_ref, above_ref, got_ref)
    sub = lax.broadcasted_iota(jnp.int32, (8, 128), 0)
    for k in range(3):
        at = 200 + 8 * k
        meta_ref[8 * k : 8 * k + 8, :] = jnp.where(
            sub < 4, old_ref[at : at + 8, :], got_ref[at : at + 8, :]
        )
    masks = orient_masks(meta_ref[8:16, :])
    build_maps(plain_ref, turned_ref, meta_ref[0:8, :], maps_ref)
    sent = map_sent(maps_ref, old_ref, meta_ref, masks)
    planes = combine(got_ref, old_ref, sent, maps_ref, meta_ref[16:24, :], masks)
    add_faces(volume_ref, planes, index_ref, pieces_ref, field_ref)
    next_messages(field_ref, index_ref, planes_ref, both_ref, up_ref, down_ref)


def third_kernel(
    core_ref,
    partner_ref,
    below_ref,
    above_ref,
    old_ref,
    sent_ref,
    volume_ref,
    index_ref,
    meta_ref,
    maps_ref,
    field_ref,
    planes_ref,
    both_ref,
    up_ref,
    down_ref,
    got_ref,
    pieces_ref,
):
    read_messages(core_ref, partner_ref, below_ref, above_ref, got_ref)
    masks = orient_masks(meta_ref[8:16, :])
    sent = read_planes(sent_ref)
    planes = combine(got_ref, old_ref, sent, maps_ref, meta_ref[16:24, :], masks)
    add_faces(volume_ref, planes, index_ref, pieces_ref, field_ref)
    next_messages(field_ref, index_ref, planes_ref, both_ref, up_ref, down_ref)


def fourth_kernel(
    core_ref,
    partner_ref,
    below_ref,
    above_ref,
    old_ref,
    sent_ref,
    volume_ref,
    index_ref,
    meta_ref,
    maps_ref,
    power0_ref,
    power1_ref,
    power2_ref,
    field_ref,
    moments_ref,
    got_ref,
    pieces_ref,
):
    read_messages(core_ref, partner_ref, below_ref, above_ref, got_ref)
    masks = orient_masks(meta_ref[8:16, :])
    sent = read_planes(sent_ref)
    planes = combine(got_ref, old_ref, sent, maps_ref, meta_ref[16:24, :], masks)
    add_faces(volume_ref, planes, index_ref, pieces_ref, field_ref)
    powers = [power0_ref[...], power1_ref[...], power2_ref[...], field_ref[...]]
    lane = lax.broadcasted_iota(jnp.int32, (1, 128), 1)
    result = jnp.zeros((1, 128), f32)
    for k in range(2 * ITERS):
        row = jnp.sum(powers[k // 2] * powers[(k + 1) // 2], axis=0, keepdims=True)
        result = jnp.where(lane == k, jnp.sum(row, axis=1, keepdims=True), result)
    moments_ref[...] = jnp.broadcast_to(result, moments_ref.shape)


def repeat_sum_kernel(rows_ref, out_ref):
    total = jnp.sum(rows_ref[...], axis=0, keepdims=True)
    out_ref[...] = jnp.broadcast_to(total, out_ref.shape)


def coefficients(moments):
    def inner(one, two, shift):
        total = None
        for i in range(len(one)):
            for j in range(len(two)):
                term = one[i] * two[j] * moments[i + j + shift]
                total = term if total is None else total + term
        return total

    unit = jnp.ones_like(moments[0])
    none = jnp.zeros_like(moments[0])
    iterate, remains, search = [], [unit], [unit]
    norm_now = moments[0]
    for iteration in range(ITERS):
        step = norm_now / inner(search, search, 1)
        iterate = [
            (iterate[i] if i < len(iterate) else none) + step * search[i]
            for i in range(len(search))
        ]
        image = [none] + search
        remains = [
            (remains[i] if i < len(remains) else none) - step * image[i]
            for i in range(len(image))
        ]
        if iteration + 1 < ITERS:
            norm_next = inner(remains, remains, 0)
            blend = norm_next / norm_now
            search = [
                remains[i] + (blend * search[i] if i < len(search) else none)
                for i in range(len(remains))
            ]
            norm_now = norm_next
    return iterate, remains


def last_kernel(
    rows_ref, power0_ref, power1_ref, power2_ref, power3_ref, solution_ref, residual_ref
):
    total = jnp.sum(rows_ref[...], axis=0, keepdims=True)
    lane = lax.broadcasted_iota(jnp.int32, (1, 128), 1)
    moments = [
        jnp.broadcast_to(
            jnp.sum(jnp.where(lane == k, total, 0.0), axis=1, keepdims=True), (1, 128)
        )
        for k in range(2 * ITERS)
    ]
    iterate, remains = coefficients(moments)
    powers = (power0_ref, power1_ref, power2_ref, power3_ref)
    for a in range(5):
        for b in range(5):
            at = 25 * a + 5 * b
            values = [ref[at : at + 5, :] for ref in powers]
            answer = sum((c * (1.0 / SIGMA)) * v for c, v in zip(iterate, values))
            solution_ref[a, b] = answer
            residual_ref[a, b] = sum(c * v for c, v in zip(remains, values))


def call(kernel, outs, ins, scratch=(), scalars=0, flops=0, bytes_accessed=0):
    in_specs = [pl.BlockSpec(memory_space=pltpu.SMEM)] * scalars
    in_specs += [pl.BlockSpec(memory_space=pltpu.VMEM)] * (len(ins) - scalars)
    return pl.pallas_call(
        kernel,
        out_shape=[jax.ShapeDtypeStruct(shape, kind) for shape, kind in outs],
        in_specs=in_specs,
        out_specs=[pl.BlockSpec(memory_space=pltpu.VMEM)] * len(outs),
        scratch_shapes=list(scratch),
        compiler_params=pltpu.CompilerParams(vmem_limit_bytes=VMEM_LIMIT),
        cost_estimate=pl.CostEstimate(
            flops=flops, bytes_accessed=bytes_accessed, transcendentals=0
        ),
    )(*ins)


def shifted(block, axis, distance):
    devices = range(lax.axis_size(axis))
    route = [(i - distance, i) for i in devices if i - distance in devices]
    return lax.ppermute(block, axis, route)


def exchange(both, up, down):
    partner = lax.ppermute(both, "grp", [(0, 1), (1, 0)])
    below = shifted(jnp.concatenate([up, partner[:56]], axis=0), SFC, 1)
    above = shifted(jnp.concatenate([down, partner[56:]], axis=0), SFC, -1)
    return partner, below, above


def sum_over(rows, axes):
    return lax.all_to_all(rows, axes, 0, 0, tiled=True)


def body(
    right_side,
    cell_level,
    own_slot,
    near_slot,
    face_kind,
    orientation,
    penalty,
    send_slots,
    subface_maps,
):
    field_shape, planes_shape = ((128, 128), f32), ((256, 128), f32)
    messages = [((112, 128), f32), ((56, 128), f32), ((56, 128), f32)]
    core = lax.axis_index("grp").astype(jnp.int32).reshape(1)
    grads, mass = (jnp.asarray(table) for table in volume_tables())
    level = cell_level.reshape(1, 128)
    send = jnp.pad(send_slots.reshape(4, GHOST), ((4, 0), (0, 128 - GHOST)))
    identity = jnp.eye(WIDTH, dtype=f32)[None]
    plain, turned = (
        jnp.pad(
            jnp.concatenate([maps, identity], axis=0).reshape(5, WIDTH * WIDTH), ((0, 3), (0, 15))
        )
        for maps in (subface_maps, jnp.swapaxes(subface_maps, 1, 2))
    )
    power0, planes, index, *sends = call(
        first_kernel,
        [field_shape, planes_shape, ((16, 128), jnp.int32)] + messages,
        [right_side, level]
        + [a.reshape(1, -1) for a in (own_slot, near_slot, face_kind, orientation, penalty)]
        + [send],
    )
    scratch = [pltpu.VMEM((224, 128), f32), pltpu.VMEM((256, 128), f32)]
    got = exchange(*sends)
    (volume,) = call(volume_kernel, [field_shape], [power0, level, grads, mass], flops=10**7)
    power1, new_planes, meta, maps, *sends = call(
        second_kernel,
        [field_shape, planes_shape, ((24, 128), f32), ((5120, 128), f32)] + messages,
        [core, *got, planes, volume, index, plain, turned],
        scratch,
        scalars=1,
    )
    planes = new_planes

    def middle(field):
        return call(
            middle_kernel,
            [field_shape, planes_shape],
            [field, level, grads, mass, maps, planes, meta],
            flops=10**7,
        )

    got = exchange(*sends)
    volume, sent = middle(power1)
    power2, new_planes, *sends = call(
        third_kernel,
        [field_shape, planes_shape] + messages,
        [core, *got, planes, sent, volume, index, meta, maps],
        scratch,
        scalars=1,
    )
    planes = new_planes
    got = exchange(*sends)
    volume, sent = middle(power2)
    count = lax.axis_size(Z_AXIS)
    power3, rows = call(
        fourth_kernel,
        [field_shape, ((count, 128), f32)],
        [core, *got, planes, sent, volume, index, meta, maps, power0, power1, power2],
        scratch,
        scalars=1,
    )
    rows = sum_over(rows, Z_AXIS)
    (rows,) = call(repeat_sum_kernel, [((lax.axis_size(OTHERS), 128), f32)], [rows])
    rows = sum_over(rows, OTHERS)
    shape = (right_side.shape, f32)
    return tuple(
        call(last_kernel, [shape, shape], [rows, power0, power1, power2, power3])
    )


def solution(mesh):
    chips, cores = mesh.shape["sfc"], mesh.shape["grp"]
    sizes = (4, 4, chips // 16) if chips % 16 == 0 else (1, 1, chips)
    finer = Mesh(mesh.devices.reshape(*sizes, cores), SFC_GRP)
    split_cells = P(SFC_GRP)
    in_specs = (P(None, None, None, SFC_GRP),) + (split_cells,) * 7 + (P(),)
    out_specs = (P(None, None, None, SFC_GRP), P(None, None, None, SFC_GRP))
    return jax.shard_map(body, mesh=finer, in_specs=in_specs, out_specs=out_specs, check_vma=False)
```

time: 224 us -> 117 us (0.52)
  starting transfers between devices: 66.5 us -> 31.8 us
  other arithmetic: 28.7 us -> 0.06 us
  local copies, waits for them, and re-layouts: 32.3 us -> 12.4 us
  between operations: 16 us -> 0.9 us
  blocking collectives: 69.8 us -> 58.7 us
  Pallas kernels: 0 us -> 5.16 us
  matrix products: 4.32 us -> 0 us
    ppermute x12 -> x6, starting transfers between devices: 34.9 us -> 9.38 us  [shifted(): return lax.ppermute(block, axis, route)]
    scatter-add x19 -> x0, other arithmetic: 22.9 us -> none  [the longest x3 8.54 us: apply_operator(): gathered = gathered.at[:, near_slot].add(near_term.reshape(width, -1))]
    gather x10 -> x0, local copies, waits for them, and re-layouts: 12.8 us -> none  [the longest x3 3.37 us: apply_operator(): own_values = jnp.take(pool, own_slot, axis=1).reshape(NODES, NODES, -1)]
    all_to_all x2, blocking collectives: 69.8 us -> 58.7 us  [sum_over(): return lax.all_to_all(rows, axes, 0, 0, tiled=True)]
    ppermute x6 -> x3, starting transfers between devices: 31.6 us -> 22.4 us  [exchange(): partner = lax.ppermute(both, 'grp', [(0, 1), (1, 0)])]
    another operation x46 -> x0, local copies, waits for them, and re-layouts: 6.16 us -> none  [the longest x1 3.8 us: body(): totals = jnp.pad(jnp.stack(local), (0, 128 - 2 * ITERS))[None]]
    pallas_call x0 -> x9, Pallas kernels: none -> 5.16 us  [call(): pl.pallas_call(kernel, out_shape=[jax.ShapeDtypeStruct(shape, kind) for s...]
    dot_general x15 -> x0, matrix products: 4.32 us -> none  [the longest x6 2.26 us: map_traces(): jnp.dot(stacked.reshape(4 * width, width), flat, precision=highest)]
  transfers between devices with their start and end apart: 18 -> 9, of which waited for: 11 -> 5; matrix products, arithmetic and copies ran while one was open for 3% -> 2% of each run, Pallas kernels for 0% -> 1%
where the time goes in v2:
time: 117 us
  blocking collectives  58.7 us (50%)
  starting transfers between devices  31.8 us (27%)
  local copies, waits for them, and re-layouts  12.4 us (11%)
  waiting for transfers between devices  7.53 us (6%)
  Pallas kernels  5.16 us (4%)
    all_to_all x2, blocking collectives, sum_over(): return lax.all_to_all(rows, axes, 0, 0, tiled=True)  58.7 us
    ppermute x3, starting transfers between devices, exchange(): partner = lax.ppermute(both, 'grp', [(0, 1), (1, 0)])  22.4 us
    ppermute x6, starting transfers between devices, shifted(): return lax.ppermute(block, axis, route)  9.38 us
    unnamed x19, local copies, waits for them, and re-layouts  7.02 us
    ppermute x6, waiting for transfers between devices, shifted(): return lax.ppermute(block, axis, route)  5.78 us
    pallas_call x9, Pallas kernels, call(): pl.pallas_call(kernel, out_shape=[jax.ShapeDtypeStruct(shape, kind) for s...  5.16 us
    reshape x5, local copies, waits for them, and re-layouts, body(): a.reshape(1, -1)  3.41 us
  transfers between devices with their start and end apart: 9, of which 5 were waited for; matrix products, arithmetic and copies ran while one was open for 2% of the time, Pallas kernels for 1%

profile of v2, /device:TPU:1, one launch (start us, length us, event | category | flops | bytes accessed | tf_op | source)
XLA Modules:
  0.0 116.5 jit_solution(5525372407293725308)
XLA Ops:
  0.6 0.7 reshape.67.own_ref
  1.3 0.7 reshape.68.near_ref
  2.0 0.7 reshape.69.kind_ref
  2.7 0.7 reshape.70.orient_ref
  3.4 0.7 reshape.71.penalty_ref
  4.0 0.8 reshape.72
  4.8 0.9 copy-done.5
  5.7 0.7 copy-done.6
  6.4 0.4 shard_map.122
  6.8 16.1 %collective-permute-start = (f32[112,128]{1,0:T(8,128)S(1)}, f32[112,128]{1,0:T(8,128)S(1)}, u32[]{:S(2)}, u32[]{:S(2)}) collective-permute-start(f32[112,128]{1,0:T(8,128)S(1)} %get-tuple-element.26), channel_id=1, source_target_pairs={{0,1},{1,0},{2,3},{3,2},{4,5},{5,4},{6,7},{7,6},{8,9},{9,8},{10,11... | collective-permute-start | bytes 172040 | tf_op jit(solution)/shard_map/ppermute | solution.py:525
  22.9 0.1 reshape.73
  23.0 0.8 copy.17
  23.8 0.9 copy.18
  24.7 0.1 concatenate.34
  24.8 0.1 concatenate.32
  24.9 0.0 collective-permute-done.partner_ref
  24.9 1.3 %collective-permute-start.1 = (f32[112,128]{1,0:T(8,128)S(1)}, f32[112,128]{1,0:T(8,128)S(1)}, u32[]{:S(2)}, u32[]{:S(2)}) collective-permute-start(f32[112,128]{1,0:T(8,128)S(1)} %pad_maximum_fusion), channel_id=1, source_target_pairs={{0,2},{2,4},{4,6},{6,8},{8,10},{10,12},{12,14},{14,16},{16,18},{18... | collective-permute-start | bytes 172040 | tf_op jit(solution)/shard_map/ppermute | solution.py:521
  26.3 1.3 %collective-permute-start.2 = (f32[112,128]{1,0:T(8,128)S(1)}, f32[112,128]{1,0:T(8,128)S(1)}, u32[]{:S(2)}, u32[]{:S(2)}) collective-permute-start(f32[112,128]{1,0:T(8,128)S(1)} %pad_maximum_fusion.1), channel_id=1, source_target_pairs={{2,0},{4,2},{6,4},{8,6},{10,8},{12,10},{14,12},{16,14},{18,16},{20... | collective-permute-start | bytes 172040 | tf_op jit(solution)/shard_map/ppermute | solution.py:521
  27.6 0.0 copy-start
  27.6 0.8 copy-done
  28.5 0.8 copy-done.2
  29.3 0.7 copy-done.7
  30.0 0.2 shard_map.123.volume_ref
  30.2 1.5 %collective-permute-done.2.above_ref = f32[112,128]{1,0:T(8,128)S(1)} collective-permute-done((f32[112,128]{1,0:T(8,128)S(1)}, f32[112,128]{1,0:T(8,128)S(1)}, u32[]{:S(2)}, u32[]{:S(2)}) %collective-permute-start.2) | collective-permute-done | bytes 57376 | tf_op jit(solution)/shard_map/ppermute | solution.py:521
  31.7 1.6 %shard_map.124 = (f32[128,128]{1,0:T(8,128)S(1)}, f32[256,128]{1,0:T(8,128)S(1)}, f32[24,128]{1,0:T(8,128)S(1)}, f32[5120,128]{1,0:T(8,128)S(1)}, f32[112,128]{1...) custom-call(s32[1]{0:T(128)} %bitcast.core_ref, f32[112,128]{1,0:T(8,128)S(1)} %collective-permute-done.partner_ref, ...), custom_call_target="tpu_custom_call" | custom-call | tf_op jit(solution)/shard_map/pallas_call | solution.py:505
  33.3 2.7 %collective-permute-start.3 = (f32[112,128]{1,0:T(8,128)S(1)}, f32[112,128]{1,0:T(8,128)S(1)}, u32[]{:S(2)}, u32[]{:S(2)}) collective-permute-start(f32[112,128]{1,0:T(8,128)S(1)} %get-tuple-element.32), channel_id=1, source_target_pairs={{0,1},{1,0},{2,3},{3,2},{4,5},{5,4},{6,7},{7,6},{8,9},{9,8},{10,11... | collective-permute-start | bytes 172040 | tf_op jit(solution)/shard_map/ppermute | solution.py:525
  36.1 0.9 collective-permute-done.3.partner_ref
  36.9 2.0 %collective-permute-start.4 = (f32[112,128]{1,0:T(8,128)S(1)}, f32[112,128]{1,0:T(8,128)S(1)}, u32[]{:S(2)}, u32[]{:S(2)}) collective-permute-start(f32[112,128]{1,0:T(8,128)S(1)} %pad_maximum_fusion.2), channel_id=1, source_target_pairs={{0,2},{2,4},{4,6},{6,8},{8,10},{10,12},{12,14},{14,16},{16,18},{18... | collective-permute-start | bytes 172040 | tf_op jit(solution)/shard_map/ppermute | solution.py:521
  39.0 1.3 %collective-permute-start.5 = (f32[112,128]{1,0:T(8,128)S(1)}, f32[112,128]{1,0:T(8,128)S(1)}, u32[]{:S(2)}, u32[]{:S(2)}) collective-permute-start(f32[112,128]{1,0:T(8,128)S(1)} %pad_maximum_fusion.3), channel_id=1, source_target_pairs={{2,0},{4,2},{6,4},{8,6},{10,8},{12,10},{14,12},{16,14},{18,16},{20... | collective-permute-start | bytes 172040 | tf_op jit(solution)/shard_map/ppermute | solution.py:521
  40.3 0.0 copy-start.1
  40.3 0.8 copy-done.1
  41.1 0.8 copy-done.3
  42.0 0.7 copy-done.8
  42.6 0.3 shard_map.125
  42.9 0.0 collective-permute-done.4.below_ref
  43.0 1.0 collective-permute-done.5.above_ref
  43.9 0.7 shard_map.126
  44.7 3.6 %collective-permute-start.6 = (f32[112,128]{1,0:T(8,128)S(1)}, f32[112,128]{1,0:T(8,128)S(1)}, u32[]{:S(2)}, u32[]{:S(2)}) collective-permute-start(f32[112,128]{1,0:T(8,128)S(1)} %get-tuple-element.41), channel_id=1, source_target_pairs={{0,1},{1,0},{2,3},{3,2},{4,5},{5,4},{6,7},{7,6},{8,9},{9,8},{10,11... | collective-permute-start | bytes 172040 | tf_op jit(solution)/shard_map/ppermute | solution.py:525
  48.3 0.9 collective-permute-done.6.partner_ref
  49.2 2.2 %collective-permute-start.7 = (f32[112,128]{1,0:T(8,128)S(1)}, f32[112,128]{1,0:T(8,128)S(1)}, u32[]{:S(2)}, u32[]{:S(2)}) collective-permute-start(f32[112,128]{1,0:T(8,128)S(1)} %pad_maximum_fusion.4), channel_id=1, source_target_pairs={{0,2},{2,4},{4,6},{6,8},{8,10},{10,12},{12,14},{14,16},{16,18},{18... | collective-permute-start | bytes 172040 | tf_op jit(solution)/shard_map/ppermute | solution.py:521
  51.4 1.3 %collective-permute-start.8 = (f32[112,128]{1,0:T(8,128)S(1)}, f32[112,128]{1,0:T(8,128)S(1)}, u32[]{:S(2)}, u32[]{:S(2)}) collective-permute-start(f32[112,128]{1,0:T(8,128)S(1)} %pad_maximum_fusion.5), channel_id=1, source_target_pairs={{2,0},{4,2},{6,4},{8,6},{10,8},{12,10},{14,12},{16,14},{18,16},{20... | collective-permute-start | bytes 172040 | tf_op jit(solution)/shard_map/ppermute | solution.py:521
  52.7 0.3 shard_map.127
  53.0 0.0 collective-permute-done.7.below_ref
  53.0 3.3 %collective-permute-done.8.above_ref = f32[112,128]{1,0:T(8,128)S(1)} collective-permute-done((f32[112,128]{1,0:T(8,128)S(1)}, f32[112,128]{1,0:T(8,128)S(1)}, u32[]{:S(2)}, u32[]{:S(2)}) %collective-permute-start.8) | collective-permute-done | bytes 57376 | tf_op jit(solution)/shard_map/ppermute | solution.py:521
  56.3 0.7 shard_map.128
  57.0 41.6 %all_to_all.22 = f32[32,1,128]{2,1,0:T(1,128)S(1)} all-to-all(f32[32,1,128]{2,1,0:T(1,128)S(1)} %bitcast.14), channel_id=1, replica_groups=mesh['sfc_0'=4,'sfc_1'=4,'sfc_2'=32,'grp'=2] {'sfc_2'}, dimensions={0} | all-to-all | bytes 32768 | tf_op jit(solution)/shard_map/all_to_all | solution.py:532
  98.6 17.1 %all_to_all.23 = f32[32,1,128]{2,1,0:T(1,128)S(1)} all-to-all(f32[32,1,128]{2,1,0:T(1,128)S(1)} %bitcast.13), channel_id=1, replica_groups=mesh['sfc_0'=4,'sfc_1'=4,'sfc_2'=32,'grp'=2] {'sfc_0','sfc_1','grp'}, dimensions={0} | all-to-all | bytes 32768 | tf_op jit(solution)/shard_map/all_to_all | solution.py:532
  115.7 0.9 shard_map.130
  (24 shorter events, 0.1 us)
Async XLA Ops:
  4.8 0.9 copy-start.5
  5.7 0.7 copy-start.6
  6.8 18.1 %collective-permute-start = (f32[112,128]{1,0:T(8,128)S(1)}, f32[112,128]{1,0:T(8,128)S(1)}, u32[]{:S(2)}, u32[]{:S(2)}) collective-permute-start(f32[112,128]{1,0:T(8,128)S(1)} %get-tuple-element.26), channel_id=1, source_target_pairs={{0,1},{1,0},{2,3},{3,2},{4,5},{5,4},{6,7},{7,6},{8,9},{9,8},{10,11... | collective-permute-start | bytes 172040 | tf_op jit(solution)/shard_map/ppermute | solution.py:525
  24.9 5.2 %collective-permute-start.1 = (f32[112,128]{1,0:T(8,128)S(1)}, f32[112,128]{1,0:T(8,128)S(1)}, u32[]{:S(2)}, u32[]{:S(2)}) collective-permute-start(f32[112,128]{1,0:T(8,128)S(1)} %pad_maximum_fusion), channel_id=1, source_target_pairs={{0,2},{2,4},{4,6},{6,8},{8,10},{10,12},{12,14},{14,16},{16,18},{18... | collective-permute-start | bytes 172040 | tf_op jit(solution)/shard_map/ppermute | solution.py:521
  26.3 5.4 %collective-permute-start.2 = (f32[112,128]{1,0:T(8,128)S(1)}, f32[112,128]{1,0:T(8,128)S(1)}, u32[]{:S(2)}, u32[]{:S(2)}) collective-permute-start(f32[112,128]{1,0:T(8,128)S(1)} %pad_maximum_fusion.1), channel_id=1, source_target_pairs={{2,0},{4,2},{6,4},{8,6},{10,8},{12,10},{14,12},{16,14},{18,16},{20... | collective-permute-start | bytes 172040 | tf_op jit(solution)/shard_map/ppermute | solution.py:521
  27.6 0.8 copy-start
  28.5 0.8 copy-start.2
  29.3 0.7 copy-start.7
  33.3 3.6 %collective-permute-start.3 = (f32[112,128]{1,0:T(8,128)S(1)}, f32[112,128]{1,0:T(8,128)S(1)}, u32[]{:S(2)}, u32[]{:S(2)}) collective-permute-start(f32[112,128]{1,0:T(8,128)S(1)} %get-tuple-element.32), channel_id=1, source_target_pairs={{0,1},{1,0},{2,3},{3,2},{4,5},{5,4},{6,7},{7,6},{8,9},{9,8},{10,11... | collective-permute-start | bytes 172040 | tf_op jit(solution)/shard_map/ppermute | solution.py:525
  36.9 6.0 %collective-permute-start.4 = (f32[112,128]{1,0:T(8,128)S(1)}, f32[112,128]{1,0:T(8,128)S(1)}, u32[]{:S(2)}, u32[]{:S(2)}) collective-permute-start(f32[112,128]{1,0:T(8,128)S(1)} %pad_maximum_fusion.2), channel_id=1, source_target_pairs={{0,2},{2,4},{4,6},{6,8},{8,10},{10,12},{12,14},{14,16},{16,18},{18... | collective-permute-start | bytes 172040 | tf_op jit(solution)/shard_map/ppermute | solution.py:521
  39.0 4.9 %collective-permute-start.5 = (f32[112,128]{1,0:T(8,128)S(1)}, f32[112,128]{1,0:T(8,128)S(1)}, u32[]{:S(2)}, u32[]{:S(2)}) collective-permute-start(f32[112,128]{1,0:T(8,128)S(1)} %pad_maximum_fusion.3), channel_id=1, source_target_pairs={{2,0},{4,2},{6,4},{8,6},{10,8},{12,10},{14,12},{16,14},{18,16},{20... | collective-permute-start | bytes 172040 | tf_op jit(solution)/shard_map/ppermute | solution.py:521
  40.3 0.8 copy-start.1
  41.1 0.8 copy-start.3
  42.0 0.7 copy-start.8
  42.6 10.0 %copy-start.4 = (f32[128,128]{1,0:T(8,128)S(1)}, f32[128,128]{1,0:T(8,128)}, u32[]{:S(2)}) copy-start(f32[128,128]{1,0:T(8,128)} %constant.12.clone.grads_ref) | copy-start | bytes 196612
  44.7 4.5 %collective-permute-start.6 = (f32[112,128]{1,0:T(8,128)S(1)}, f32[112,128]{1,0:T(8,128)S(1)}, u32[]{:S(2)}, u32[]{:S(2)}) collective-permute-start(f32[112,128]{1,0:T(8,128)S(1)} %get-tuple-element.41), channel_id=1, source_target_pairs={{0,1},{1,0},{2,3},{3,2},{4,5},{5,4},{6,7},{7,6},{8,9},{9,8},{10,11... | collective-permute-start | bytes 172040 | tf_op jit(solution)/shard_map/ppermute | solution.py:525
  49.2 3.8 %collective-permute-start.7 = (f32[112,128]{1,0:T(8,128)S(1)}, f32[112,128]{1,0:T(8,128)S(1)}, u32[]{:S(2)}, u32[]{:S(2)}) collective-permute-start(f32[112,128]{1,0:T(8,128)S(1)} %pad_maximum_fusion.4), channel_id=1, source_target_pairs={{0,2},{2,4},{4,6},{6,8},{8,10},{10,12},{12,14},{14,16},{16,18},{18... | collective-permute-start | bytes 172040 | tf_op jit(solution)/shard_map/ppermute | solution.py:521
  51.4 4.9 %collective-permute-start.8 = (f32[112,128]{1,0:T(8,128)S(1)}, f32[112,128]{1,0:T(8,128)S(1)}, u32[]{:S(2)}, u32[]{:S(2)}) collective-permute-start(f32[112,128]{1,0:T(8,128)S(1)} %pad_maximum_fusion.5), channel_id=1, source_target_pairs={{2,0},{4,2},{6,4},{8,6},{10,8},{12,10},{14,12},{16,14},{18,16},{20... | collective-permute-start | bytes 172040 | tf_op jit(solution)/shard_map/ppermute | solution.py:521

commit v3 on v2

--- a/solution.py
+++ b/solution.py
@@ -136,6 +136,25 @@
 
 
 def first_kernel(
+    rhs_hbm,
+    level_hbm,
+    own_hbm,
+    near_hbm,
+    kind_hbm,
+    orient_hbm,
+    penalty_hbm,
+    send_hbm,
+    grads_hbm,
+    mass_hbm,
+    field_ref,
+    planes_ref,
+    index_ref,
+    scale_ref,
+    grads_ref,
+    mass_ref,
+    both_ref,
+    up_ref,
+    down_ref,
     rhs_ref,
     level_ref,
     own_ref,
@@ -144,13 +163,29 @@
     orient_ref,
     penalty_ref,
     send_ref,
-    field_ref,
-    planes_ref,
-    index_ref,
-    both_ref,
-    up_ref,
-    down_ref,
-):
+    sems,
+):
+    copies = [
+        pltpu.make_async_copy(source, target, sems.at[k])
+        for k, (source, target) in enumerate(
+            (
+                (own_hbm, own_ref.at[0]),
+                (near_hbm, near_ref.at[0]),
+                (kind_hbm, kind_ref.at[0]),
+                (orient_hbm, orient_ref.at[0]),
+                (penalty_hbm, penalty_ref.at[0]),
+                (send_hbm, send_ref.at[0]),
+                (level_hbm, level_ref.at[0]),
+                (rhs_hbm, rhs_ref),
+                (grads_hbm, grads_ref),
+                (mass_hbm, mass_ref),
+            )
+        )
+    ]
+    for copy in copies:
+        copy.start()
+    for copy in copies:
+        copy.wait()
     for a in range(5):
         for b in range(5):
             field_ref[25 * a + 5 * b : 25 * a + 5 * b + 5, :] = rhs_ref[a, b]
@@ -183,13 +218,19 @@
 
     own_face, own_cell = upper(moved[0:1]), upper(moved[1:2])
     penalty = upper(moved[4:5] + moved[5:6] + moved[6:7])
-    send = send_ref[...]
+    lanes = lax.broadcasted_iota(jnp.int32, (1, 128), 1)
+    send = [
+        jnp.where(lanes < GHOST, pltpu.roll(send_ref[...], (384 - GHOST * k) % 384, 1)[:, :128], 0)
+        for k in range(4)
+    ]
+    send = jnp.concatenate([jnp.zeros((4, 128), jnp.int32)] + send, axis=0)
     sub = lax.broadcasted_iota(jnp.int32, (8, 128), 0)
     face = jnp.where(sub < 4, own_face.astype(jnp.int32), send >> 7)
     cell = jnp.where(sub < 4, own_cell.astype(jnp.int32), send & 127)
     index_ref[0:8, :] = face
     index_ref[8:16, :] = cell
     scale = jnp.exp2(-jnp.broadcast_to(level_ref[...], (8, 128)).astype(f32))
+    scale_ref[...] = scale
     scaled = penalty * jnp.take_along_axis(scale, cell, axis=1, mode="promise_in_bounds")
     for t, plane in enumerate(gather_planes(field_ref, face, cell)):
         planes_ref[8 * t : 8 * t + 8, :] = plane
@@ -199,14 +240,39 @@
     write_messages(planes_ref, both_ref, up_ref, down_ref)
 
 
-def local_volume(field, level_ref, grads_ref, mass_ref):
-    scale = jnp.exp2(-level_ref[...].astype(f32))
+def local_volume(field, scale_ref, grads_ref, mass_ref):
+    scale = scale_ref[0:1, :]
     grads = jnp.dot(grads_ref[...], field, precision=highest, preferred_element_type=f32)
     return scale * grads + (scale * scale * scale) * (mass_ref[...] * field)
 
 
-def volume_kernel(field_ref, level_ref, grads_ref, mass_ref, volume_ref):
-    volume_ref[...] = local_volume(field_ref[...], level_ref, grads_ref, mass_ref)
+def volume_kernel(
+    field_ref,
+    scale_ref,
+    grads_ref,
+    mass_ref,
+    subface_hbm,
+    volume_ref,
+    plain_ref,
+    turned_ref,
+    subface_ref,
+    sem,
+):
+    copy = pltpu.make_async_copy(subface_hbm, subface_ref, sem)
+    copy.start()
+    volume_ref[...] = local_volume(field_ref[...], scale_ref, grads_ref, mass_ref)
+    plain_ref[...] = jnp.zeros((640, 128), f32)
+    turned_ref[...] = jnp.zeros((640, 128), f32)
+    copy.wait()
+    lane = lax.broadcasted_iota(jnp.int32, (4, WIDTH), 1)
+    sub = lax.broadcasted_iota(jnp.int32, (4, WIDTH), 0)
+    for i in range(WIDTH):
+        unit = jnp.where((lane == i) & (sub == 0), 1.0, 0.0)
+        rows = jnp.concatenate([subface_ref[i], unit], axis=0)
+        rows = jnp.concatenate(split(rows), axis=0)
+        columns = jnp.transpose(rows)
+        plain_ref[25 * i : 25 * i + 25, 0:24] = columns
+        turned_ref[pl.ds(i, 25, stride=25), 0:24] = columns
 
 
 def map_sent(maps_ref, planes_ref, meta_ref, masks):
@@ -223,9 +289,9 @@
 
 
 def middle_kernel(
-    field_ref, level_ref, grads_ref, mass_ref, maps_ref, planes_ref, meta_ref, volume_ref, sent_ref
-):
-    volume_ref[...] = local_volume(field_ref[...], level_ref, grads_ref, mass_ref)
+    field_ref, scale_ref, grads_ref, mass_ref, maps_ref, planes_ref, meta_ref, volume_ref, sent_ref
+):
+    volume_ref[...] = local_volume(field_ref[...], scale_ref, grads_ref, mass_ref)
     masks = orient_masks(meta_ref[8:16, :])
     for t, plane in enumerate(map_sent(maps_ref, planes_ref, meta_ref, masks)):
         sent_ref[8 * t : 8 * t + 8, :] = plane
@@ -253,13 +319,13 @@
     code = lax.broadcasted_iota(jnp.int32, (8, 128), 0)
     code = jnp.where(code < 4, code + 2, jnp.where(code == 4, 1, -1)).astype(f32)
     for half, table_ref in enumerate((plain_ref, turned_ref)):
-        table = jnp.concatenate(split(table_ref[...]), axis=0)
-        table = jnp.transpose(table).astype(bf16)
+        table = table_ref[...].astype(bf16)
         chosen = []
         for row in range(4 * half, 4 * half + 4):
             chosen.append(jnp.where(code == kind[row : row + 1, :], 1.0, 0.0))
         chosen = jnp.concatenate(chosen, axis=1)
-        chosen = jnp.concatenate([chosen] * 3, axis=0).astype(bf16)
+        unused = jnp.zeros((104, 512), f32)
+        chosen = jnp.concatenate([chosen] * 3 + [unused], axis=0).astype(bf16)
         values = jnp.dot(table, chosen, preferred_element_type=f32)
         for k in range(4):
             maps_ref[pl.ds(4 * half + k, 640, stride=8), :] = values[:, 128 * k : 128 * k + 128]
@@ -499,9 +565,13 @@
             residual_ref[a, b] = sum(c * v for c, v in zip(remains, values))
 
 
-def call(kernel, outs, ins, scratch=(), scalars=0, flops=0, bytes_accessed=0):
-    in_specs = [pl.BlockSpec(memory_space=pltpu.SMEM)] * scalars
-    in_specs += [pl.BlockSpec(memory_space=pltpu.VMEM)] * (len(ins) - scalars)
+def call(kernel, outs, ins, scratch=(), places=None, flops=0):
+    places = places or {}
+    ins = [
+        pltpu.with_memory_space_constraint(x, pltpu.HBM) if places.get(k) is pltpu.HBM else x
+        for k, x in enumerate(ins)
+    ]
+    in_specs = [pl.BlockSpec(memory_space=places.get(k, pltpu.VMEM)) for k in range(len(ins))]
     return pl.pallas_call(
         kernel,
         out_shape=[jax.ShapeDtypeStruct(shape, kind) for shape, kind in outs],
@@ -509,9 +579,7 @@
         out_specs=[pl.BlockSpec(memory_space=pltpu.VMEM)] * len(outs),
         scratch_shapes=list(scratch),
         compiler_params=pltpu.CompilerParams(vmem_limit_bytes=VMEM_LIMIT),
-        cost_estimate=pl.CostEstimate(
-            flops=flops, bytes_accessed=bytes_accessed, transcendentals=0
-        ),
+        cost_estimate=pl.CostEstimate(flops=flops, bytes_accessed=0, transcendentals=0),
     )(*ins)
 
 
@@ -546,32 +614,34 @@
     field_shape, planes_shape = ((128, 128), f32), ((256, 128), f32)
     messages = [((112, 128), f32), ((56, 128), f32), ((56, 128), f32)]
     core = lax.axis_index("grp").astype(jnp.int32).reshape(1)
-    grads, mass = (jnp.asarray(table) for table in volume_tables())
-    level = cell_level.reshape(1, 128)
-    send = jnp.pad(send_slots.reshape(4, GHOST), ((4, 0), (0, 128 - GHOST)))
-    identity = jnp.eye(WIDTH, dtype=f32)[None]
-    plain, turned = (
-        jnp.pad(
-            jnp.concatenate([maps, identity], axis=0).reshape(5, WIDTH * WIDTH), ((0, 3), (0, 15))
-        )
-        for maps in (subface_maps, jnp.swapaxes(subface_maps, 1, 2))
-    )
-    power0, planes, index, *sends = call(
+    tables = [jnp.asarray(table) for table in volume_tables()]
+    row, whole = ((1, 384), jnp.int32), ((128, 128), f32)
+    power0, planes, index, scale, grads, mass, *sends = call(
         first_kernel,
-        [field_shape, planes_shape, ((16, 128), jnp.int32)] + messages,
-        [right_side, level]
-        + [a.reshape(1, -1) for a in (own_slot, near_slot, face_kind, orientation, penalty)]
-        + [send],
+        [field_shape, planes_shape, ((16, 128), jnp.int32), ((8, 128), f32), whole, whole] + messages,
+        [right_side, cell_level, own_slot, near_slot, face_kind, orientation, penalty, send_slots]
+        + tables,
+        [pltpu.VMEM(right_side.shape, f32), pltpu.VMEM((1, 128), jnp.int32)]
+        + [pltpu.VMEM(*row)] * 4
+        + [pltpu.VMEM((1, 384), f32), pltpu.VMEM(*row), pltpu.SemaphoreType.DMA((10,))],
+        {k: pltpu.HBM for k in range(10)},
     )
     scratch = [pltpu.VMEM((224, 128), f32), pltpu.VMEM((256, 128), f32)]
     got = exchange(*sends)
-    (volume,) = call(volume_kernel, [field_shape], [power0, level, grads, mass], flops=10**7)
+    volume, plain, turned = call(
+        volume_kernel,
+        [field_shape, ((640, 128), f32), ((640, 128), f32)],
+        [power0, scale, grads, mass, jnp.transpose(subface_maps, (1, 0, 2))],
+        [pltpu.VMEM((WIDTH, 4, WIDTH), f32), pltpu.SemaphoreType.DMA],
+        {4: pltpu.HBM},
+        flops=10**7,
+    )
     power1, new_planes, meta, maps, *sends = call(
         second_kernel,
         [field_shape, planes_shape, ((24, 128), f32), ((5120, 128), f32)] + messages,
         [core, *got, planes, volume, index, plain, turned],
         scratch,
-        scalars=1,
+        {0: pltpu.SMEM},
     )
     planes = new_planes
 
@@ -579,7 +649,7 @@
         return call(
             middle_kernel,
             [field_shape, planes_shape],
-            [field, level, grads, mass, maps, planes, meta],
+            [field, scale, grads, mass, maps, planes, meta],
             flops=10**7,
         )
 
@@ -590,7 +660,7 @@
         [field_shape, planes_shape] + messages,
         [core, *got, planes, sent, volume, index, meta, maps],
         scratch,
-        scalars=1,
+        {0: pltpu.SMEM},
     )
     planes = new_planes
     got = exchange(*sends)
@@ -601,7 +671,7 @@
         [field_shape, ((count, 128), f32)],
         [core, *got, planes, sent, volume, index, meta, maps, power0, power1, power2],
         scratch,
-        scalars=1,
+        {0: pltpu.SMEM},
     )
     rows = sum_over(rows, Z_AXIS)
     (rows,) = call(repeat_sum_kernel, [((lax.axis_size(OTHERS), 128), f32)], [rows])

time: 117 us -> 110 us (0.940)
  local copies, waits for them, and re-layouts: 12.4 us -> 0.01 us
  waiting for transfers between devices: 7.53 us -> 11.9 us
  Pallas kernels: 5.16 us -> 6.98 us
    unnamed x19 -> x0, local copies, waits for them, and re-layouts: 7.02 us -> none
    reshape x6 -> x0, local copies, waits for them, and re-layouts: 4.18 us -> none  [the longest x5 3.41 us: body(): a.reshape(1, -1)]
    ppermute x6, waiting for transfers between devices: 5.78 us -> 9.24 us  [shifted(): return lax.ppermute(block, axis, route)]
    pallas_call x9, Pallas kernels: 5.16 us -> 6.98 us  [call(): pl.pallas_call(kernel, out_shape=[jax.ShapeDtypeStruct(shape, kind) for s...]
    ppermute x6, starting transfers between devices: 9.38 us -> 8.11 us  [shifted(): return lax.ppermute(block, axis, route)]
  transfers between devices with their start and end apart: 9 -> 9, of which waited for: 5 -> 6; matrix products, arithmetic and copies ran while one was open for 2% -> 0% of each run, Pallas kernels for 1% -> 1%
where the time goes in v3:
time: 110 us
  blocking collectives  59 us (54%)
  starting transfers between devices  31.3 us (28%)
  waiting for transfers between devices  11.9 us (11%)
  Pallas kernels  6.98 us (6%)
    all_to_all x2, blocking collectives, sum_over(): return lax.all_to_all(rows, axes, 0, 0, tiled=True)  59 us
    ppermute x3, starting transfers between devices, exchange(): partner = lax.ppermute(both, 'grp', [(0, 1), (1, 0)])  23.2 us
    ppermute x6, waiting for transfers between devices, shifted(): return lax.ppermute(block, axis, route)  9.24 us
    ppermute x6, starting transfers between devices, shifted(): return lax.ppermute(block, axis, route)  8.11 us
    pallas_call x9, Pallas kernels, call(): pl.pallas_call(kernel, out_shape=[jax.ShapeDtypeStruct(shape, kind) for s...  6.98 us
    ppermute x3, waiting for transfers between devices, exchange(): partner = lax.ppermute(both, 'grp', [(0, 1), (1, 0)])  2.61 us
  transfers between devices with their start and end apart: 9, of which 6 were waited for; matrix products, arithmetic and copies ran while one was open for 0% of the time, Pallas kernels for 1%

profile of v3, /device:TPU:1, one launch (start us, length us, event | category | flops | bytes accessed | tf_op | source)
XLA Modules:
  0.0 110.0 jit_solution(433600252281072581)
XLA Ops:
  0.6 1.5 %shard_map.122 = (f32[128,128]{1,0:T(8,128)S(1)}, f32[256,128]{1,0:T(8,128)S(1)}, s32[16,128]{1,0:T(8,128)S(1)}, f32[8,128]{1,0:T(8,128)S(1)}, f32[128,128]{1,0:...) custom-call(f32[5,5,5,128]{3,2,1,0:T(8,128)} %rhs_hbm.1, ...), custom_call_target="tpu_custom_call" | custom-call | tf_op jit(solution)/shard_map/pallas_call | solution.py:575
  2.2 16.1 %collective-permute-start = (f32[112,128]{1,0:T(8,128)S(1)}, f32[112,128]{1,0:T(8,128)S(1)}, u32[]{:S(2)}, u32[]{:S(2)}) collective-permute-start(f32[112,128]{1,0:T(8,128)S(1)} %get-tuple-element.32), channel_id=1, source_target_pairs={{0,1},{1,0},{2,3},{3,2},{4,5},{5,4},{6,7},{7,6},{8,9},{9,8},{10,11... | collective-permute-start | bytes 172040 | tf_op jit(solution)/shard_map/ppermute | solution.py:593
  18.2 0.9 collective-permute-done.partner_ref
  19.1 1.3 %collective-permute-start.1 = (f32[112,128]{1,0:T(8,128)S(1)}, f32[112,128]{1,0:T(8,128)S(1)}, u32[]{:S(2)}, u32[]{:S(2)}) collective-permute-start(f32[112,128]{1,0:T(8,128)S(1)} %pad_maximum_fusion), channel_id=1, source_target_pairs={{0,2},{2,4},{4,6},{6,8},{8,10},{10,12},{12,14},{14,16},{16,18},{18... | collective-permute-start | bytes 172040 | tf_op jit(solution)/shard_map/ppermute | solution.py:589
  20.4 1.3 %collective-permute-start.2 = (f32[112,128]{1,0:T(8,128)S(1)}, f32[112,128]{1,0:T(8,128)S(1)}, u32[]{:S(2)}, u32[]{:S(2)}) collective-permute-start(f32[112,128]{1,0:T(8,128)S(1)} %pad_maximum_fusion.1), channel_id=1, source_target_pairs={{2,0},{4,2},{6,4},{8,6},{10,8},{12,10},{14,12},{16,14},{18,16},{20... | collective-permute-start | bytes 172040 | tf_op jit(solution)/shard_map/ppermute | solution.py:589
  21.7 1.0 shard_map.123
  22.7 0.0 collective-permute-done.1.below_ref
  22.7 2.6 %collective-permute-done.2.above_ref = f32[112,128]{1,0:T(8,128)S(1)} collective-permute-done((f32[112,128]{1,0:T(8,128)S(1)}, f32[112,128]{1,0:T(8,128)S(1)}, u32[]{:S(2)}, u32[]{:S(2)}) %collective-permute-start.2) | collective-permute-done | bytes 57376 | tf_op jit(solution)/shard_map/ppermute | solution.py:589
  25.4 1.6 %shard_map.124 = (f32[128,128]{1,0:T(8,128)S(1)}, f32[256,128]{1,0:T(8,128)S(1)}, f32[24,128]{1,0:T(8,128)S(1)}, f32[5120,128]{1,0:T(8,128)S(1)}, f32[112,128]{1...) custom-call(s32[1]{0:T(128)} %bitcast.core_ref, f32[112,128]{1,0:T(8,128)S(1)} %collective-permute-done.partner_ref, ...), custom_call_target="tpu_custom_call" | custom-call | tf_op jit(solution)/shard_map/pallas_call | solution.py:575
  26.9 3.4 %collective-permute-start.3 = (f32[112,128]{1,0:T(8,128)S(1)}, f32[112,128]{1,0:T(8,128)S(1)}, u32[]{:S(2)}, u32[]{:S(2)}) collective-permute-start(f32[112,128]{1,0:T(8,128)S(1)} %get-tuple-element.44), channel_id=1, source_target_pairs={{0,1},{1,0},{2,3},{3,2},{4,5},{5,4},{6,7},{7,6},{8,9},{9,8},{10,11... | collective-permute-start | bytes 172040 | tf_op jit(solution)/shard_map/ppermute | solution.py:593
  30.4 0.9 collective-permute-done.3.partner_ref
  31.2 1.3 %collective-permute-start.4 = (f32[112,128]{1,0:T(8,128)S(1)}, f32[112,128]{1,0:T(8,128)S(1)}, u32[]{:S(2)}, u32[]{:S(2)}) collective-permute-start(f32[112,128]{1,0:T(8,128)S(1)} %pad_maximum_fusion.2), channel_id=1, source_target_pairs={{0,2},{2,4},{4,6},{6,8},{8,10},{10,12},{12,14},{14,16},{16,18},{18... | collective-permute-start | bytes 172040 | tf_op jit(solution)/shard_map/ppermute | solution.py:589
  32.6 1.3 %collective-permute-start.5 = (f32[112,128]{1,0:T(8,128)S(1)}, f32[112,128]{1,0:T(8,128)S(1)}, u32[]{:S(2)}, u32[]{:S(2)}) collective-permute-start(f32[112,128]{1,0:T(8,128)S(1)} %pad_maximum_fusion.3), channel_id=1, source_target_pairs={{2,0},{4,2},{6,4},{8,6},{10,8},{12,10},{14,12},{16,14},{18,16},{20... | collective-permute-start | bytes 172040 | tf_op jit(solution)/shard_map/ppermute | solution.py:589
  33.9 0.3 shard_map.125
  34.2 0.0 collective-permute-done.4.below_ref
  34.2 3.3 %collective-permute-done.5.above_ref = f32[112,128]{1,0:T(8,128)S(1)} collective-permute-done((f32[112,128]{1,0:T(8,128)S(1)}, f32[112,128]{1,0:T(8,128)S(1)}, u32[]{:S(2)}, u32[]{:S(2)}) %collective-permute-start.5) | collective-permute-done | bytes 57376 | tf_op jit(solution)/shard_map/ppermute | solution.py:589
  37.5 0.7 shard_map.126
  38.2 3.7 %collective-permute-start.6 = (f32[112,128]{1,0:T(8,128)S(1)}, f32[112,128]{1,0:T(8,128)S(1)}, u32[]{:S(2)}, u32[]{:S(2)}) collective-permute-start(f32[112,128]{1,0:T(8,128)S(1)} %get-tuple-element.53), channel_id=1, source_target_pairs={{0,1},{1,0},{2,3},{3,2},{4,5},{5,4},{6,7},{7,6},{8,9},{9,8},{10,11... | collective-permute-start | bytes 172040 | tf_op jit(solution)/shard_map/ppermute | solution.py:593
  41.9 0.9 collective-permute-done.6.partner_ref
  42.8 1.6 %collective-permute-start.7 = (f32[112,128]{1,0:T(8,128)S(1)}, f32[112,128]{1,0:T(8,128)S(1)}, u32[]{:S(2)}, u32[]{:S(2)}) collective-permute-start(f32[112,128]{1,0:T(8,128)S(1)} %pad_maximum_fusion.4), channel_id=1, source_target_pairs={{0,2},{2,4},{4,6},{6,8},{8,10},{10,12},{12,14},{14,16},{16,18},{18... | collective-permute-start | bytes 172040 | tf_op jit(solution)/shard_map/ppermute | solution.py:589
  44.5 1.3 %collective-permute-start.8 = (f32[112,128]{1,0:T(8,128)S(1)}, f32[112,128]{1,0:T(8,128)S(1)}, u32[]{:S(2)}, u32[]{:S(2)}) collective-permute-start(f32[112,128]{1,0:T(8,128)S(1)} %pad_maximum_fusion.5), channel_id=1, source_target_pairs={{2,0},{4,2},{6,4},{8,6},{10,8},{12,10},{14,12},{16,14},{18,16},{20... | collective-permute-start | bytes 172040 | tf_op jit(solution)/shard_map/ppermute | solution.py:589
  45.8 0.3 shard_map.127
  46.1 0.0 collective-permute-done.7.below_ref
  46.1 3.3 %collective-permute-done.8.above_ref = f32[112,128]{1,0:T(8,128)S(1)} collective-permute-done((f32[112,128]{1,0:T(8,128)S(1)}, f32[112,128]{1,0:T(8,128)S(1)}, u32[]{:S(2)}, u32[]{:S(2)}) %collective-permute-start.8) | collective-permute-done | bytes 57376 | tf_op jit(solution)/shard_map/ppermute | solution.py:589
  49.4 0.7 shard_map.128
  50.1 42.3 %all_to_all.22 = f32[32,1,128]{2,1,0:T(1,128)S(1)} all-to-all(f32[32,1,128]{2,1,0:T(1,128)S(1)} %bitcast.13), channel_id=1, replica_groups=mesh['sfc_0'=4,'sfc_1'=4,'sfc_2'=32,'grp'=2] {'sfc_2'}, dimensions={0} | all-to-all | bytes 32768 | tf_op jit(solution)/shard_map/all_to_all | solution.py:600
  92.3 16.8 %all_to_all.23 = f32[32,1,128]{2,1,0:T(1,128)S(1)} all-to-all(f32[32,1,128]{2,1,0:T(1,128)S(1)} %bitcast.12), channel_id=1, replica_groups=mesh['sfc_0'=4,'sfc_1'=4,'sfc_2'=32,'grp'=2] {'sfc_0','sfc_1','grp'}, dimensions={0} | all-to-all | bytes 32768 | tf_op jit(solution)/shard_map/all_to_all | solution.py:600
  109.1 0.9 shard_map.130
  (10 shorter events, 0.1 us)
Async XLA Ops:
  2.2 16.9 %collective-permute-start = (f32[112,128]{1,0:T(8,128)S(1)}, f32[112,128]{1,0:T(8,128)S(1)}, u32[]{:S(2)}, u32[]{:S(2)}) collective-permute-start(f32[112,128]{1,0:T(8,128)S(1)} %get-tuple-element.32), channel_id=1, source_target_pairs={{0,1},{1,0},{2,3},{3,2},{4,5},{5,4},{6,7},{7,6},{8,9},{9,8},{10,11... | collective-permute-start | bytes 172040 | tf_op jit(solution)/shard_map/ppermute | solution.py:593
  19.1 3.6 %collective-permute-start.1 = (f32[112,128]{1,0:T(8,128)S(1)}, f32[112,128]{1,0:T(8,128)S(1)}, u32[]{:S(2)}, u32[]{:S(2)}) collective-permute-start(f32[112,128]{1,0:T(8,128)S(1)} %pad_maximum_fusion), channel_id=1, source_target_pairs={{0,2},{2,4},{4,6},{6,8},{8,10},{10,12},{12,14},{14,16},{16,18},{18... | collective-permute-start | bytes 172040 | tf_op jit(solution)/shard_map/ppermute | solution.py:589
  20.4 4.9 %collective-permute-start.2 = (f32[112,128]{1,0:T(8,128)S(1)}, f32[112,128]{1,0:T(8,128)S(1)}, u32[]{:S(2)}, u32[]{:S(2)}) collective-permute-start(f32[112,128]{1,0:T(8,128)S(1)} %pad_maximum_fusion.1), channel_id=1, source_target_pairs={{2,0},{4,2},{6,4},{8,6},{10,8},{12,10},{14,12},{16,14},{18,16},{20... | collective-permute-start | bytes 172040 | tf_op jit(solution)/shard_map/ppermute | solution.py:589
  26.9 4.3 %collective-permute-start.3 = (f32[112,128]{1,0:T(8,128)S(1)}, f32[112,128]{1,0:T(8,128)S(1)}, u32[]{:S(2)}, u32[]{:S(2)}) collective-permute-start(f32[112,128]{1,0:T(8,128)S(1)} %get-tuple-element.44), channel_id=1, source_target_pairs={{0,1},{1,0},{2,3},{3,2},{4,5},{5,4},{6,7},{7,6},{8,9},{9,8},{10,11... | collective-permute-start | bytes 172040 | tf_op jit(solution)/shard_map/ppermute | solution.py:593
  31.2 2.9 %collective-permute-start.4 = (f32[112,128]{1,0:T(8,128)S(1)}, f32[112,128]{1,0:T(8,128)S(1)}, u32[]{:S(2)}, u32[]{:S(2)}) collective-permute-start(f32[112,128]{1,0:T(8,128)S(1)} %pad_maximum_fusion.2), channel_id=1, source_target_pairs={{0,2},{2,4},{4,6},{6,8},{8,10},{10,12},{12,14},{14,16},{16,18},{18... | collective-permute-start | bytes 172040 | tf_op jit(solution)/shard_map/ppermute | solution.py:589
  32.6 4.9 %collective-permute-start.5 = (f32[112,128]{1,0:T(8,128)S(1)}, f32[112,128]{1,0:T(8,128)S(1)}, u32[]{:S(2)}, u32[]{:S(2)}) collective-permute-start(f32[112,128]{1,0:T(8,128)S(1)} %pad_maximum_fusion.3), channel_id=1, source_target_pairs={{2,0},{4,2},{6,4},{8,6},{10,8},{12,10},{14,12},{16,14},{18,16},{20... | collective-permute-start | bytes 172040 | tf_op jit(solution)/shard_map/ppermute | solution.py:589
  38.2 4.6 %collective-permute-start.6 = (f32[112,128]{1,0:T(8,128)S(1)}, f32[112,128]{1,0:T(8,128)S(1)}, u32[]{:S(2)}, u32[]{:S(2)}) collective-permute-start(f32[112,128]{1,0:T(8,128)S(1)} %get-tuple-element.53), channel_id=1, source_target_pairs={{0,1},{1,0},{2,3},{3,2},{4,5},{5,4},{6,7},{7,6},{8,9},{9,8},{10,11... | collective-permute-start | bytes 172040 | tf_op jit(solution)/shard_map/ppermute | solution.py:593
  42.8 3.3 %collective-permute-start.7 = (f32[112,128]{1,0:T(8,128)S(1)}, f32[112,128]{1,0:T(8,128)S(1)}, u32[]{:S(2)}, u32[]{:S(2)}) collective-permute-start(f32[112,128]{1,0:T(8,128)S(1)} %pad_maximum_fusion.4), channel_id=1, source_target_pairs={{0,2},{2,4},{4,6},{6,8},{8,10},{10,12},{12,14},{14,16},{16,18},{18... | collective-permute-start | bytes 172040 | tf_op jit(solution)/shard_map/ppermute | solution.py:589
  44.5 4.9 %collective-permute-start.8 = (f32[112,128]{1,0:T(8,128)S(1)}, f32[112,128]{1,0:T(8,128)S(1)}, u32[]{:S(2)}, u32[]{:S(2)}) collective-permute-start(f32[112,128]{1,0:T(8,128)S(1)} %pad_maximum_fusion.5), channel_id=1, source_target_pairs={{2,0},{4,2},{6,4},{8,6},{10,8},{12,10},{14,12},{16,14},{18,16},{20... | collective-permute-start | bytes 172040 | tf_op jit(solution)/shard_map/ppermute | solution.py:589

commit v4 on v3

--- a/solution.py
+++ b/solution.py
@@ -17,7 +17,7 @@
 SIGMA = 32.0
 MASS_SHIFT = 1.0
 Z_AXIS = ("sfc_2",)
-OTHERS = ("sfc_0", "sfc_1", "grp")
+OTHERS = ("sfc_0", "sfc_1")
 SFC = ("sfc_0", "sfc_1", "sfc_2")
 SFC_GRP = ("sfc_0", "sfc_1", "sfc_2", "grp")
 VMEM_LIMIT = 24 * 1024 * 1024
@@ -124,18 +124,19 @@
     return planes
 
 
-def write_messages(source, both_ref, up_ref, down_ref):
-    def pair(ref, start, sent, own):
+def write_messages(sources, up_ref, down_ref):
+    def pair(ref, start, source, sent, own):
         ref[pl.ds(start, 28, stride=2), :] = source[pl.ds(4 + sent, 28, stride=8), :]
         ref[pl.ds(start + 1, 28, stride=2), :] = source[pl.ds(own, 28, stride=8), :]
 
-    pair(both_ref, 0, 0, 1)
-    pair(both_ref, 56, 1, 0)
-    pair(up_ref, 0, 2, 3)
-    pair(down_ref, 0, 3, 2)
-
-
-def first_kernel(
+    for half in range(2):
+        pair(up_ref, 56 * half, sources[half], 2, 3)
+        pair(down_ref, 56 * half, sources[half], 3, 2)
+    pair(up_ref, 112, sources[1], 0, 1)
+    pair(down_ref, 112, sources[0], 1, 0)
+
+
+def pack_kernel(
     rhs_hbm,
     level_hbm,
     own_hbm,
@@ -144,17 +145,7 @@
     orient_hbm,
     penalty_hbm,
     send_hbm,
-    grads_hbm,
-    mass_hbm,
-    field_ref,
-    planes_ref,
-    index_ref,
-    scale_ref,
-    grads_ref,
-    mass_ref,
-    both_ref,
-    up_ref,
-    down_ref,
+    raw_ref,
     rhs_ref,
     level_ref,
     own_ref,
@@ -177,8 +168,6 @@
                 (send_hbm, send_ref.at[0]),
                 (level_hbm, level_ref.at[0]),
                 (rhs_hbm, rhs_ref),
-                (grads_hbm, grads_ref),
-                (mass_hbm, mass_ref),
             )
         )
     ]
@@ -188,15 +177,47 @@
         copy.wait()
     for a in range(5):
         for b in range(5):
-            field_ref[25 * a + 5 * b : 25 * a + 5 * b + 5, :] = rhs_ref[a, b]
-    field_ref[125:128, :] = jnp.zeros((3, 128), f32)
-    own = own_ref[...]
-    pieces = split(penalty_ref[...])
+            raw_ref[25 * a + 5 * b : 25 * a + 5 * b + 5, :] = rhs_ref[a, b]
+    raw_ref[125:128, :] = jnp.zeros((3, 128), f32)
+    for k, ref in enumerate((own_ref, near_ref, kind_ref, orient_ref, penalty_ref, send_ref)):
+        for third in range(3):
+            at = 128 + 3 * k + third
+            raw_ref[at : at + 1, :] = ref[:, 128 * third : 128 * third + 128].astype(f32)
+    raw_ref[146:147, :] = level_ref[...].astype(f32)
+    raw_ref[147:152, :] = jnp.zeros((5, 128), f32)
+
+
+def first_kernel(core_ref, mine_ref, other_ref, grads_hbm, mass_hbm, *refs):
+    outs, (grads_ref, mass_ref, up_ref, down_ref, sems) = refs[:8], refs[8:]
+    copies = [
+        pltpu.make_async_copy(grads_hbm, grads_ref, sems.at[0]),
+        pltpu.make_async_copy(mass_hbm, mass_ref, sems.at[1]),
+    ]
+    for copy in copies:
+        copy.start()
+    low = core_ref[0] == 0
+    for half in range(2):
+        first, second = (mine_ref, other_ref) if half == 0 else (other_ref, mine_ref)
+        outs[4 * half][...] = jnp.where(low, first[0:128, :], second[0:128, :])
+        raw = jnp.where(low, first[128:152, :], second[128:152, :])
+        prepare_half(raw, *outs[4 * half : 4 * half + 4])
+    write_messages((outs[1], outs[5]), up_ref, down_ref)
+    for copy in copies:
+        copy.wait()
+
+
+def prepare_half(raw, field_ref, planes_ref, index_ref, scale_ref):
+    def entries(k):
+        return jnp.concatenate([raw[3 * k + third : 3 * k + third + 1] for third in range(3)], axis=1)
+
+    own = entries(0).astype(jnp.int32)
+    near = entries(1).astype(jnp.int32)
+    pieces = split(entries(4))
     rows = [
         (own >> 7).astype(f32),
         (own & 127).astype(f32),
-        kind_ref[...].astype(f32),
-        orient_ref[...].astype(f32),
+        entries(2),
+        entries(3),
         pieces[0],
         pieces[1],
         pieces[2],
@@ -206,7 +227,7 @@
     spot = lax.broadcasted_iota(jnp.int32, (512, 384), 0)
     lane = spot & 127
     wanted = jnp.where(lane < GHOST, 6 * CELLS + (spot >> 7) * GHOST + lane, -1)
-    onehot = jnp.where(wanted == near_ref[...], 1.0, 0.0).astype(bf16)
+    onehot = jnp.where(wanted == near, 1.0, 0.0).astype(bf16)
     moved = lax.dot_general(
         table, onehot, (((1,), (1,)), ((), ())), preferred_element_type=f32
     )
@@ -219,8 +240,9 @@
     own_face, own_cell = upper(moved[0:1]), upper(moved[1:2])
     penalty = upper(moved[4:5] + moved[5:6] + moved[6:7])
     lanes = lax.broadcasted_iota(jnp.int32, (1, 128), 1)
+    sends = entries(5).astype(jnp.int32)
     send = [
-        jnp.where(lanes < GHOST, pltpu.roll(send_ref[...], (384 - GHOST * k) % 384, 1)[:, :128], 0)
+        jnp.where(lanes < GHOST, pltpu.roll(sends, (384 - GHOST * k) % 384, 1)[:, :128], 0)
         for k in range(4)
     ]
     send = jnp.concatenate([jnp.zeros((4, 128), jnp.int32)] + send, axis=0)
@@ -229,7 +251,7 @@
     cell = jnp.where(sub < 4, own_cell.astype(jnp.int32), send & 127)
     index_ref[0:8, :] = face
     index_ref[8:16, :] = cell
-    scale = jnp.exp2(-jnp.broadcast_to(level_ref[...], (8, 128)).astype(f32))
+    scale = jnp.exp2(-jnp.broadcast_to(raw[18:19], (8, 128)))
     scale_ref[...] = scale
     scaled = penalty * jnp.take_along_axis(scale, cell, axis=1, mode="promise_in_bounds")
     for t, plane in enumerate(gather_planes(field_ref, face, cell)):
@@ -237,7 +259,6 @@
     planes_ref[200:208, :] = upper(moved[2:3])
     planes_ref[208:216, :] = upper(moved[3:4])
     planes_ref[216:224, :] = scaled
-    write_messages(planes_ref, both_ref, up_ref, down_ref)
 
 
 def local_volume(field, scale_ref, grads_ref, mass_ref):
@@ -247,12 +268,15 @@
 
 
 def volume_kernel(
-    field_ref,
-    scale_ref,
+    field0_ref,
+    field1_ref,
+    scale0_ref,
+    scale1_ref,
     grads_ref,
     mass_ref,
     subface_hbm,
-    volume_ref,
+    volume0_ref,
+    volume1_ref,
     plain_ref,
     turned_ref,
     subface_ref,
@@ -260,7 +284,8 @@
 ):
     copy = pltpu.make_async_copy(subface_hbm, subface_ref, sem)
     copy.start()
-    volume_ref[...] = local_volume(field_ref[...], scale_ref, grads_ref, mass_ref)
+    volume0_ref[...] = local_volume(field0_ref[...], scale0_ref, grads_ref, mass_ref)
+    volume1_ref[...] = local_volume(field1_ref[...], scale1_ref, grads_ref, mass_ref)
     plain_ref[...] = jnp.zeros((640, 128), f32)
     turned_ref[...] = jnp.zeros((640, 128), f32)
     copy.wait()
@@ -288,31 +313,39 @@
     return result
 
 
-def middle_kernel(
-    field_ref, scale_ref, grads_ref, mass_ref, maps_ref, planes_ref, meta_ref, volume_ref, sent_ref
-):
-    volume_ref[...] = local_volume(field_ref[...], scale_ref, grads_ref, mass_ref)
-    masks = orient_masks(meta_ref[8:16, :])
-    for t, plane in enumerate(map_sent(maps_ref, planes_ref, meta_ref, masks)):
-        sent_ref[8 * t : 8 * t + 8, :] = plane
-
-
-def read_messages(core_ref, partner_ref, below_ref, above_ref, got_ref):
-    low = core_ref[0] == 0
+def middle_kernel(grads_ref, mass_ref, *refs):
+    for half in range(2):
+        field_ref, scale_ref, maps_ref, planes_ref, meta_ref = refs[5 * half : 5 * half + 5]
+        volume_ref, sent_ref = refs[10 + 2 * half : 12 + 2 * half]
+        volume_ref[...] = local_volume(field_ref[...], scale_ref, grads_ref, mass_ref)
+        masks = orient_masks(meta_ref[8:16, :])
+        for t, plane in enumerate(map_sent(maps_ref, planes_ref, meta_ref, masks)):
+            sent_ref[8 * t : 8 * t + 8, :] = plane
+
+
+def read_messages(below_ref, above_ref, sources, gots):
+    def put(half, row, value):
+        gots[half][pl.ds(row, 28, stride=8), :] = value
 
     def rows(ref, start):
         return ref[pl.ds(start, 28, stride=2), :]
 
-    def put(row, value):
-        got_ref[pl.ds(row, 28, stride=8), :] = value
-
-    for j, (from_below, from_above) in enumerate(((0, 1), (5, 4))):
-        put(from_below, jnp.where(low, rows(below_ref, 56 + j), rows(partner_ref, j)))
-        put(from_above, jnp.where(low, rows(partner_ref, 56 + j), rows(above_ref, 56 + j)))
-    put(2, rows(below_ref, 0))
-    put(7, rows(below_ref, 1))
-    put(3, rows(above_ref, 0))
-    put(6, rows(above_ref, 1))
+    def local(half, row):
+        return sources[half][pl.ds(row, 28, stride=8), :]
+
+    for half in range(2):
+        put(half, 2, rows(below_ref, 56 * half))
+        put(half, 7, rows(below_ref, 56 * half + 1))
+        put(half, 3, rows(above_ref, 56 * half))
+        put(half, 6, rows(above_ref, 56 * half + 1))
+    put(0, 0, rows(below_ref, 112))
+    put(0, 5, rows(below_ref, 113))
+    put(1, 1, rows(above_ref, 112))
+    put(1, 4, rows(above_ref, 113))
+    put(0, 1, local(1, 5))
+    put(0, 4, local(1, 0))
+    put(1, 0, local(0, 4))
+    put(1, 5, local(0, 1))
 
 
 def build_maps(plain_ref, turned_ref, kind, maps_ref):
@@ -400,105 +433,72 @@
     ]
 
 
-def next_messages(field_ref, index_ref, planes_ref, both_ref, up_ref, down_ref):
+def next_planes(field_ref, index_ref, planes_ref):
     face, cell = index_ref[0:8, :], index_ref[8:16, :]
     for t, plane in enumerate(gather_planes(field_ref, face, cell)):
         planes_ref[8 * t : 8 * t + 8, :] = plane
     planes_ref[200:224, :] = jnp.zeros((24, 128), f32)
-    write_messages(planes_ref, both_ref, up_ref, down_ref)
-
-
-def second_kernel(
-    core_ref,
-    partner_ref,
-    below_ref,
-    above_ref,
-    old_ref,
-    volume_ref,
-    index_ref,
-    plain_ref,
-    turned_ref,
-    field_ref,
-    planes_ref,
-    meta_ref,
-    maps_ref,
-    both_ref,
-    up_ref,
-    down_ref,
-    got_ref,
-    pieces_ref,
-):
-    read_messages(core_ref, partner_ref, below_ref, above_ref, got_ref)
+
+
+def second_kernel(below_ref, above_ref, plain_ref, turned_ref, *refs):
+    ins, outs = (refs[0:3], refs[3:6]), (refs[6:10], refs[10:14])
+    up_ref, down_ref, got0_ref, got1_ref, pieces_ref = refs[14:]
+    gots = (got0_ref, got1_ref)
+    read_messages(below_ref, above_ref, (ins[0][0], ins[1][0]), gots)
     sub = lax.broadcasted_iota(jnp.int32, (8, 128), 0)
-    for k in range(3):
-        at = 200 + 8 * k
-        meta_ref[8 * k : 8 * k + 8, :] = jnp.where(
-            sub < 4, old_ref[at : at + 8, :], got_ref[at : at + 8, :]
-        )
-    masks = orient_masks(meta_ref[8:16, :])
-    build_maps(plain_ref, turned_ref, meta_ref[0:8, :], maps_ref)
-    sent = map_sent(maps_ref, old_ref, meta_ref, masks)
-    planes = combine(got_ref, old_ref, sent, maps_ref, meta_ref[16:24, :], masks)
-    add_faces(volume_ref, planes, index_ref, pieces_ref, field_ref)
-    next_messages(field_ref, index_ref, planes_ref, both_ref, up_ref, down_ref)
-
-
-def third_kernel(
-    core_ref,
-    partner_ref,
-    below_ref,
-    above_ref,
-    old_ref,
-    sent_ref,
-    volume_ref,
-    index_ref,
-    meta_ref,
-    maps_ref,
-    field_ref,
-    planes_ref,
-    both_ref,
-    up_ref,
-    down_ref,
-    got_ref,
-    pieces_ref,
-):
-    read_messages(core_ref, partner_ref, below_ref, above_ref, got_ref)
+    for half in range(2):
+        old_ref, volume_ref, index_ref = ins[half]
+        field_ref, planes_ref, meta_ref, maps_ref = outs[half]
+        got_ref = gots[half]
+        for k in range(3):
+            at = 200 + 8 * k
+            meta_ref[8 * k : 8 * k + 8, :] = jnp.where(
+                sub < 4, old_ref[at : at + 8, :], got_ref[at : at + 8, :]
+            )
+        masks = orient_masks(meta_ref[8:16, :])
+        build_maps(plain_ref, turned_ref, meta_ref[0:8, :], maps_ref)
+        sent = map_sent(maps_ref, old_ref, meta_ref, masks)
+        planes = combine(got_ref, old_ref, sent, maps_ref, meta_ref[16:24, :], masks)
+        add_faces(volume_ref, planes, index_ref, pieces_ref, field_ref)
+        next_planes(field_ref, index_ref, planes_ref)
+    write_messages((outs[0][1], outs[1][1]), up_ref, down_ref)
+
+
+def apply_half(got_ref, ins, pieces_ref, field_ref):
+    old_ref, sent_ref, volume_ref, index_ref, meta_ref, maps_ref = ins
     masks = orient_masks(meta_ref[8:16, :])
     sent = read_planes(sent_ref)
     planes = combine(got_ref, old_ref, sent, maps_ref, meta_ref[16:24, :], masks)
     add_faces(volume_ref, planes, index_ref, pieces_ref, field_ref)
-    next_messages(field_ref, index_ref, planes_ref, both_ref, up_ref, down_ref)
-
-
-def fourth_kernel(
-    core_ref,
-    partner_ref,
-    below_ref,
-    above_ref,
-    old_ref,
-    sent_ref,
-    volume_ref,
-    index_ref,
-    meta_ref,
-    maps_ref,
-    power0_ref,
-    power1_ref,
-    power2_ref,
-    field_ref,
-    moments_ref,
-    got_ref,
-    pieces_ref,
-):
-    read_messages(core_ref, partner_ref, below_ref, above_ref, got_ref)
-    masks = orient_masks(meta_ref[8:16, :])
-    sent = read_planes(sent_ref)
-    planes = combine(got_ref, old_ref, sent, maps_ref, meta_ref[16:24, :], masks)
-    add_faces(volume_ref, planes, index_ref, pieces_ref, field_ref)
-    powers = [power0_ref[...], power1_ref[...], power2_ref[...], field_ref[...]]
+
+
+def third_kernel(below_ref, above_ref, *refs):
+    ins, outs = (refs[0:6], refs[6:12]), (refs[12:14], refs[14:16])
+    up_ref, down_ref, got0_ref, got1_ref, pieces_ref = refs[16:]
+    gots = (got0_ref, got1_ref)
+    read_messages(below_ref, above_ref, (ins[0][0], ins[1][0]), gots)
+    for half in range(2):
+        field_ref, planes_ref = outs[half]
+        apply_half(gots[half], ins[half], pieces_ref, field_ref)
+        next_planes(field_ref, ins[half][3], planes_ref)
+    write_messages((outs[0][1], outs[1][1]), up_ref, down_ref)
+
+
+def fourth_kernel(below_ref, above_ref, *refs):
+    ins, old_powers = (refs[0:6], refs[6:12]), (refs[12:15], refs[15:18])
+    fields, (moments_ref, got0_ref, got1_ref, pieces_ref) = refs[18:20], refs[20:]
+    gots = (got0_ref, got1_ref)
+    read_messages(below_ref, above_ref, (ins[0][0], ins[1][0]), gots)
+    for half in range(2):
+        apply_half(gots[half], ins[half], pieces_ref, fields[half])
+    powers = [
+        [ref[...] for ref in old_powers[half]] + [fields[half][...]] for half in range(2)
+    ]
     lane = lax.broadcasted_iota(jnp.int32, (1, 128), 1)
     result = jnp.zeros((1, 128), f32)
     for k in range(2 * ITERS):
-        row = jnp.sum(powers[k // 2] * powers[(k + 1) // 2], axis=0, keepdims=True)
+        both = sum(powers[half][k // 2] * powers[half][(k + 1) // 2] for half in range(2))
+        row = jnp.sum(both, axis=0, keepdims=True)
         result = jnp.where(lane == k, jnp.sum(row, axis=1, keepdims=True), result)
     moments_ref[...] = jnp.broadcast_to(result, moments_ref.shape)
 
@@ -543,9 +543,9 @@
     return iterate, remains
 
 
-def last_kernel(
-    rows_ref, power0_ref, power1_ref, power2_ref, power3_ref, solution_ref, residual_ref
-):
+def last_kernel(core_ref, rows_ref, *refs):
+    halves, (solution_ref, residual_ref) = (refs[0:4], refs[4:8]), refs[8:]
+    low = core_ref[0] == 0
     total = jnp.sum(rows_ref[...], axis=0, keepdims=True)
     lane = lax.broadcasted_iota(jnp.int32, (1, 128), 1)
     moments = [
@@ -555,11 +555,12 @@
         for k in range(2 * ITERS)
     ]
     iterate, remains = coefficients(moments)
-    powers = (power0_ref, power1_ref, power2_ref, power3_ref)
     for a in range(5):
         for b in range(5):
             at = 25 * a + 5 * b
-            values = [ref[at : at + 5, :] for ref in powers]
+            values = [
+                jnp.where(low, one[at : at + 5, :], two[at : at + 5, :]) for one, two in zip(*halves)
+            ]
             answer = sum((c * (1.0 / SIGMA)) * v for c, v in zip(iterate, values))
             solution_ref[a, b] = answer
             residual_ref[a, b] = sum(c * v for c, v in zip(remains, values))
@@ -589,11 +590,8 @@
     return lax.ppermute(block, axis, route)
 
 
-def exchange(both, up, down):
-    partner = lax.ppermute(both, "grp", [(0, 1), (1, 0)])
-    below = shifted(jnp.concatenate([up, partner[:56]], axis=0), SFC, 1)
-    above = shifted(jnp.concatenate([down, partner[56:]], axis=0), SFC, -1)
-    return partner, below, above
+def exchange(up, down):
+    return shifted(up, SFC, 1), shifted(down, SFC, -1)
 
 
 def sum_over(rows, axes):
@@ -611,74 +609,93 @@
     send_slots,
     subface_maps,
 ):
-    field_shape, planes_shape = ((128, 128), f32), ((256, 128), f32)
-    messages = [((112, 128), f32), ((56, 128), f32), ((56, 128), f32)]
+    field_shape, planes_shape, index_shape = ((128, 128), f32), ((256, 128), f32), ((16, 128), jnp.int32)
+    table_shape = ((640, 128), f32)
+    messages = [((168, 128), f32)] * 2
     core = lax.axis_index("grp").astype(jnp.int32).reshape(1)
     tables = [jnp.asarray(table) for table in volume_tables()]
-    row, whole = ((1, 384), jnp.int32), ((128, 128), f32)
-    power0, planes, index, scale, grads, mass, *sends = call(
-        first_kernel,
-        [field_shape, planes_shape, ((16, 128), jnp.int32), ((8, 128), f32), whole, whole] + messages,
-        [right_side, cell_level, own_slot, near_slot, face_kind, orientation, penalty, send_slots]
-        + tables,
+    row = ((1, 384), jnp.int32)
+    (raw,) = call(
+        pack_kernel,
+        [((152, 128), f32)],
+        [right_side, cell_level, own_slot, near_slot, face_kind, orientation, penalty, send_slots],
         [pltpu.VMEM(right_side.shape, f32), pltpu.VMEM((1, 128), jnp.int32)]
         + [pltpu.VMEM(*row)] * 4
-        + [pltpu.VMEM((1, 384), f32), pltpu.VMEM(*row), pltpu.SemaphoreType.DMA((10,))],
-        {k: pltpu.HBM for k in range(10)},
-    )
-    scratch = [pltpu.VMEM((224, 128), f32), pltpu.VMEM((256, 128), f32)]
-    got = exchange(*sends)
-    volume, plain, turned = call(
+        + [pltpu.VMEM((1, 384), f32), pltpu.VMEM(*row), pltpu.SemaphoreType.DMA((8,))],
+        {k: pltpu.HBM for k in range(8)},
+    )
+    other = lax.ppermute(raw, "grp", [(0, 1), (1, 0)])
+    half_shapes = [field_shape, planes_shape, index_shape, ((8, 128), f32)]
+    *halves, grads, mass, up, down = call(
+        first_kernel,
+        half_shapes * 2 + [((128, 128), f32)] * 2 + messages,
+        [core, raw, other] + tables,
+        [pltpu.SemaphoreType.DMA((2,))],
+        {0: pltpu.SMEM, 3: pltpu.HBM, 4: pltpu.HBM},
+    )
+    power0, planes, index, scale = zip(halves[:4], halves[4:])
+    scratch = [pltpu.VMEM((224, 128), f32)] * 2 + [pltpu.VMEM((256, 128), f32)]
+    got = exchange(up, down)
+    volume0, volume1, plain, turned = call(
         volume_kernel,
-        [field_shape, ((640, 128), f32), ((640, 128), f32)],
-        [power0, scale, grads, mass, jnp.transpose(subface_maps, (1, 0, 2))],
+        [field_shape, field_shape, table_shape, table_shape],
+        [*power0, *scale, grads, mass, jnp.transpose(subface_maps, (1, 0, 2))],
         [pltpu.VMEM((WIDTH, 4, WIDTH), f32), pltpu.SemaphoreType.DMA],
-        {4: pltpu.HBM},
+        {6: pltpu.HBM},
         flops=10**7,
     )
-    power1, new_planes, meta, maps, *sends = call(
+    volume = (volume0, volume1)
+    *halves, up, down = call(
         second_kernel,
-        [field_shape, planes_shape, ((24, 128), f32), ((5120, 128), f32)] + messages,
-        [core, *got, planes, volume, index, plain, turned],
+        [field_shape, planes_shape, ((24, 128), f32), ((5120, 128), f32)] * 2 + messages,
+        [*got, plain, turned]
+        + [a[half] for half in range(2) for a in (planes, volume, index)],
         scratch,
-        {0: pltpu.SMEM},
-    )
-    planes = new_planes
-
-    def middle(field):
-        return call(
+    )
+    power1, planes, meta, maps = zip(halves[:4], halves[4:])
+
+    def middle(field, planes):
+        volume0, sent0, volume1, sent1 = call(
             middle_kernel,
-            [field_shape, planes_shape],
-            [field, scale, grads, mass, maps, planes, meta],
+            [field_shape, planes_shape] * 2,
+            [grads, mass]
+            + [a[half] for half in range(2) for a in (field, scale, maps, planes, meta)],
             flops=10**7,
         )
-
-    got = exchange(*sends)
-    volume, sent = middle(power1)
-    power2, new_planes, *sends = call(
+        return (volume0, volume1), (sent0, sent1)
+
+    got = exchange(up, down)
+    volume, sent = middle(power1, planes)
+    *halves, up, down = call(
         third_kernel,
-        [field_shape, planes_shape] + messages,
-        [core, *got, planes, sent, volume, index, meta, maps],
+        [field_shape, planes_shape] * 2 + messages,
+        [*got] + [a[half] for half in range(2) for a in (planes, sent, volume, index, meta, maps)],
         scratch,
-        {0: pltpu.SMEM},
-    )
-    planes = new_planes
-    got = exchange(*sends)
-    volume, sent = middle(power2)
-    count = lax.axis_size(Z_AXIS)
-    power3, rows = call(
+    )
+    power2, planes = zip(halves[:2], halves[2:])
+    got = exchange(up, down)
+    volume, sent = middle(power2, planes)
+    *power3, rows = call(
         fourth_kernel,
-        [field_shape, ((count, 128), f32)],
-        [core, *got, planes, sent, volume, index, meta, maps, power0, power1, power2],
+        [field_shape, field_shape, ((lax.axis_size(Z_AXIS), 128), f32)],
+        [*got]
+        + [a[half] for half in range(2) for a in (planes, sent, volume, index, meta, maps)]
+        + [a[half] for half in range(2) for a in (power0, power1, power2)],
         scratch,
-        {0: pltpu.SMEM},
     )
     rows = sum_over(rows, Z_AXIS)
     (rows,) = call(repeat_sum_kernel, [((lax.axis_size(OTHERS), 128), f32)], [rows])
     rows = sum_over(rows, OTHERS)
     shape = (right_side.shape, f32)
     return tuple(
-        call(last_kernel, [shape, shape], [rows, power0, power1, power2, power3])
+        call(
+            last_kernel,
+            [shape, shape],
+            [core, rows]
+            + [a[half] for half in range(2) for a in (power0, power1, power2, power3)],
+            (),
+            {0: pltpu.SMEM},
+        )
     )
 
 

time: 110 us -> 106 us (0.964)
  the two profiles are of different devices: /device:TPU:1 before, /device:TPU:2 now
where the time goes in v4:
time: 106 us
  blocking collectives  49.9 us (47%)
  starting transfers between devices  39.2 us (37%)
  Pallas kernels  10.6 us (10%)
  waiting for transfers between devices  5.22 us (5%)
    all_to_all x2, blocking collectives, sum_over(): return lax.all_to_all(rows, axes, 0, 0, tiled=True)  49.9 us
    ppermute x6, starting transfers between devices, shifted(): return lax.ppermute(block, axis, route)  37.3 us
    pallas_call x10, Pallas kernels, call(): pl.pallas_call(kernel, out_shape=[jax.ShapeDtypeStruct(shape, kind) for s...  10.6 us
    ppermute x6, waiting for transfers between devices, shifted(): return lax.ppermute(block, axis, route)  3.99 us
  transfers between devices with their start and end apart: 7, of which 4 were waited for; matrix products, arithmetic and copies ran while one was open for 0% of the time, Pallas kernels for 2%

profile of v4, /device:TPU:2, one launch (start us, length us, event | category | flops | bytes accessed | tf_op | source)
XLA Modules:
  0.0 105.7 jit_solution(3000124237394607295)
XLA Ops:
  0.6 1.0 shard_map.122.mine_ref
  1.7 1.9 %collective-permute-start = (f32[152,128]{1,0:T(8,128)S(1)}, f32[152,128]{1,0:T(8,128)S(1)}, u32[]{:S(2)}, u32[]{:S(2)}) collective-permute-start(f32[152,128]{1,0:T(8,128)S(1)} %shard_map.122.mine_ref), channel_id=1, source_target_pairs={{0,1},{1,0},{2,3},{3,2},{4,5},{5,4},{6,7},{7,6},{8,9},{9,8},{10,11... | collective-permute-start | bytes 233480 | tf_op jit(solution)/shard_map/ppermute | solution.py:627
  3.6 1.2 %collective-permute-done.other_ref = f32[152,128]{1,0:T(8,128)S(1)} collective-permute-done((f32[152,128]{1,0:T(8,128)S(1)}, f32[152,128]{1,0:T(8,128)S(1)}, u32[]{:S(2)}, u32[]{:S(2)}) %collective-permute-start) | collective-permute-done | bytes 77856 | tf_op jit(solution)/shard_map/ppermute | solution.py:627
  4.8 1.1 %shard_map.123 = (f32[128,128]{1,0:T(8,128)S(1)}, f32[256,128]{1,0:T(8,128)S(1)}, s32[16,128]{1,0:T(8,128)S(1)}, f32[8,128]{1,0:T(8,128)S(1)}, f32[128,128]{1,0:...) custom-call(s32[1]{0:T(128)} %bitcast.core_ref, ...), custom_call_target="tpu_custom_call" | custom-call | tf_op jit(solution)/shard_map/pallas_call | solution.py:576
  6.0 3.8 %collective-permute-start.1 = (f32[168,128]{1,0:T(8,128)S(1)}, f32[168,128]{1,0:T(8,128)S(1)}, u32[]{:S(2)}, u32[]{:S(2)}) collective-permute-start(f32[168,128]{1,0:T(8,128)S(1)} %get-tuple-element.45), channel_id=1, source_target_pairs={{0,2},{2,4},{4,6},{6,8},{8,10},{10,12},{12,14},{14,16},{16,18},{18... | collective-permute-start | bytes 258056 | tf_op jit(solution)/shard_map/ppermute | solution.py:590
  9.8 16.7 %collective-permute-start.2 = (f32[168,128]{1,0:T(8,128)S(1)}, f32[168,128]{1,0:T(8,128)S(1)}, u32[]{:S(2)}, u32[]{:S(2)}) collective-permute-start(f32[168,128]{1,0:T(8,128)S(1)} %get-tuple-element.46), channel_id=1, source_target_pairs={{2,0},{4,2},{6,4},{8,6},{10,8},{12,10},{14,12},{16,14},{18,16},{20... | collective-permute-start | bytes 258056 | tf_op jit(solution)/shard_map/ppermute | solution.py:590
  26.6 1.0 shard_map.124
  27.6 0.0 collective-permute-done.1.below_ref
  27.6 1.1 %collective-permute-done.2.above_ref = f32[168,128]{1,0:T(8,128)S(1)} collective-permute-done((f32[168,128]{1,0:T(8,128)S(1)}, f32[168,128]{1,0:T(8,128)S(1)}, u32[]{:S(2)}, u32[]{:S(2)}) %collective-permute-start.2) | collective-permute-done | bytes 86048 | tf_op jit(solution)/shard_map/ppermute | solution.py:590
  28.7 2.7 %shard_map.125 = (f32[128,128]{1,0:T(8,128)S(1)}, f32[256,128]{1,0:T(8,128)S(1)}, f32[24,128]{1,0:T(8,128)S(1)}, f32[5120,128]{1,0:T(8,128)S(1)}, f32[128,128]{1...) custom-call(f32[168,128]{1,0:T(8,128)S(1)} %collective-permute-done., ...), custom_call_target="tpu_custom_call" | custom-call | tf_op jit(solution)/shard_map/pallas_call | solution.py:576
  31.3 1.9 %collective-permute-start.3 = (f32[168,128]{1,0:T(8,128)S(1)}, f32[168,128]{1,0:T(8,128)S(1)}, u32[]{:S(2)}, u32[]{:S(2)}) collective-permute-start(f32[168,128]{1,0:T(8,128)S(1)} %get-tuple-element.61), channel_id=1, source_target_pairs={{0,2},{2,4},{4,6},{6,8},{8,10},{10,12},{12,14},{14,16},{16,18},{18... | collective-permute-start | bytes 258056 | tf_op jit(solution)/shard_map/ppermute | solution.py:590
  33.3 6.5 %collective-permute-start.4 = (f32[168,128]{1,0:T(8,128)S(1)}, f32[168,128]{1,0:T(8,128)S(1)}, u32[]{:S(2)}, u32[]{:S(2)}) collective-permute-start(f32[168,128]{1,0:T(8,128)S(1)} %get-tuple-element.62), channel_id=1, source_target_pairs={{2,0},{4,2},{6,4},{8,6},{10,8},{12,10},{14,12},{16,14},{18,16},{20... | collective-permute-start | bytes 258056 | tf_op jit(solution)/shard_map/ppermute | solution.py:590
  39.8 0.6 shard_map.126
  40.4 0.0 collective-permute-done.3.below_ref
  40.4 1.5 %collective-permute-done.4.above_ref = f32[168,128]{1,0:T(8,128)S(1)} collective-permute-done((f32[168,128]{1,0:T(8,128)S(1)}, f32[168,128]{1,0:T(8,128)S(1)}, u32[]{:S(2)}, u32[]{:S(2)}) %collective-permute-start.4) | collective-permute-done | bytes 86048 | tf_op jit(solution)/shard_map/ppermute | solution.py:590
  41.8 1.4 %shard_map.127 = (f32[128,128]{1,0:T(8,128)S(1)}, f32[256,128]{1,0:T(8,128)S(1)}, f32[128,128]{1,0:T(8,128)S(1)}, f32[256,128]{1,0:T(8,128)S(1)}, f32[168,128]{1,0:T(8,128)S(1)}, /*index=5*/f32[168,128]{1,0:T(8,128)S(1)}) custom-call(f32[168,128]{1,0:T(8,128)S(1)} %collective-permute-done.3.below_ref, f32[168,128]{1,0:T(8,128)S(1)} %collective-permute-done.4.above_ref, ...), custom_call_target="tpu_custom_call" | custom-call | tf_op jit(solution)/shard_map/pallas_call | solution.py:576
  43.3 1.9 %collective-permute-start.5 = (f32[168,128]{1,0:T(8,128)S(1)}, f32[168,128]{1,0:T(8,128)S(1)}, u32[]{:S(2)}, u32[]{:S(2)}) collective-permute-start(f32[168,128]{1,0:T(8,128)S(1)} %get-tuple-element.75), channel_id=1, source_target_pairs={{0,2},{2,4},{4,6},{6,8},{8,10},{10,12},{12,14},{14,16},{16,18},{18... | collective-permute-start | bytes 258056 | tf_op jit(solution)/shard_map/ppermute | solution.py:590
  45.2 6.4 %collective-permute-start.6 = (f32[168,128]{1,0:T(8,128)S(1)}, f32[168,128]{1,0:T(8,128)S(1)}, u32[]{:S(2)}, u32[]{:S(2)}) collective-permute-start(f32[168,128]{1,0:T(8,128)S(1)} %get-tuple-element.76), channel_id=1, source_target_pairs={{2,0},{4,2},{6,4},{8,6},{10,8},{12,10},{14,12},{16,14},{18,16},{20... | collective-permute-start | bytes 258056 | tf_op jit(solution)/shard_map/ppermute | solution.py:590
  51.6 0.6 shard_map.128
  52.2 0.0 collective-permute-done.5.below_ref
  52.2 1.5 %collective-permute-done.6.above_ref = f32[168,128]{1,0:T(8,128)S(1)} collective-permute-done((f32[168,128]{1,0:T(8,128)S(1)}, f32[168,128]{1,0:T(8,128)S(1)}, u32[]{:S(2)}, u32[]{:S(2)}) %collective-permute-start.6) | collective-permute-done | bytes 86048 | tf_op jit(solution)/shard_map/ppermute | solution.py:590
  53.7 1.2 %shard_map.129 = (f32[128,128]{1,0:T(8,128)S(1)}, f32[128,128]{1,0:T(8,128)S(1)}, f32[32,128]{1,0:T(8,128)S(1)}) custom-call(f32[168,128]{1,0:T(8,128)S(1)} %collective-permute-done.5.below_ref, f32[168,128]{1,0:T(8,128)S(1)} %collective-permute-done.6.above_ref, f32[256,128]{1,0:T(8,128)S(1)} %get-tuple-element.77.refs_3_.refs_0_, ...), custom_call_target="tpu_custom_call" | custom-call | tf_op jit(solution)/shard_map/pallas_call | solution.py:576
  54.9 36.5 %all_to_all.22 = f32[32,1,128]{2,1,0:T(1,128)S(1)} all-to-all(f32[32,1,128]{2,1,0:T(1,128)S(1)} %bitcast.13), channel_id=1, replica_groups=mesh['sfc_0'=4,'sfc_1'=4,'sfc_2'=32,'grp'=2] {'sfc_2'}, dimensions={0} | all-to-all | bytes 32768 | tf_op jit(solution)/shard_map/all_to_all | solution.py:598
  91.4 13.5 %all_to_all.23 = f32[16,1,128]{2,1,0:T(1,128)S(1)} all-to-all(f32[16,1,128]{2,1,0:T(1,128)S(1)} %bitcast.12), channel_id=1, replica_groups=mesh['sfc_0'=4,'sfc_1'=4,'sfc_2'=32,'grp'=2] {'sfc_0','sfc_1'}, dimensions={0} | all-to-all | bytes 16384 | tf_op jit(solution)/shard_map/all_to_all | solution.py:598
  104.8 0.9 shard_map.131
  (1 shorter events, 0.0 us)
Async XLA Ops:
  1.7 3.2 %collective-permute-start = (f32[152,128]{1,0:T(8,128)S(1)}, f32[152,128]{1,0:T(8,128)S(1)}, u32[]{:S(2)}, u32[]{:S(2)}) collective-permute-start(f32[152,128]{1,0:T(8,128)S(1)} %shard_map.122.mine_ref), channel_id=1, source_target_pairs={{0,1},{1,0},{2,3},{3,2},{4,5},{5,4},{6,7},{7,6},{8,9},{9,8},{10,11... | collective-permute-start | bytes 233480 | tf_op jit(solution)/shard_map/ppermute | solution.py:627
  6.0 21.6 %collective-permute-start.1 = (f32[168,128]{1,0:T(8,128)S(1)}, f32[168,128]{1,0:T(8,128)S(1)}, u32[]{:S(2)}, u32[]{:S(2)}) collective-permute-start(f32[168,128]{1,0:T(8,128)S(1)} %get-tuple-element.45), channel_id=1, source_target_pairs={{0,2},{2,4},{4,6},{6,8},{8,10},{10,12},{12,14},{14,16},{16,18},{18... | collective-permute-start | bytes 258056 | tf_op jit(solution)/shard_map/ppermute | solution.py:590
  9.8 18.8 %collective-permute-start.2 = (f32[168,128]{1,0:T(8,128)S(1)}, f32[168,128]{1,0:T(8,128)S(1)}, u32[]{:S(2)}, u32[]{:S(2)}) collective-permute-start(f32[168,128]{1,0:T(8,128)S(1)} %get-tuple-element.46), channel_id=1, source_target_pairs={{2,0},{4,2},{6,4},{8,6},{10,8},{12,10},{14,12},{16,14},{18,16},{20... | collective-permute-start | bytes 258056 | tf_op jit(solution)/shard_map/ppermute | solution.py:590
  31.3 9.0 %collective-permute-start.3 = (f32[168,128]{1,0:T(8,128)S(1)}, f32[168,128]{1,0:T(8,128)S(1)}, u32[]{:S(2)}, u32[]{:S(2)}) collective-permute-start(f32[168,128]{1,0:T(8,128)S(1)} %get-tuple-element.61), channel_id=1, source_target_pairs={{0,2},{2,4},{4,6},{6,8},{8,10},{10,12},{12,14},{14,16},{16,18},{18... | collective-permute-start | bytes 258056 | tf_op jit(solution)/shard_map/ppermute | solution.py:590
  33.3 8.6 %collective-permute-start.4 = (f32[168,128]{1,0:T(8,128)S(1)}, f32[168,128]{1,0:T(8,128)S(1)}, u32[]{:S(2)}, u32[]{:S(2)}) collective-permute-start(f32[168,128]{1,0:T(8,128)S(1)} %get-tuple-element.62), channel_id=1, source_target_pairs={{2,0},{4,2},{6,4},{8,6},{10,8},{12,10},{14,12},{16,14},{18,16},{20... | collective-permute-start | bytes 258056 | tf_op jit(solution)/shard_map/ppermute | solution.py:590
  43.3 9.0 %collective-permute-start.5 = (f32[168,128]{1,0:T(8,128)S(1)}, f32[168,128]{1,0:T(8,128)S(1)}, u32[]{:S(2)}, u32[]{:S(2)}) collective-permute-start(f32[168,128]{1,0:T(8,128)S(1)} %get-tuple-element.75), channel_id=1, source_target_pairs={{0,2},{2,4},{4,6},{6,8},{8,10},{10,12},{12,14},{14,16},{16,18},{18... | collective-permute-start | bytes 258056 | tf_op jit(solution)/shard_map/ppermute | solution.py:590
  45.2 8.5 %collective-permute-start.6 = (f32[168,128]{1,0:T(8,128)S(1)}, f32[168,128]{1,0:T(8,128)S(1)}, u32[]{:S(2)}, u32[]{:S(2)}) collective-permute-start(f32[168,128]{1,0:T(8,128)S(1)} %get-tuple-element.76), channel_id=1, source_target_pairs={{2,0},{4,2},{6,4},{8,6},{10,8},{12,10},{14,12},{16,14},{18,16},{20... | collective-permute-start | bytes 258056 | tf_op jit(solution)/shard_map/ppermute | solution.py:590

commit v5 on v4

--- a/solution.py
+++ b/solution.py
@@ -124,7 +124,18 @@
     return planes
 
 
-def write_messages(sources, up_ref, down_ref):
+def write_messages(even, sources, first_ref, second_ref):
+    @pl.when(even)
+    def _():
+        fill_messages(sources, first_ref, second_ref)
+
+    @pl.when(jnp.logical_not(even))
+    def _():
+        fill_messages(sources, second_ref, first_ref)
+
+
+def fill_messages(sources, up_ref, down_ref):
+
     def pair(ref, start, source, sent, own):
         ref[pl.ds(start, 28, stride=2), :] = source[pl.ds(4 + sent, 28, stride=8), :]
         ref[pl.ds(start + 1, 28, stride=2), :] = source[pl.ds(own, 28, stride=8), :]
@@ -187,21 +198,22 @@
     raw_ref[147:152, :] = jnp.zeros((5, 128), f32)
 
 
-def first_kernel(core_ref, mine_ref, other_ref, grads_hbm, mass_hbm, *refs):
+def first_kernel(place_ref, mine_ref, other_ref, grads_hbm, mass_hbm, *refs):
     outs, (grads_ref, mass_ref, up_ref, down_ref, sems) = refs[:8], refs[8:]
+    even = place_ref[1] == 0
     copies = [
         pltpu.make_async_copy(grads_hbm, grads_ref, sems.at[0]),
         pltpu.make_async_copy(mass_hbm, mass_ref, sems.at[1]),
     ]
     for copy in copies:
         copy.start()
-    low = core_ref[0] == 0
+    low = place_ref[0] == 0
     for half in range(2):
         first, second = (mine_ref, other_ref) if half == 0 else (other_ref, mine_ref)
         outs[4 * half][...] = jnp.where(low, first[0:128, :], second[0:128, :])
         raw = jnp.where(low, first[128:152, :], second[128:152, :])
         prepare_half(raw, *outs[4 * half : 4 * half + 4])
-    write_messages((outs[1], outs[5]), up_ref, down_ref)
+    write_messages(even, (outs[1], outs[5]), up_ref, down_ref)
     for copy in copies:
         copy.wait()
 
@@ -323,25 +335,32 @@
             sent_ref[8 * t : 8 * t + 8, :] = plane
 
 
-def read_messages(below_ref, above_ref, sources, gots):
+def read_messages(even, first_ref, second_ref, sources, gots):
     def put(half, row, value):
         gots[half][pl.ds(row, 28, stride=8), :] = value
 
-    def rows(ref, start):
-        return ref[pl.ds(start, 28, stride=2), :]
+    def rows(when_even_ref, when_odd_ref, start):
+        at = pl.ds(start, 28, stride=2)
+        return jnp.where(even, when_even_ref[at, :], when_odd_ref[at, :])
+
+    def below(start):
+        return rows(second_ref, first_ref, start)
+
+    def above(start):
+        return rows(first_ref, second_ref, start)
 
     def local(half, row):
         return sources[half][pl.ds(row, 28, stride=8), :]
 
     for half in range(2):
-        put(half, 2, rows(below_ref, 56 * half))
-        put(half, 7, rows(below_ref, 56 * half + 1))
-        put(half, 3, rows(above_ref, 56 * half))
-        put(half, 6, rows(above_ref, 56 * half + 1))
-    put(0, 0, rows(below_ref, 112))
-    put(0, 5, rows(below_ref, 113))
-    put(1, 1, rows(above_ref, 112))
-    put(1, 4, rows(above_ref, 113))
+        put(half, 2, below(56 * half))
+        put(half, 7, below(56 * half + 1))
+        put(half, 3, above(56 * half))
+        put(half, 6, above(56 * half + 1))
+    put(0, 0, below(112))
+    put(0, 5, below(113))
+    put(1, 1, above(112))
+    put(1, 4, above(113))
     put(0, 1, local(1, 5))
     put(0, 4, local(1, 0))
     put(1, 0, local(0, 4))
@@ -440,11 +459,12 @@
     planes_ref[200:224, :] = jnp.zeros((24, 128), f32)
 
 
-def second_kernel(below_ref, above_ref, plain_ref, turned_ref, *refs):
+def second_kernel(place_ref, came_first_ref, came_second_ref, plain_ref, turned_ref, *refs):
     ins, outs = (refs[0:3], refs[3:6]), (refs[6:10], refs[10:14])
     up_ref, down_ref, got0_ref, got1_ref, pieces_ref = refs[14:]
     gots = (got0_ref, got1_ref)
-    read_messages(below_ref, above_ref, (ins[0][0], ins[1][0]), gots)
+    even = place_ref[1] == 0
+    read_messages(even, came_first_ref, came_second_ref, (ins[0][0], ins[1][0]), gots)
     sub = lax.broadcasted_iota(jnp.int32, (8, 128), 0)
     for half in range(2):
         old_ref, volume_ref, index_ref = ins[half]
@@ -461,7 +481,7 @@
         planes = combine(got_ref, old_ref, sent, maps_ref, meta_ref[16:24, :], masks)
         add_faces(volume_ref, planes, index_ref, pieces_ref, field_ref)
         next_planes(field_ref, index_ref, planes_ref)
-    write_messages((outs[0][1], outs[1][1]), up_ref, down_ref)
+    write_messages(even, (outs[0][1], outs[1][1]), up_ref, down_ref)
 
 
 def apply_half(got_ref, ins, pieces_ref, field_ref):
@@ -472,23 +492,25 @@
     add_faces(volume_ref, planes, index_ref, pieces_ref, field_ref)
 
 
-def third_kernel(below_ref, above_ref, *refs):
+def third_kernel(place_ref, came_first_ref, came_second_ref, *refs):
     ins, outs = (refs[0:6], refs[6:12]), (refs[12:14], refs[14:16])
     up_ref, down_ref, got0_ref, got1_ref, pieces_ref = refs[16:]
     gots = (got0_ref, got1_ref)
-    read_messages(below_ref, above_ref, (ins[0][0], ins[1][0]), gots)
+    even = place_ref[1] == 0
+    read_messages(even, came_first_ref, came_second_ref, (ins[0][0], ins[1][0]), gots)
     for half in range(2):
         field_ref, planes_ref = outs[half]
         apply_half(gots[half], ins[half], pieces_ref, field_ref)
         next_planes(field_ref, ins[half][3], planes_ref)
-    write_messages((outs[0][1], outs[1][1]), up_ref, down_ref)
-
-
-def fourth_kernel(below_ref, above_ref, *refs):
+    write_messages(even, (outs[0][1], outs[1][1]), up_ref, down_ref)
+
+
+def fourth_kernel(place_ref, came_first_ref, came_second_ref, *refs):
     ins, old_powers = (refs[0:6], refs[6:12]), (refs[12:15], refs[15:18])
     fields, (moments_ref, got0_ref, got1_ref, pieces_ref) = refs[18:20], refs[20:]
     gots = (got0_ref, got1_ref)
-    read_messages(below_ref, above_ref, (ins[0][0], ins[1][0]), gots)
+    even = place_ref[1] == 0
+    read_messages(even, came_first_ref, came_second_ref, (ins[0][0], ins[1][0]), gots)
     for half in range(2):
         apply_half(gots[half], ins[half], pieces_ref, fields[half])
     powers = [
@@ -543,9 +565,9 @@
     return iterate, remains
 
 
-def last_kernel(core_ref, rows_ref, *refs):
+def last_kernel(place_ref, rows_ref, *refs):
     halves, (solution_ref, residual_ref) = (refs[0:4], refs[4:8]), refs[8:]
-    low = core_ref[0] == 0
+    low = place_ref[0] == 0
     total = jnp.sum(rows_ref[...], axis=0, keepdims=True)
     lane = lax.broadcasted_iota(jnp.int32, (1, 128), 1)
     moments = [
@@ -584,14 +606,14 @@
     )(*ins)
 
 
-def shifted(block, axis, distance):
-    devices = range(lax.axis_size(axis))
-    route = [(i - distance, i) for i in devices if i - distance in devices]
-    return lax.ppermute(block, axis, route)
-
-
-def exchange(up, down):
-    return shifted(up, SFC, 1), shifted(down, SFC, -1)
+def paired(block, start):
+    chips = lax.axis_size(SFC)
+    lower = range(start, chips - 1, 2)
+    return lax.ppermute(block, SFC, [(i, i + 1) for i in lower] + [(i + 1, i) for i in lower])
+
+
+def exchange(first, second):
+    return paired(first, 0), paired(second, 1)
 
 
 def sum_over(rows, axes):
@@ -612,7 +634,7 @@
     field_shape, planes_shape, index_shape = ((128, 128), f32), ((256, 128), f32), ((16, 128), jnp.int32)
     table_shape = ((640, 128), f32)
     messages = [((168, 128), f32)] * 2
-    core = lax.axis_index("grp").astype(jnp.int32).reshape(1)
+    place = jnp.stack([lax.axis_index("grp"), lax.axis_index("sfc_2") & 1]).astype(jnp.int32)
     tables = [jnp.asarray(table) for table in volume_tables()]
     row = ((1, 384), jnp.int32)
     (raw,) = call(
@@ -629,7 +651,7 @@
     *halves, grads, mass, up, down = call(
         first_kernel,
         half_shapes * 2 + [((128, 128), f32)] * 2 + messages,
-        [core, raw, other] + tables,
+        [place, raw, other] + tables,
         [pltpu.SemaphoreType.DMA((2,))],
         {0: pltpu.SMEM, 3: pltpu.HBM, 4: pltpu.HBM},
     )
@@ -648,9 +670,10 @@
     *halves, up, down = call(
         second_kernel,
         [field_shape, planes_shape, ((24, 128), f32), ((5120, 128), f32)] * 2 + messages,
-        [*got, plain, turned]
+        [place, *got, plain, turned]
         + [a[half] for half in range(2) for a in (planes, volume, index)],
         scratch,
+        {0: pltpu.SMEM},
     )
     power1, planes, meta, maps = zip(halves[:4], halves[4:])
 
@@ -669,8 +692,10 @@
     *halves, up, down = call(
         third_kernel,
         [field_shape, planes_shape] * 2 + messages,
-        [*got] + [a[half] for half in range(2) for a in (planes, sent, volume, index, meta, maps)],
+        [place, *got]
+        + [a[half] for half in range(2) for a in (planes, sent, volume, index, meta, maps)],
         scratch,
+        {0: pltpu.SMEM},
     )
     power2, planes = zip(halves[:2], halves[2:])
     got = exchange(up, down)
@@ -678,10 +703,11 @@
     *power3, rows = call(
         fourth_kernel,
         [field_shape, field_shape, ((lax.axis_size(Z_AXIS), 128), f32)],
-        [*got]
+        [place, *got]
         + [a[half] for half in range(2) for a in (planes, sent, volume, index, meta, maps)]
         + [a[half] for half in range(2) for a in (power0, power1, power2)],
         scratch,
+        {0: pltpu.SMEM},
     )
     rows = sum_over(rows, Z_AXIS)
     (rows,) = call(repeat_sum_kernel, [((lax.axis_size(OTHERS), 128), f32)], [rows])
@@ -691,7 +717,7 @@
         call(
             last_kernel,
             [shape, shape],
-            [core, rows]
+            [place, rows]
             + [a[half] for half in range(2) for a in (power0, power1, power2, power3)],
             (),
             {0: pltpu.SMEM},

time: 106 us -> 110 us (1.038)
  Pallas kernels: 10.6 us -> 13.4 us
  waiting for transfers between devices: 5.22 us -> 6.57 us
    pallas_call x10, Pallas kernels: 10.6 us -> 13.4 us  [call(): pl.pallas_call(kernel, out_shape=[jax.ShapeDtypeStruct(shape, kind) for s...]
    ppermute x6, waiting for transfers between devices: 3.99 us -> 5.41 us  [paired(): lax.ppermute(block, SFC, [(i, i + 1) for i in lower] + [(i + 1, i) for i...]
where the time goes in v5:
time: 110 us
  blocking collectives  49.8 us (45%)
  starting transfers between devices  39.2 us (36%)
  Pallas kernels  13.4 us (12%)
  waiting for transfers between devices  6.57 us (6%)
    all_to_all x2, blocking collectives, sum_over(): return lax.all_to_all(rows, axes, 0, 0, tiled=True)  49.8 us
    ppermute x6, starting transfers between devices, paired(): lax.ppermute(block, SFC, [(i, i + 1) for i in lower] + [(i + 1, i) for i...  37.3 us
    pallas_call x10, Pallas kernels, call(): pl.pallas_call(kernel, out_shape=[jax.ShapeDtypeStruct(shape, kind) for s...  13.4 us
    ppermute x6, waiting for transfers between devices, paired(): lax.ppermute(block, SFC, [(i, i + 1) for i in lower] + [(i + 1, i) for i...  5.41 us
  transfers between devices with their start and end apart: 7, of which 4 were waited for; matrix products, arithmetic and copies ran while one was open for 0% of the time, Pallas kernels for 2%

profile of v5, /device:TPU:2, one launch (start us, length us, event | category | flops | bytes accessed | tf_op | source)
XLA Modules:
  0.0 109.8 jit_solution(10798148406277867947)
XLA Ops:
  0.6 1.0 shard_map.122.mine_ref
  1.7 1.9 %collective-permute-start = (f32[152,128]{1,0:T(8,128)S(1)}, f32[152,128]{1,0:T(8,128)S(1)}, u32[]{:S(2)}, u32[]{:S(2)}) collective-permute-start(f32[152,128]{1,0:T(8,128)S(1)} %shard_map.122.mine_ref), channel_id=1, source_target_pairs={{0,1},{1,0},{2,3},{3,2},{4,5},{5,4},{6,7},{7,6},{8,9},{9,8},{10,11... | collective-permute-start | bytes 233480 | tf_op jit(solution)/shard_map/ppermute | solution.py:649
  3.6 0.1 pad_add_fusion.place_ref
  3.7 1.2 %collective-permute-done.other_ref = f32[152,128]{1,0:T(8,128)S(1)} collective-permute-done((f32[152,128]{1,0:T(8,128)S(1)}, f32[152,128]{1,0:T(8,128)S(1)}, u32[]{:S(2)}, u32[]{:S(2)}) %collective-permute-start) | collective-permute-done | bytes 77856 | tf_op jit(solution)/shard_map/ppermute | solution.py:649
  4.8 1.8 %shard_map.123 = (f32[128,128]{1,0:T(8,128)S(1)}, f32[256,128]{1,0:T(8,128)S(1)}, s32[16,128]{1,0:T(8,128)S(1)}, f32[8,128]{1,0:T(8,128)S(1)}, f32[128,128]{1,0:...) custom-call(s32[2]{0:T(128)S(1)} %pad_add_fusion.place_ref, ...), custom_call_target="tpu_custom_call" | custom-call | tf_op jit(solution)/shard_map/pallas_call | solution.py:598
  6.7 3.8 %collective-permute-start.1 = (f32[168,128]{1,0:T(8,128)S(1)}, f32[168,128]{1,0:T(8,128)S(1)}, u32[]{:S(2)}, u32[]{:S(2)}) collective-permute-start(f32[168,128]{1,0:T(8,128)S(1)} %get-tuple-element.45), channel_id=1, source_target_pairs={{0,2},{4,6},{8,10},{12,14},{16,18},{20,22},{24,26},{28,30},{32,34}... | collective-permute-start | bytes 258056 | tf_op jit(solution)/shard_map/ppermute | solution.py:612
  10.5 17.7 %collective-permute-start.2 = (f32[168,128]{1,0:T(8,128)S(1)}, f32[168,128]{1,0:T(8,128)S(1)}, u32[]{:S(2)}, u32[]{:S(2)}) collective-permute-start(f32[168,128]{1,0:T(8,128)S(1)} %get-tuple-element.46), channel_id=1, source_target_pairs={{2,4},{6,8},{10,12},{14,16},{18,20},{22,24},{26,28},{30,32},{34,36... | collective-permute-start | bytes 258056 | tf_op jit(solution)/shard_map/ppermute | solution.py:612
  28.3 1.0 shard_map.124
  29.3 0.0 collective-permute-done.1.came_first_ref
  29.3 1.5 %collective-permute-done.2.came_second_ref = f32[168,128]{1,0:T(8,128)S(1)} collective-permute-done((f32[168,128]{1,0:T(8,128)S(1)}, f32[168,128]{1,0:T(8,128)S(1)}, u32[]{:S(2)}, u32[]{:S(2)}) %collective-permute-start.2) | collective-permute-done | bytes 86048 | tf_op jit(solution)/shard_map/ppermute | solution.py:612
  30.8 3.2 %shard_map.125 = (f32[128,128]{1,0:T(8,128)S(1)}, f32[256,128]{1,0:T(8,128)S(1)}, f32[24,128]{1,0:T(8,128)S(1)}, f32[5120,128]{1,0:T(8,128)S(1)}, f32[128,128]{1...) custom-call(s32[2]{0:T(128)S(1)} %pad_add_fusion.place_ref, ...), custom_call_target="tpu_custom_call" | custom-call | tf_op jit(solution)/shard_map/pallas_call | solution.py:598
  34.0 1.9 %collective-permute-start.3 = (f32[168,128]{1,0:T(8,128)S(1)}, f32[168,128]{1,0:T(8,128)S(1)}, u32[]{:S(2)}, u32[]{:S(2)}) collective-permute-start(f32[168,128]{1,0:T(8,128)S(1)} %get-tuple-element.61), channel_id=1, source_target_pairs={{0,2},{4,6},{8,10},{12,14},{16,18},{20,22},{24,26},{28,30},{32,34}... | collective-permute-start | bytes 258056 | tf_op jit(solution)/shard_map/ppermute | solution.py:612
  36.0 5.9 %collective-permute-start.4 = (f32[168,128]{1,0:T(8,128)S(1)}, f32[168,128]{1,0:T(8,128)S(1)}, u32[]{:S(2)}, u32[]{:S(2)}) collective-permute-start(f32[168,128]{1,0:T(8,128)S(1)} %get-tuple-element.62), channel_id=1, source_target_pairs={{2,4},{6,8},{10,12},{14,16},{18,20},{22,24},{26,28},{30,32},{34,36... | collective-permute-start | bytes 258056 | tf_op jit(solution)/shard_map/ppermute | solution.py:612
  41.9 0.6 shard_map.126
  42.5 0.0 collective-permute-done.3.came_first_ref
  42.5 1.9 %collective-permute-done.4.came_second_ref = f32[168,128]{1,0:T(8,128)S(1)} collective-permute-done((f32[168,128]{1,0:T(8,128)S(1)}, f32[168,128]{1,0:T(8,128)S(1)}, u32[]{:S(2)}, u32[]{:S(2)}) %collective-permute-start.4) | collective-permute-done | bytes 86048 | tf_op jit(solution)/shard_map/ppermute | solution.py:612
  44.4 1.9 %shard_map.127 = (f32[128,128]{1,0:T(8,128)S(1)}, f32[256,128]{1,0:T(8,128)S(1)}, f32[128,128]{1,0:T(8,128)S(1)}, f32[256,128]{1,0:T(8,128)S(1)}, f32[168,128]{1,0:T(8,128)S(1)}, /*index=5*/f32[168,128]{1,0:T(8,128)S(1)}) custom-call(s32[2]{0:T(128)S(1)} %pad_add_fusion.place_ref, f32[168,128]{1,0:T(8,128)S(1)} %collective-permute-done.3.came_first_ref, ...), custom_call_target="tpu_custom_call" | custom-call | tf_op jit(solution)/shard_map/pallas_call | solution.py:598
  46.4 1.9 %collective-permute-start.5 = (f32[168,128]{1,0:T(8,128)S(1)}, f32[168,128]{1,0:T(8,128)S(1)}, u32[]{:S(2)}, u32[]{:S(2)}) collective-permute-start(f32[168,128]{1,0:T(8,128)S(1)} %get-tuple-element.75), channel_id=1, source_target_pairs={{0,2},{4,6},{8,10},{12,14},{16,18},{20,22},{24,26},{28,30},{32,34}... | collective-permute-start | bytes 258056 | tf_op jit(solution)/shard_map/ppermute | solution.py:612
  48.3 5.9 %collective-permute-start.6 = (f32[168,128]{1,0:T(8,128)S(1)}, f32[168,128]{1,0:T(8,128)S(1)}, u32[]{:S(2)}, u32[]{:S(2)}) collective-permute-start(f32[168,128]{1,0:T(8,128)S(1)} %get-tuple-element.76), channel_id=1, source_target_pairs={{2,4},{6,8},{10,12},{14,16},{18,20},{22,24},{26,28},{30,32},{34,36... | collective-permute-start | bytes 258056 | tf_op jit(solution)/shard_map/ppermute | solution.py:612
  54.3 0.6 shard_map.128
  54.9 0.0 collective-permute-done.5.came_first_ref
  54.9 1.9 %collective-permute-done.6.came_second_ref = f32[168,128]{1,0:T(8,128)S(1)} collective-permute-done((f32[168,128]{1,0:T(8,128)S(1)}, f32[168,128]{1,0:T(8,128)S(1)}, u32[]{:S(2)}, u32[]{:S(2)}) %collective-permute-start.6) | collective-permute-done | bytes 86048 | tf_op jit(solution)/shard_map/ppermute | solution.py:612
  56.8 1.7 %shard_map.129 = (f32[128,128]{1,0:T(8,128)S(1)}, f32[128,128]{1,0:T(8,128)S(1)}, f32[32,128]{1,0:T(8,128)S(1)}) custom-call(s32[2]{0:T(128)S(1)} %pad_add_fusion.place_ref, f32[168,128]{1,0:T(8,128)S(1)} %collective-permute-done.5.came_first_ref, f32[168,128]{1,0:T(8,128)S(1)} %collective-permute-done.6.came_second_ref, ...), custom_call_target="tpu_custom_call" | custom-call | tf_op jit(solution)/shard_map/pallas_call | solution.py:598
  58.6 36.3 %all_to_all.22 = f32[32,1,128]{2,1,0:T(1,128)S(1)} all-to-all(f32[32,1,128]{2,1,0:T(1,128)S(1)} %bitcast.14), channel_id=1, replica_groups=mesh['sfc_0'=4,'sfc_1'=4,'sfc_2'=32,'grp'=2] {'sfc_2'}, dimensions={0} | all-to-all | bytes 32768 | tf_op jit(solution)/shard_map/all_to_all | solution.py:620
  94.9 13.5 %all_to_all.23 = f32[16,1,128]{2,1,0:T(1,128)S(1)} all-to-all(f32[16,1,128]{2,1,0:T(1,128)S(1)} %bitcast.13), channel_id=1, replica_groups=mesh['sfc_0'=4,'sfc_1'=4,'sfc_2'=32,'grp'=2] {'sfc_0','sfc_1'}, dimensions={0} | all-to-all | bytes 16384 | tf_op jit(solution)/shard_map/all_to_all | solution.py:620
  108.4 1.4 %shard_map.131 = (f32[5,5,5,128]{3,2,1,0:T(8,128)}, f32[5,5,5,128]{3,2,1,0:T(8,128)}) custom-call(s32[2]{0:T(128)S(1)} %pad_add_fusion.place_ref, f32[16,128]{1,0:T(8,128)S(1)} %bitcast.12, f32[128,128]{1,0:T(8,128)S(1)} %get-tuple-element.47.field0_ref.refs_12_.refs_0_, f32[128,128]{1,0:T(8,128)S(1)} %get-tuple-element.64.refs_0_.refs_13_.refs_1_, ...), custom_call_target="tpu_custom_call" | custom-call | tf_op jit(solution)/shard_map/pallas_call | solution.py:598
  (1 shorter events, 0.0 us)
Async XLA Ops:
  1.7 3.2 %collective-permute-start = (f32[152,128]{1,0:T(8,128)S(1)}, f32[152,128]{1,0:T(8,128)S(1)}, u32[]{:S(2)}, u32[]{:S(2)}) collective-permute-start(f32[152,128]{1,0:T(8,128)S(1)} %shard_map.122.mine_ref), channel_id=1, source_target_pairs={{0,1},{1,0},{2,3},{3,2},{4,5},{5,4},{6,7},{7,6},{8,9},{9,8},{10,11... | collective-permute-start | bytes 233480 | tf_op jit(solution)/shard_map/ppermute | solution.py:649
  6.7 22.6 %collective-permute-start.1 = (f32[168,128]{1,0:T(8,128)S(1)}, f32[168,128]{1,0:T(8,128)S(1)}, u32[]{:S(2)}, u32[]{:S(2)}) collective-permute-start(f32[168,128]{1,0:T(8,128)S(1)} %get-tuple-element.45), channel_id=1, source_target_pairs={{0,2},{4,6},{8,10},{12,14},{16,18},{20,22},{24,26},{28,30},{32,34}... | collective-permute-start | bytes 258056 | tf_op jit(solution)/shard_map/ppermute | solution.py:612
  10.5 20.3 %collective-permute-start.2 = (f32[168,128]{1,0:T(8,128)S(1)}, f32[168,128]{1,0:T(8,128)S(1)}, u32[]{:S(2)}, u32[]{:S(2)}) collective-permute-start(f32[168,128]{1,0:T(8,128)S(1)} %get-tuple-element.46), channel_id=1, source_target_pairs={{2,4},{6,8},{10,12},{14,16},{18,20},{22,24},{26,28},{30,32},{34,36... | collective-permute-start | bytes 258056 | tf_op jit(solution)/shard_map/ppermute | solution.py:612
  34.0 8.5 %collective-permute-start.3 = (f32[168,128]{1,0:T(8,128)S(1)}, f32[168,128]{1,0:T(8,128)S(1)}, u32[]{:S(2)}, u32[]{:S(2)}) collective-permute-start(f32[168,128]{1,0:T(8,128)S(1)} %get-tuple-element.61), channel_id=1, source_target_pairs={{0,2},{4,6},{8,10},{12,14},{16,18},{20,22},{24,26},{28,30},{32,34}... | collective-permute-start | bytes 258056 | tf_op jit(solution)/shard_map/ppermute | solution.py:612
  36.0 8.5 %collective-permute-start.4 = (f32[168,128]{1,0:T(8,128)S(1)}, f32[168,128]{1,0:T(8,128)S(1)}, u32[]{:S(2)}, u32[]{:S(2)}) collective-permute-start(f32[168,128]{1,0:T(8,128)S(1)} %get-tuple-element.62), channel_id=1, source_target_pairs={{2,4},{6,8},{10,12},{14,16},{18,20},{22,24},{26,28},{30,32},{34,36... | collective-permute-start | bytes 258056 | tf_op jit(solution)/shard_map/ppermute | solution.py:612
  46.4 8.5 %collective-permute-start.5 = (f32[168,128]{1,0:T(8,128)S(1)}, f32[168,128]{1,0:T(8,128)S(1)}, u32[]{:S(2)}, u32[]{:S(2)}) collective-permute-start(f32[168,128]{1,0:T(8,128)S(1)} %get-tuple-element.75), channel_id=1, source_target_pairs={{0,2},{4,6},{8,10},{12,14},{16,18},{20,22},{24,26},{28,30},{32,34}... | collective-permute-start | bytes 258056 | tf_op jit(solution)/shard_map/ppermute | solution.py:612
  48.3 8.5 %collective-permute-start.6 = (f32[168,128]{1,0:T(8,128)S(1)}, f32[168,128]{1,0:T(8,128)S(1)}, u32[]{:S(2)}, u32[]{:S(2)}) collective-permute-start(f32[168,128]{1,0:T(8,128)S(1)} %get-tuple-element.76), channel_id=1, source_target_pairs={{2,4},{6,8},{10,12},{14,16},{18,20},{22,24},{26,28},{30,32},{34,36... | collective-permute-start | bytes 258056 | tf_op jit(solution)/shard_map/ppermute | solution.py:612
